TPU v7x, 512 devices: a whole 4x4x16 slice. The times are simulated.
512 devices in a mesh: dp: 16 (over z), expert: 32 (over x, y, core).
Axes of the slice: x: 4, y: 4, z: 16, core: 2. Of those that a mesh axis runs over, the one named last changes fastest.
Arguments:
- tokens: bfloat16 [65536, 1024], P(('dp', 'expert')), may hold values from -6 to 6
- upstream: bfloat16 [65536, 1024], P(('dp', 'expert')), may hold values from -6 to 6
- expert_ids: int32 [65536, 8], P(('dp', 'expert')), may hold values from 0 to 63, all different within a row; in each aligned block of 128 rows (0 to 127, 128 to 255, ...) at most 20 rows name the same one
- gates: float32 [65536, 8], P(('dp', 'expert')), may hold values from 0.02 to 0.5
- expert_weights: bfloat16 [64, 3, 1024, 384], P('expert', None, 'dp'), may hold values from -0.1875 to 0.1875
- router_weight: bfloat16 [1024, 64], replicated, may hold values from -0.1875 to 0.1875
Outputs:
- token_grad: bfloat16 [65536, 1024], P(('dp', 'expert'))
- router_grad: float32 [1024, 64], P('dp')
Inputs may be any that keep to these rules, and one draw needn't show every extreme that they name: `expert_ids`: within each device's aligned block of 128 rows no expert is named by more than 20 rows.
All inputs are finite; a program needn't handle non-finite values.
Results may differ from a plain program's by a relative error of at most 0.023.
Values may be sent and summed in bfloat16 or wider, within the bound.
No kernel may reach another device: no remote copies, remote signals or barrier semaphores. Data moves between devices by JAX's collectives and lax.ppermute only.
A program may use at most 64 MiB of HBM per device.

v0:
```python
import jax
import jax.numpy as jnp
from jax import lax
from jax.sharding import PartitionSpec as P


def backward_rows(pre_gate, pre_up, hidden_grad, whole):
    sigma = jax.nn.sigmoid(pre_gate)
    active = pre_gate * sigma
    hidden = (active * pre_up).astype(jnp.bfloat16)
    gate_grad = jnp.sum(hidden_grad * hidden.astype(jnp.float32), axis=-1).astype(jnp.bfloat16)
    gate_pre = (hidden_grad * pre_up * sigma * (1.0 + pre_gate * (1.0 - sigma))).astype(
        jnp.bfloat16
    )
    up_pre = (hidden_grad * active).astype(jnp.bfloat16)
    row_grad = jnp.einsum(
        "nscf,sdf->nscd", gate_pre, whole[:, 0], preferred_element_type=jnp.float32
    )
    row_grad = row_grad + jnp.einsum(
        "nscf,sdf->nscd", up_pre, whole[:, 1], preferred_element_type=jnp.float32
    )
    return (row_grad.astype(jnp.bfloat16), gate_grad)


def body(tokens, upstream, expert_ids, gates, expert_weights, router_weight):
    tok_count, width = tokens.shape
    top = expert_ids.shape[1]
    experts = router_weight.shape[1]
    hosts = lax.axis_size("expert")
    per_host = expert_weights.shape[0]
    capacity = min(tok_count, tok_count * top * 5 // (4 * experts))
    flat = expert_ids.reshape(-1)
    columns = jnp.arange(experts, dtype=jnp.int32)
    onehot = (flat[:, None] == columns[None, :]).astype(jnp.int32)
    rank = jnp.sum(jnp.cumsum(onehot, axis=0) * onehot, axis=1) - 1
    target = flat * capacity + rank
    sources = jnp.arange(flat.shape[0], dtype=jnp.int32) // top
    owner_row = jnp.full((experts * capacity,), tok_count, jnp.int32).at[target].set(sources)
    zero_row = jnp.zeros((1, width), jnp.bfloat16)
    padded_x = jnp.concatenate([tokens, zero_row], axis=0)
    padded_dy = jnp.concatenate([upstream, zero_row], axis=0)
    sent_x = padded_x[owner_row].reshape(hosts, per_host, capacity, width)
    sent_dy = padded_dy[owner_row].reshape(hosts, per_host, capacity, width)
    arrived_x, arrived_dy = (
        lax.all_to_all(sent_x, "expert", split_axis=0, concat_axis=0, tiled=True),
        lax.all_to_all(sent_dy, "expert", split_axis=0, concat_axis=0, tiled=True),
    )
    whole = lax.all_gather(expert_weights, "dp", axis=2, tiled=True)
    pre_gate = jnp.einsum(
        "nscd,sdf->nscf", arrived_x, whole[:, 0], preferred_element_type=jnp.float32
    )
    pre_up = jnp.einsum(
        "nscd,sdf->nscf", arrived_x, whole[:, 1], preferred_element_type=jnp.float32
    )
    hidden_grad = jnp.einsum(
        "nscd,sdf->nscf", arrived_dy, whole[:, 2], preferred_element_type=jnp.float32
    )
    row_grad, gate_grad = backward_rows(pre_gate, pre_up, hidden_grad, whole)
    back_rows, back_gate = (
        lax.all_to_all(row_grad, "expert", split_axis=0, concat_axis=0, tiled=True),
        lax.all_to_all(gate_grad, "expert", split_axis=0, concat_axis=0, tiled=True),
    )
    rows = back_rows.reshape(experts * capacity, width)[target].reshape(tok_count, top, width)
    mine = back_gate.reshape(-1)[target].reshape(tok_count, top).astype(jnp.float32)
    combined = jnp.sum(gates[:, :, None] * rows.astype(jnp.float32), axis=1)
    weighted = jnp.sum(gates * mine, axis=1, keepdims=True)
    logit_grad = (gates * (mine - weighted)).astype(jnp.bfloat16)
    match = expert_ids[:, :, None] == columns[None, None, :]
    full_logit_grad = jnp.sum(
        jnp.where(match, logit_grad[:, :, None], jnp.zeros((), jnp.bfloat16)), axis=1
    )
    token_grad = (
        combined + jnp.dot(full_logit_grad, router_weight.T, preferred_element_type=jnp.float32)
    ).astype(jnp.bfloat16)
    router_term = jnp.dot(tokens.T, full_logit_grad, preferred_element_type=jnp.float32)
    partial_rows = lax.psum_scatter(
        router_term.astype(jnp.bfloat16), "dp", scatter_dimension=0, tiled=True
    ).astype(jnp.float32)
    router_grad = lax.psum(partial_rows, "expert")
    return (token_grad, router_grad)


def solution(mesh):
    in_specs = (
        P(("dp", "expert"), None),
        P(("dp", "expert"), None),
        P(("dp", "expert"), None),
        P(("dp", "expert"), None),
        P("expert", None, "dp", None),
        P(),
    )
    out_specs = (P(("dp", "expert"), None), P("dp", None))
    return jax.shard_map(body, mesh=mesh, in_specs=in_specs, out_specs=out_specs, check_vma=False)
```

profile of v0, /device:TPU:1, one launch (start us, length us, event | category | flops | bytes accessed | tf_op | source)
XLA Modules:
  0.0 384.7 jit_solution(7313615299758208944)
XLA Ops:
  7.2 0.0 copy-start
  7.2 0.0 copy-start.1
  7.2 0.0 all-gather.2.cloned.1.call-start
  7.2 1.8 copy.88
  9.0 0.0 all-gather.2.cloned.1.call-update
  9.0 0.8 copy.83
  9.8 0.1 eq.42
  9.9 0.1 eq.38
  10.0 0.7 broadcast_multiply_fusion
  10.7 0.1 copy.82
  10.8 0.1 mul.60
  10.9 18.0 %reduce-window.6 = s32[64,8,128]{2,1,0:T(8,128)S(1)} reduce-window(s32[64,8,128]{2,1,0:T(8,128)S(1)} %fusion.26, s32[]{:T(128)} %constant.34.clone.1), window={size=1x1x128 pad=0_0x0_0x127_0}, to_apply=%region_0.0 | reduce-window | flops 8323072 | bytes 524292 | tf_op jit(solution)/shard_map/reduce-window
  28.9 0.1 slice.30
  29.1 0.1 copy.85
  29.3 0.1 copy.86
  29.3 0.0 copy-done.1
  29.4 0.1 broadcast_add_fusion
  29.5 0.1 fusion.25
  29.6 4.3 %scatter_custom_fusion = s32[1280]{0:T(1024)S(1)} fusion(s32[1024]{0:T(1024)S(1)} %bitcast.100, s32[1024]{0:T(1024)S(1)} %add_select_fusion, s32[]{:T(128)} %constant.32.clone.1), kind=kCustom, calls=%fused_computation.62 | custom fusion | bytes 5124 | tf_op jit(solution)/shard_map/scatter | solution.py:38
  34.0 5.1 %gather_fusion.1 = bf16[1280,1024]{1,0:T(8,128)(2,1)} fusion(bf16[129,1024]{1,0:T(8,128)(2,1)S(1)} %concatenate.7, s32[2048]{0:T(1024)S(1)} %pad_clamp_fusion), kind=kCustom, calls=%fused_computation.1 | custom fusion | bytes 5248000 | tf_op jit(solution)/shard_map/gather | solution.py:42
  39.1 3.5 reshape.79
  42.6 4.2 %copy.90 = bf16[32,2,20,1024]{3,1,2,0:T(2,128)(2,1)} copy(bf16[32,2,20,1024]{3,2,1,0:T(8,128)(2,1)S(1)} %reshape.79) | data formatting | bytes 5242880 | tf_op jit(solution)/shard_map/reshape | solution.py:42
  46.8 11.4 %all-to-all-start.1 = ((bf16[32,2,20,1024]{3,1,2,0:T(2,128)(2,1)}), bf16[32,2,20,1024]{3,1,2,0:T(2,128)(2,1)}, u32[]{:S(2)}, u32[]{:S(2)}) async-start(bf16[32,2,20,1024]{3,1,2,0:T(2,128)(2,1)} %copy.90), calls=%async_computation.1 | async-start | bytes 5242880 | tf_op jit(solution)/shard_map/all_to_all | solution.py:45
  58.2 0.0 copy-done.2
  58.3 5.1 %gather_fusion = bf16[1280,1024]{1,0:T(8,128)(2,1)} fusion(bf16[129,1024]{1,0:T(8,128)(2,1)S(1)} %concatenate.6, s32[2048]{0:T(1024)S(1)} %pad_clamp_fusion), kind=kCustom, calls=%fused_computation | custom fusion | bytes 5248000 | tf_op jit(solution)/shard_map/gather | solution.py:43
  63.4 3.5 reshape.78
  66.9 4.2 %copy.87 = bf16[32,2,20,1024]{3,1,2,0:T(2,128)(2,1)} copy(bf16[32,2,20,1024]{3,2,1,0:T(8,128)(2,1)S(1)} %reshape.78) | data formatting | bytes 5242880 | tf_op jit(solution)/shard_map/reshape | solution.py:43
  71.2 21.1 %all-to-all-done.1 = bf16[32,2,20,1024]{3,1,2,0:T(2,128)(2,1)} async-done(((bf16[32,2,20,1024]{3,1,2,0:T(2,128)(2,1)}), bf16[32,2,20,1024]{3,1,2,0:T(2,128)(2,1)}, u32[]{:S(2)}, u32[]{:S(2)}) %all-to-all-start.1) | async-done | bytes 2621472 | tf_op jit(solution)/shard_map/all_to_all | solution.py:45
  92.2 4.7 %all-to-all-start = ((bf16[32,2,20,1024]{3,1,2,0:T(2,128)(2,1)}), bf16[32,2,20,1024]{3,1,2,0:T(2,128)(2,1)S(1)}, u32[]{:S(2)}, u32[]{:S(2)}) async-start(bf16[32,2,20,1024]{3,1,2,0:T(2,128)(2,1)} %copy.87), calls=%async_computation | async-start | bytes 5242880 | tf_op jit(solution)/shard_map/all_to_all | solution.py:46
  97.0 0.0 all-gather.2.cloned.1.call-done
  97.0 6.4 %fusion.4 = f32[2,32,20,384]{3,1,2,0:T(8,128)} fusion(bf16[32,2,20,1024]{3,1,2,0:T(2,128)(2,1)} %all-to-all-done.1, bf16[2,3,1024,384]{3,2,0,1:T(8,128)(2,1)} %all-gather.2.cloned.1.call-done), kind=kOutput, calls=%fused_computation.11 | convolution fusion | flops 1006632960 | bytes 6160384 | tf_op jit(solution)/shard_map/nscd,sdf->nscf/dot_general | solution.py:49
  103.5 6.6 %fusion.6 = f32[2,32,20,384]{3,1,2,0:T(8,128)} fusion(bf16[32,2,20,1024]{3,1,2,0:T(2,128)(2,1)} %all-to-all-done.1, bf16[2,3,1024,384]{3,2,0,1:T(8,128)(2,1)} %all-gather.2.cloned.1.call-done), kind=kOutput, calls=%fused_computation.13 | convolution fusion | flops 1006632960 | bytes 6160384 | tf_op jit(solution)/shard_map/nscd,sdf->nscf/dot_general | solution.py:52
  110.0 20.9 %all-to-all-done = bf16[32,2,20,1024]{3,1,2,0:T(2,128)(2,1)S(1)} async-done(((bf16[32,2,20,1024]{3,1,2,0:T(2,128)(2,1)}), bf16[32,2,20,1024]{3,1,2,0:T(2,128)(2,1)S(1)}, u32[]{:S(2)}, u32[]{:S(2)}) %all-to-all-start) | async-done | bytes 2621472 | tf_op jit(solution)/shard_map/all_to_all | solution.py:46
  130.9 7.1 %fusion.17 = (bf16[32,2,20]{0,2,1:T(8,128)(2,1)S(1)}, f32[2,32,20,384]{3,1,2,0:T(8,128)}) fusion(f32[2,32,20,384]{3,1,2,0:T(8,128)} %fusion.6, f32[2,32,20,384]{3,1,2,0:T(8,128)} %fusion.4, bf16[2,3,1024,384]{3,2,0,1:T(8,128)(2,1)} %all-gather.2.cloned.1.call-done, bf16[32,2,20,1024]{3,1,2,0:T(2,128)(2,1)S(1)} %all-to-all-done), kind=kOutput, calls=%fused_computation.31 | convolution fusion | flops 1011055360 | bytes 10095104 | tf_op jit(solution)/shard_map/nscd,sdf->nscf/dot_general | solution.py:55
  138.0 0.7 copy.96
  138.8 4.5 %all-to-all-start.3 = ((bf16[32,2,20]{2,1,0:T(2,128)(2,1)}), bf16[32,2,20]{2,1,0:T(2,128)(2,1)S(1)}, u32[]{:S(2)}, u32[]{:S(2)}) async-start(bf16[32,2,20]{2,1,0:T(2,128)(2,1)} %copy.96), calls=%async_computation.3 | async-start | bytes 32768 | tf_op jit(solution)/shard_map/all_to_all | solution.py:61
  143.3 0.0 copy-start.5
  143.3 0.0 copy-start.6
  143.3 5.1 %fusion.18 = f32[2,32,20,1024]{3,1,2,0:T(8,128)S(1)} fusion(bf16[2,3,1024,384]{3,2,0,1:T(8,128)(2,1)} %all-gather.2.cloned.1.call-done, f32[2,32,20,384]{3,1,2,0:T(8,128)} %fusion.4, f32[2,32,20,384]{3,1,2,0:T(8,128)} %fusion.6, f32[2,32,20,384]{3,1,2,0:T(8,128)} %get-tuple-element.15), kind=kOutput, calls=%fused_computation.35 | convolution fusion | flops 1011548160 | bytes 12713984 | tf_op jit(solution)/shard_map/nscf,sdf->nscd/dot_general | solution.py:16
  148.4 3.1 fusion.1
  151.4 4.2 %copy.93 = bf16[32,2,20,1024]{3,1,2,0:T(2,128)(2,1)} copy(bf16[32,2,20,1024]{3,0,2,1:T(8,128)(2,1)S(1)} %fusion.1) | data formatting | bytes 5242880 | tf_op jit(solution)/shard_map/convert_element_type | solution.py:22
  155.6 0.0 all-to-all-done.3
  155.6 7.6 %all-to-all-start.2 = ((bf16[32,2,20,1024]{3,1,2,0:T(2,128)(2,1)}), bf16[32,2,20,1024]{3,1,2,0:T(2,128)(2,1)S(1)}, u32[]{:S(2)}, u32[]{:S(2)}) async-start(bf16[32,2,20,1024]{3,1,2,0:T(2,128)(2,1)} %copy.93), calls=%async_computation.2 | async-start | bytes 5242880 | tf_op jit(solution)/shard_map/all_to_all | solution.py:60
  163.3 0.0 copy-start.3
  163.3 0.0 reduce-scatter.4.cloned.1.call-start
  163.3 0.0 copy-done.4
  163.3 0.1 copy.81
  163.4 0.1 reshape.81
  163.6 6.8 %gather_fusion.3 = bf16[1024]{0:T(1024)(128)(2,1)S(1)} fusion(bf16[1280]{0:T(1024)(128)(2,1)S(1)} %reshape.81, s32[1024]{0:T(1024)S(1)} %broadcast_clamp_fusion), kind=kCustom, calls=%fused_computation.3 | custom fusion | bytes 8192 | tf_op jit(solution)/shard_map/gather | solution.py:64
  170.4 0.1 reshape.83
  170.5 0.1 multiply_reduce_fusion
  170.7 0.2 fusion.20
  170.9 0.8 copy.103
  171.7 0.0 reduce-scatter.4.cloned.1.call-update
  171.8 59.3 %reduce-scatter.4.cloned.1.call-done = bf16[64,64]{1,0:T(8,128)(2,1)} async-done(((bf16[1024,64]{1,0:T(8,128)(2,1)}), bf16[64,64]{1,0:T(8,128)(2,1)}) %reduce-scatter.4.cloned.1.call-update) | async-done | bytes 8208
  231.1 0.8 copy.104
  231.9 129.8 %psum.7 = f32[64,64]{0,1:T(8,128)S(1)} all-reduce(bf16[64,64]{0,1:T(8,128)(2,1)S(1)} %copy.104), channel_id=1, replica_groups=mesh['dp'=16,'expert'=32] {'expert'}, use_global_device_ids=true, to_apply=%region_9.10 | all-reduce | flops 4096 | bytes 24576 | tf_op jit(solution)/shard_map/psum | solution.py:79
  361.6 0.7 copy.99
  362.3 0.0 all-to-all-done.2
  362.3 2.6 copy.94
  365.0 3.6 reshape.80
  368.6 5.4 %gather_fusion.2 = bf16[1024,1024]{1,0:T(8,128)(2,1)} fusion(bf16[1280,1024]{1,0:T(8,128)(2,1)S(1)} %reshape.80, s32[1024]{0:T(1024)S(1)} %broadcast_clamp_fusion), kind=kCustom, calls=%fused_computation.2 | custom fusion | bytes 4198400 | tf_op jit(solution)/shard_map/gather | solution.py:63
  374.0 2.9 fusion
  376.9 0.9 fusion.19
  (20 shorter events, 0.2 us)
Async XLA Ops:
  7.2 369.8 %copy-start = (bf16[1024,64]{0,1:T(8,128)(2,1)S(1)}, bf16[1024,64]{0,1:T(8,128)(2,1)}, u32[]{:S(2)}) copy-start(bf16[1024,64]{0,1:T(8,128)(2,1)} %param.11) | copy-start | bytes 393220
  7.2 22.2 %copy-start.1 = (bf16[128,1024]{1,0:T(8,128)(2,1)S(1)}, bf16[128,1024]{1,0:T(8,128)(2,1)}, u32[]{:S(2)}) copy-start(bf16[128,1024]{1,0:T(8,128)(2,1)} %param.6) | copy-start | bytes 786436
  7.2 89.8 %all-gather.2.cloned.1.call-start = ((), (), s32[]{:S(2)}) async-start(), calls=%async_computation.5 | async-start | bytes 5013504 | tf_op jit(solution)/shard_map/all_gather | solution.py:48
  46.8 11.4 %copy-start.2 = (bf16[128,1024]{1,0:T(8,128)(2,1)S(1)}, bf16[128,1024]{1,0:T(8,128)(2,1)}, u32[]{:S(2)}) copy-start(bf16[128,1024]{1,0:T(8,128)(2,1)} %param.7) | copy-start | bytes 786436
  46.8 45.4 %all-to-all-start.1 = ((bf16[32,2,20,1024]{3,1,2,0:T(2,128)(2,1)}), bf16[32,2,20,1024]{3,1,2,0:T(2,128)(2,1)}, u32[]{:S(2)}, u32[]{:S(2)}) async-start(bf16[32,2,20,1024]{3,1,2,0:T(2,128)(2,1)} %copy.90), calls=%async_computation.1 | async-start | bytes 5242880 | tf_op jit(solution)/shard_map/all_to_all | solution.py:45
  92.2 38.7 %all-to-all-start = ((bf16[32,2,20,1024]{3,1,2,0:T(2,128)(2,1)}), bf16[32,2,20,1024]{3,1,2,0:T(2,128)(2,1)S(1)}, u32[]{:S(2)}, u32[]{:S(2)}) async-start(bf16[32,2,20,1024]{3,1,2,0:T(2,128)(2,1)} %copy.87), calls=%async_computation | async-start | bytes 5242880 | tf_op jit(solution)/shard_map/all_to_all | solution.py:46
  138.8 16.9 %all-to-all-start.3 = ((bf16[32,2,20]{2,1,0:T(2,128)(2,1)}), bf16[32,2,20]{2,1,0:T(2,128)(2,1)S(1)}, u32[]{:S(2)}, u32[]{:S(2)}) async-start(bf16[32,2,20]{2,1,0:T(2,128)(2,1)} %copy.96), calls=%async_computation.3 | async-start | bytes 32768 | tf_op jit(solution)/shard_map/all_to_all | solution.py:61
  143.3 5.1 %copy-start.5 = (f32[2,32,20,384]{3,1,2,0:T(8,128)S(1)}, f32[2,32,20,384]{3,1,2,0:T(8,128)}, u32[]{:S(2)}) copy-start(f32[2,32,20,384]{3,1,2,0:T(8,128)} %fusion.4) | copy-start | bytes 5898244
  143.3 5.1 %copy-start.6 = (f32[2,32,20,384]{3,1,2,0:T(8,128)S(1)}, f32[2,32,20,384]{3,1,2,0:T(8,128)}, u32[]{:S(2)}) copy-start(f32[2,32,20,384]{3,1,2,0:T(8,128)} %get-tuple-element.15) | copy-start | bytes 5898244
  155.6 7.7 %copy-start.4 = (f32[128,8]{0,1:T(8,128)S(1)}, f32[128,8]{0,1:T(8,128)}, u32[]{:S(2)}) copy-start(f32[128,8]{0,1:T(8,128)} %param.9) | copy-start | bytes 12292
  155.6 206.7 %all-to-all-start.2 = ((bf16[32,2,20,1024]{3,1,2,0:T(2,128)(2,1)}), bf16[32,2,20,1024]{3,1,2,0:T(2,128)(2,1)S(1)}, u32[]{:S(2)}, u32[]{:S(2)}) async-start(bf16[32,2,20,1024]{3,1,2,0:T(2,128)(2,1)} %copy.93), calls=%async_computation.2 | async-start | bytes 5242880 | tf_op jit(solution)/shard_map/all_to_all | solution.py:60
  163.3 7.4 %copy-start.3 = (s32[128,8]{0,1:T(8,128)S(1)}, s32[128,8]{0,1:T(8,128)}, u32[]{:S(2)}) copy-start(s32[128,8]{0,1:T(8,128)} %param.8) | copy-start | bytes 12292
  163.3 67.8 %reduce-scatter.4.cloned.1.call-start = ((), (), s32[]{:S(2)}) async-start(), calls=%async_computation.6 | async-start | bytes 278528
Sparse Core Ops, SparseCore 0:
  10.1 77.5 all-gather.1
  171.9 59.1 reduce-scatter.3
where the time goes:
time: 389 us; the launch traced here: 385 us
  blocking collectives  130 us (33%)
  waiting for transfers between devices  101 us (26%)
  local copies, waits for them, and re-layouts  59.4 us (15%)
  matrix products  29.4 us (8%)
  starting transfers between devices  28.3 us (7%)
  other arithmetic  22.1 us (6%)
  between operations  14.4 us (4%)
    psum x1, blocking collectives, body(): router_grad = lax.psum(partial_rows, 'expert')  130 us
    unnamed x3, waiting for transfers between devices  59.3 us
    all_to_all x1, waiting for transfers between devices, body(): lax.all_to_all(sent_x, 'expert', split_axis=0, concat_axis=0, tiled=True)  21.1 us
    all_to_all x1, waiting for transfers between devices, body(): lax.all_to_all(sent_dy, 'expert', split_axis=0, concat_axis=0, tiled=True)  20.9 us
    another operation x3, other arithmetic  18.2 us
    all_to_all x1, starting transfers between devices, body(): lax.all_to_all(sent_x, 'expert', split_axis=0, concat_axis=0, tiled=True)  11.4 us
    reshape x2, local copies, waits for them, and re-layouts, body(): sent_dy = padded_dy[owner_row].reshape(hosts, per_host, capacity, width)  7.79 us
  transfers between devices with their start and end apart: 6, of which 3 were waited for; matrix products, arithmetic and copies ran while one was open for 22% of the time, Pallas kernels for 0%

commit v1 on v0

v1 whole, which is shorter than its diff:
```python
import functools

import jax
import jax.numpy as jnp
import numpy as np
from jax import lax
from jax.experimental import pallas as pl
from jax.experimental.pallas import tpu as pltpu
from jax.sharding import PartitionSpec as P

F32 = jnp.float32
BF = jnp.bfloat16
CAP = 20
SLOTS = 2 * CAP
HOSTS = 32
ROWS = HOSTS * SLOTS
VMEM_LIMIT = 56 * 1024 * 1024


def slot_table():
    which = [0] * 16 + [1] * 16 + [0] * 4 + [1] * 4
    rank = list(range(16)) + list(range(16)) + list(range(16, 20)) + list(range(16, 20))
    return np.array(which), np.array(rank)


WHICH, RANK = slot_table()


def strict(rows, cols, upper):
    a = lax.broadcasted_iota(jnp.int32, (rows, cols), 0)
    b = lax.broadcasted_iota(jnp.int32, (rows, cols), 1)
    return jnp.where((a < b) if upper else (a > b), 1.0, 0.0).astype(BF)


def host_block(first, second):
    width = first.shape[-1]
    row = lax.broadcasted_iota(jnp.int32, (16, width), 0).astype(F32) + 1.0
    row8 = lax.broadcasted_iota(jnp.int32, (8, width), 0)
    mixed = jnp.where(
        row8 < 4, jnp.broadcast_to(first, (8, width)), jnp.broadcast_to(second, (8, width))
    )
    late = (row8 + jnp.where(row8 < 4, 17, 13)).astype(F32)
    return jnp.concatenate(
        [
            jnp.where(jnp.broadcast_to(first, (16, width)) == row, 1.0, 0.0),
            jnp.where(jnp.broadcast_to(second, (16, width)) == row, 1.0, 0.0),
            jnp.where(mixed == late, 1.0, 0.0),
        ],
        axis=0,
    )


def dispatch_kernel(ids_ref, x_ref, out_ref, hot_ref):
    experts, tokens = 2 * HOSTS, x_ref.shape[0]
    column = lax.broadcasted_iota(jnp.int32, (experts, tokens), 0)
    member = jnp.zeros((experts, tokens), F32)
    for k in range(ids_ref.shape[0]):
        member += jnp.where(ids_ref[k : k + 1, :] == column, 1.0, 0.0)
    before = jnp.dot(member.astype(BF), strict(tokens, tokens, True), preferred_element_type=F32)
    order = jnp.where(member > 0.0, before + 1.0, 0.0)
    for pair in range(HOSTS // 2):
        blocks = [
            host_block(order[2 * h : 2 * h + 1], order[2 * h + 1 : 2 * h + 2])
            for h in (2 * pair, 2 * pair + 1)
        ]
        hot_ref[80 * pair : 80 * pair + 80, :] = jnp.concatenate(blocks, axis=0).astype(BF)

    def step(i, carry):
        at = pl.ds(pl.multiple_of(i * 320, 320), 320)
        out_ref[at, :] = jnp.dot(
            hot_ref[at, :], x_ref[...], preferred_element_type=F32
        ).astype(BF)
        return carry

    lax.fori_loop(0, ROWS // 320, step, 0)


def vmem():
    return pl.BlockSpec(memory_space=pltpu.VMEM)


def smem():
    return pl.BlockSpec(memory_space=pltpu.SMEM)


def dispatch(ids_t, values):
    return pl.pallas_call(
        dispatch_kernel,
        out_shape=jax.ShapeDtypeStruct((ROWS, values.shape[1]), BF),
        in_specs=[vmem(), vmem()],
        out_specs=vmem(),
        scratch_shapes=[pltpu.VMEM((ROWS, values.shape[0]), BF)],
        compiler_params=pltpu.CompilerParams(vmem_limit_bytes=VMEM_LIMIT),
        name="dispatch",
    )(ids_t, values)


def pieces(block):
    return tuple(
        jnp.concatenate(
            [
                block[16 * e : 16 * e + 16],
                block[40 + 16 * e : 56 + 16 * e],
                block[32:40],
                block[72:80],
            ],
            axis=0,
        )
        for e in (0, 1)
    )


def expert_kernel(
    host_ref, route_ref, x_ref, dy_ref, w_ref, rw_ref,
    out_ref, share_ref, gg_ref, gate_ref, order_ref,
    xe_ref, dye_ref, re_ref, hot_ref, gcol_ref,
):
    sources = route_ref.shape[0]
    pairs = sources // 2
    width = route_ref.shape[2]
    ff = w_ref.shape[2] // 3
    ids = route_ref[:, 0:8, :]
    gates = route_ref[:, 8:16, :]
    upper = strict(width, width, True)
    host = host_ref[0]
    row8 = lax.broadcasted_iota(jnp.int32, (8, width), 0)
    row16 = lax.broadcasted_iota(jnp.int32, (16, width), 0).astype(F32) + 1.0
    total = jnp.zeros((sources, width), F32)
    for p in range(pairs):
        xs = pieces(x_ref[80 * p : 80 * p + 80, :].astype(F32))
        ys = pieces(dy_ref[80 * p : 80 * p + 80, :].astype(F32))
        for e in (0, 1):
            xe_ref[e, 48 * p : 48 * p + 48, :] = xs[e].astype(BF)
            dye_ref[e, 48 * p : 48 * p + 48, :] = ys[e].astype(BF)
    for e in (0, 1):
        wanted = (2 * host + e).astype(F32)
        match = ids == wanted
        member = jnp.sum(jnp.where(match, 1.0, 0.0), axis=1)
        gate = jnp.sum(jnp.where(match, gates, 0.0), axis=1)
        before = jnp.dot(member.astype(BF), upper, preferred_element_type=F32)
        order = jnp.where(member > 0.0, before + 1.0, 0.0)
        gate_ref[e] = gate
        order_ref[e] = order
        if e == 0:
            late = jnp.where(row8 < 4, row8 + 17, -1).astype(F32)
        else:
            late = jnp.where(row8 < 4, -1, row8 + 13).astype(F32)
        for p in range(pairs):
            a, b = order[2 * p : 2 * p + 1], order[2 * p + 1 : 2 * p + 2]
            ga, gb = gate[2 * p : 2 * p + 1], gate[2 * p + 1 : 2 * p + 2]
            wide = lambda v, n: jnp.broadcast_to(v, (n, width))
            hot = jnp.concatenate(
                [
                    jnp.where(wide(a, 16) == row16, 1.0, 0.0),
                    jnp.where(wide(b, 16) == row16, 1.0, 0.0),
                    jnp.where(wide(a, 8) == late, 1.0, 0.0),
                    jnp.where(wide(b, 8) == late, 1.0, 0.0),
                ],
                axis=0,
            )
            weight = jnp.concatenate([wide(ga, 16), wide(gb, 16), wide(ga, 8), wide(gb, 8)], axis=0)
            hot_ref[48 * p : 48 * p + 48, :] = hot
            gcol_ref[48 * p : 48 * p + 48, :] = jnp.sum(hot * weight, axis=1, keepdims=True)
        pre = jnp.dot(xe_ref[e], w_ref[e, :, 0 : 2 * ff], preferred_element_type=F32)
        hidden_grad = jnp.dot(dye_ref[e], w_ref[e, :, 2 * ff :], preferred_element_type=F32)
        pre_gate, pre_up = pre[:, 0:ff], pre[:, ff:]
        sigma = jax.nn.sigmoid(pre_gate)
        active = pre_gate * sigma
        hidden = (active * pre_up).astype(BF).astype(F32)
        gg = jnp.sum(hidden_grad * hidden, axis=1, keepdims=True).astype(BF).astype(F32)
        gcol = gcol_ref[...]
        scaled = hidden_grad * gcol
        gate_pre = (scaled * pre_up * sigma * (1.0 + pre_gate * (1.0 - sigma))).astype(BF)
        up_pre = (scaled * active).astype(BF)
        row = lax.dot_general(
            jnp.concatenate([gate_pre, up_pre], axis=1),
            w_ref[e, :, 0 : 2 * ff],
            (((1,), (1,)), ((), ())),
            preferred_element_type=F32,
        )
        row = row + (gcol * gg) * rw_ref[e : e + 1, :]
        re_ref[e] = row.astype(BF)
        for p in range(pairs):
            hit = hot_ref[48 * p : 48 * p + 48, :] * gg[48 * p : 48 * p + 48]
            first = jnp.sum(hit[0:16], axis=0, keepdims=True) + jnp.sum(hit[32:40], axis=0, keepdims=True)
            second = jnp.sum(hit[16:32], axis=0, keepdims=True) + jnp.sum(hit[40:48], axis=0, keepdims=True)
            gg_ref[e, 2 * p : 2 * p + 1, :] = first
            gg_ref[e, 2 * p + 1 : 2 * p + 2, :] = second
        total = total + gate * gg_ref[e]
    share_ref[...] = total
    for p in range(pairs):
        r0 = re_ref[0, 48 * p : 48 * p + 48, :].astype(F32)
        r1 = re_ref[1, 48 * p : 48 * p + 48, :].astype(F32)
        out_ref[80 * p : 80 * p + 80, :] = jnp.concatenate(
            [
                r0[0:16], r1[0:16], r0[32:40] + r1[32:40],
                r0[16:32], r1[16:32], r0[40:48] + r1[40:48],
            ],
            axis=0,
        ).astype(BF)


def expert_rows(host, route, x_rows, dy_rows, weights, rw_rows):
    steps = 2
    sources = HOSTS // steps
    rows = ROWS // steps
    width = route.shape[2]
    model = x_rows.shape[1]
    compact = sources * 24
    dense = jax.ShapeDtypeStruct((2, HOSTS, width), F32)
    dense_spec = pl.BlockSpec((2, sources, width), lambda i: (0, i, 0))
    row_spec = pl.BlockSpec((rows, model), lambda i: (i, 0))
    return pl.pallas_call(
        expert_kernel,
        grid=(steps,),
        out_shape=(
            jax.ShapeDtypeStruct((ROWS, model), BF),
            jax.ShapeDtypeStruct((HOSTS, width), F32),
            dense, dense, dense,
        ),
        in_specs=[
            smem(),
            pl.BlockSpec((sources, 16, width), lambda i: (i, 0, 0)),
            row_spec, row_spec,
            pl.BlockSpec(weights.shape, lambda i: (0, 0, 0)),
            pl.BlockSpec(rw_rows.shape, lambda i: (0, 0)),
        ],
        out_specs=(
            row_spec,
            pl.BlockSpec((sources, width), lambda i: (i, 0)),
            dense_spec, dense_spec, dense_spec,
        ),
        scratch_shapes=[
            pltpu.VMEM((2, compact, model), BF),
            pltpu.VMEM((2, compact, model), BF),
            pltpu.VMEM((2, compact, model), BF),
            pltpu.VMEM((compact, width), F32),
            pltpu.VMEM((compact, 1), F32),
        ],
        compiler_params=pltpu.CompilerParams(vmem_limit_bytes=VMEM_LIMIT),
        name="expert_rows",
    )(host, route, x_rows, dy_rows, weights, rw_rows)


def router_kernel(shares_ref, gg_ref, gate_ref, order_ref, mask_ref, x_ref, part_ref, sum_ref, hot_ref):
    total = shares_ref[0:HOSTS, :]
    for h in range(1, HOSTS):
        total = total + shares_ref[HOSTS * h : HOSTS * h + HOSTS, :]
    sum_ref[...] = total
    logit = jnp.concatenate([gate_ref[e] * (gg_ref[e] - total) for e in (0, 1)], axis=0).astype(BF)
    for pair in range(HOSTS // 2):
        blocks = [
            host_block(order_ref[0, s : s + 1, :], order_ref[1, s : s + 1, :])
            for s in (2 * pair, 2 * pair + 1)
        ]
        hot_ref[80 * pair : 80 * pair + 80, :] = jnp.concatenate(blocks, axis=0).astype(BF)
    spread = lax.dot_general(
        logit, hot_ref[...], (((1,), (1,)), ((), ())), preferred_element_type=F32
    ) * mask_ref[...].astype(F32)
    lines = [jnp.sum(spread[32 * e : 32 * e + 32], axis=0, keepdims=True) for e in (0, 1)]
    lines = jnp.concatenate(lines + [jnp.zeros((6, ROWS), F32)], axis=0).astype(BF)
    part_ref[...] = jnp.dot(lines, x_ref[...], preferred_element_type=F32)


def router_part(shares, gg, gate, order, x_rows):
    slot = np.arange(ROWS)
    mask = np.concatenate(
        [
            (np.arange(HOSTS)[:, None] == slot[None, :] // SLOTS) & (WHICH[slot % SLOTS] == e)[None, :]
            for e in (0, 1)
        ],
        axis=0,
    )
    return pl.pallas_call(
        router_kernel,
        out_shape=(
            jax.ShapeDtypeStruct((8, x_rows.shape[1]), F32),
            jax.ShapeDtypeStruct((HOSTS, gg.shape[2]), F32),
        ),
        in_specs=[vmem()] * 6,
        out_specs=(vmem(), vmem()),
        scratch_shapes=[pltpu.VMEM((ROWS, gg.shape[2]), BF)],
        compiler_params=pltpu.CompilerParams(vmem_limit_bytes=VMEM_LIMIT),
        name="router_part",
    )(shares, gg, gate, order, jnp.asarray(mask.astype(np.float32), BF), x_rows)


def combine_kernel(host_ref, ids_ref, gates_ref, sum_ref, expand_ref, rank_ref, rw_ref, rows_ref, out_ref):
    tokens, top = ids_ref.shape
    experts = rw_ref.shape[0]
    column = lax.broadcasted_iota(jnp.int32, (tokens, experts), 1)
    member = jnp.zeros((tokens, experts), F32)
    dense = jnp.zeros((tokens, experts), F32)
    for k in range(top):
        match = ids_ref[:, k : k + 1] == column
        member += jnp.where(match, 1.0, 0.0)
        dense += jnp.where(match, gates_ref[:, k : k + 1], 0.0)
    before = jnp.dot(strict(tokens, tokens, False), member.astype(BF), preferred_element_type=F32)
    order = jnp.where(member > 0.0, before + 1.0, 0.0).astype(BF)
    wide = jnp.dot(order, expand_ref[...], preferred_element_type=F32)
    hot = jnp.where(wide == rank_ref[...], 1.0, 0.0).astype(BF)
    own = jnp.broadcast_to(sum_ref[pl.ds(host_ref[0], 1), :], (tokens, tokens))
    diagonal = lax.broadcasted_iota(jnp.int32, (tokens, tokens), 0) == lax.broadcasted_iota(
        jnp.int32, (tokens, tokens), 1
    )
    own = jnp.sum(jnp.where(diagonal, own, 0.0), axis=1, keepdims=True)
    lost = jnp.dot((dense * own).astype(BF), rw_ref[...], preferred_element_type=F32)
    out_ref[...] = (jnp.dot(hot, rows_ref[...], preferred_element_type=F32) - lost).astype(BF)


def combine(host, ids, gates, sums, rw_t, rows):
    slot = np.arange(ROWS)
    expert = 2 * (slot // SLOTS) + WHICH[slot % SLOTS]
    expand = (np.arange(2 * HOSTS)[:, None] == expert[None, :]).astype(np.float32)
    rank = (RANK[slot % SLOTS] + 1.0).astype(np.float32)[None, :]
    return pl.pallas_call(
        combine_kernel,
        out_shape=jax.ShapeDtypeStruct((ids.shape[0], rows.shape[1]), BF),
        in_specs=[smem()] + [vmem()] * 7,
        out_specs=vmem(),
        compiler_params=pltpu.CompilerParams(vmem_limit_bytes=VMEM_LIMIT),
        name="combine",
    )(host, ids, gates, sums, jnp.asarray(expand, BF), jnp.asarray(rank), rw_t, rows)


def exchange(rows):
    return lax.all_to_all(rows, "expert", split_axis=0, concat_axis=0, tiled=True)


def body(tokens, upstream, expert_ids, gates, expert_weights, router_weight):
    model = tokens.shape[1]
    per_host, _, part, ff = expert_weights.shape
    host = lax.axis_index("expert").astype(jnp.int32)
    group = lax.axis_index("dp").astype(jnp.int32)
    host_arr = host.reshape(1)
    ids_t = expert_ids.T
    shard = expert_weights.transpose(0, 2, 1, 3).reshape(per_host, part, 3 * ff)
    weights = lax.all_gather(shard, "dp", axis=1, tiled=True)
    x_rows = exchange(dispatch(ids_t, tokens))
    dy_rows = exchange(dispatch(ids_t, upstream))
    route = jnp.concatenate([ids_t.astype(F32), gates.T], axis=0)
    route = lax.all_gather(route, "expert", axis=0, tiled=False)
    rw_t = router_weight.T
    rw_rows = lax.dynamic_slice_in_dim(rw_t, per_host * host, per_host, 0).astype(F32)
    rows, share, gg, gate, order = expert_rows(host_arr, route, x_rows, dy_rows, weights, rw_rows)
    back = exchange(rows)
    shares = lax.all_gather(share, "expert", axis=0, tiled=True)
    piece, sums = router_part(shares, gg, gate, order, x_rows)
    everyone = lax.all_gather(piece[:per_host].reshape(-1, 128), "dp", axis=0, tiled=False)
    column = jnp.sum(everyone, axis=0).reshape(per_host, model)
    column = lax.dynamic_slice_in_dim(column, part * group, part, 1)
    columns = lax.all_gather(column.reshape(1, -1), "expert", axis=0, tiled=True)
    router_grad = columns.reshape(-1, part).T
    token_grad = combine(host_arr, expert_ids, gates, sums, rw_t, back)
    return (token_grad, router_grad)


def solution(mesh):
    in_specs = (
        P(("dp", "expert"), None),
        P(("dp", "expert"), None),
        P(("dp", "expert"), None),
        P(("dp", "expert"), None),
        P("expert", None, "dp", None),
        P(),
    )
    out_specs = (P(("dp", "expert"), None), P("dp", None))
    return jax.shard_map(body, mesh=mesh, in_specs=in_specs, out_specs=out_specs, check_vma=False)
```

time: 389 us -> 261 us (0.67)
  waiting for transfers between devices: 101 us -> 30 us
  local copies, waits for them, and re-layouts: 59.4 us -> 8.43 us
  matrix products: 29.4 us -> 0 us
  Pallas kernels: 0 us -> 27.5 us
  blocking collectives: 130 us -> 157 us
  other arithmetic: 22.1 us -> 2.03 us
  starting transfers between devices: 28.3 us -> 21.2 us
    all_gather x0 -> x4, blocking collectives: none -> 157 us  [the longest x1 51.8 us: body(): route = lax.all_gather(route, 'expert', axis=0, tiled=False)]
    psum x1 -> x0, blocking collectives: 130 us -> none  [body(): router_grad = lax.psum(partial_rows, 'expert')]
    unnamed x3 -> x1, waiting for transfers between devices: 59.3 us -> 0.02 us
    dot_general x7 -> x0, matrix products: 29.4 us -> none  [the longest x1 7.09 us: body(): jnp.einsum('nscd,sdf->nscf', arrived_dy, whole[:, 2], preferred_element_t...]
    pallas_call x0 -> x5, Pallas kernels: none -> 27.5 us  [the longest x1 12.3 us: expert_rows(): pl.pallas_call(expert_kernel, grid=(steps,), out_shape=(jax.ShapeDtypeStr...]
    gather x4 -> x0, local copies, waits for them, and re-layouts: 22.4 us -> none  [the longest x1 6.8 us: body(): back_gate.reshape(-1)[target].reshape(tok_count, top).astype(jnp.float32)]
    another operation x3 -> x0, other arithmetic: 18.2 us -> none
    reshape x6 -> x4, local copies, waits for them, and re-layouts: 19.2 us -> 2.49 us  [the longest x1 1.71 us: body(): shard = expert_weights.transpose(0, 2, 1, 3).reshape(per_host, part, 3 * ff)]
  transfers between devices with their start and end apart: 6 -> 4, of which waited for: 3 -> 1; matrix products, arithmetic and copies ran while one was open for 22% -> 2% of each run, Pallas kernels for 0% -> 4%
where the time goes in v1:
time: 261 us; the launch traced here: 260 us
  blocking collectives  157 us (60%)
  waiting for transfers between devices  30 us (11%)
  Pallas kernels  27.5 us (11%)
  starting transfers between devices  21.2 us (8%)
  between operations  14.1 us (5%)
  local copies, waits for them, and re-layouts  8.43 us (3%)
    all_gather x1, blocking collectives, body(): route = lax.all_gather(route, 'expert', axis=0, tiled=False)  51.8 us
    all_gather x1, blocking collectives, body(): shares = lax.all_gather(share, 'expert', axis=0, tiled=True)  50.6 us
    all_to_all x3, waiting for transfers between devices, exchange(): lax.all_to_all(rows, 'expert', split_axis=0, concat_axis=0, tiled=True)  30 us
    all_gather x1, blocking collectives, body(): lax.all_gather(column.reshape(1, -1), 'expert', axis=0, tiled=True)  27.5 us
    all_gather x1, blocking collectives, body(): lax.all_gather(piece[:per_host].reshape(-1, 128), 'dp', axis=0, tiled=False)  26.8 us
    all_to_all x3, starting transfers between devices, exchange(): lax.all_to_all(rows, 'expert', split_axis=0, concat_axis=0, tiled=True)  21.2 us
    pallas_call x1, Pallas kernels, expert_rows(): pl.pallas_call(expert_kernel, grid=(steps,), out_shape=(jax.ShapeDtypeStr...  12.3 us
    pallas_call x2, Pallas kernels, dispatch(): pl.pallas_call(dispatch_kernel, out_shape=jax.ShapeDtypeStruct((ROWS, val...  7.95 us
  transfers between devices with their start and end apart: 4, of which 1 were waited for; matrix products, arithmetic and copies ran while one was open for 2% of the time, Pallas kernels for 4%

profile of v1, /device:TPU:1, one launch (start us, length us, event | category | flops | bytes accessed | tf_op | source)
XLA Modules:
  0.0 259.8 jit_solution(13223399181045464040)
XLA Ops:
  7.2 0.0 all-gather.4.cloned.1.call-start
  7.2 1.7 copy.23
  8.9 0.0 all-gather.4.cloned.1.call-update
  8.9 4.0 %dispatch.2 = bf16[1280,1024]{1,0:T(8,128)(2,1)} custom-call(s32[8,128]{1,0:T(8,128)} %bitcast.28, bf16[128,1024]{1,0:T(8,128)(2,1)} %x_ref.2), custom_call_target="tpu_custom_call" | custom-call | tf_op jit(solution)/shard_map/dispatch/pallas_call | solution.py:87
  12.9 10.6 %all-to-all-start = ((bf16[32,40,1024]{2,1,0:T(8,128)(2,1)}), bf16[32,40,1024]{2,1,0:T(8,128)(2,1)S(1)}, u32[]{:S(2)}, u32[]{:S(2)}) async-start(bf16[32,40,1024]{2,1,0:T(8,128)(2,1)} %bitcast.22), calls=%async_computation | async-start | bytes 5242880 | tf_op jit(solution)/shard_map/all_to_all | solution.py:327
  23.5 4.0 %dispatch.3 = bf16[1280,1024]{1,0:T(8,128)(2,1)} custom-call(s32[8,128]{1,0:T(8,128)} %bitcast.29, bf16[128,1024]{1,0:T(8,128)(2,1)} %x_ref.3), custom_call_target="tpu_custom_call" | custom-call | tf_op jit(solution)/shard_map/dispatch/pallas_call | solution.py:87
  27.5 30.0 %all-to-all-done = bf16[32,40,1024]{2,1,0:T(8,128)(2,1)S(1)} async-done(((bf16[32,40,1024]{2,1,0:T(8,128)(2,1)}), bf16[32,40,1024]{2,1,0:T(8,128)(2,1)S(1)}, u32[]{:S(2)}, u32[]{:S(2)}) %all-to-all-start) | async-done | bytes 2621472 | tf_op jit(solution)/shard_map/all_to_all | solution.py:327
  57.5 0.0 copy-start
  57.5 0.0 copy-start.2
  57.5 0.0 copy-start.4
  57.5 1.5 copy-done
  59.0 5.4 %all-to-all-start.1 = ((bf16[32,40,1024]{2,1,0:T(8,128)(2,1)}), bf16[32,40,1024]{2,1,0:T(8,128)(2,1)}, u32[]{:S(2)}, u32[]{:S(2)}) async-start(bf16[32,40,1024]{2,1,0:T(8,128)(2,1)} %bitcast.21), calls=%async_computation.1 | async-start | bytes 5242880 | tf_op jit(solution)/shard_map/all_to_all | solution.py:327
  64.4 0.0 copy-done.2
  64.4 0.0 copy-done.4
  64.4 51.8 %all-gather = f32[512,128]{1,0:T(8,128)} all-gather(f32[16,128]{1,0:T(8,128)S(1)} %pad_maximum_fusion), channel_id=2, replica_groups=mesh['dp'=16,'expert'=32] {'expert'}, dimensions={0}, use_global_device_ids=true | all-gather | bytes 270336 | tf_op jit(solution)/shard_map/all_gather | solution.py:342
  116.2 1.3 convert_bitcast_fusion.rw_ref
  117.5 0.0 all-to-all-done.1
  117.5 0.0 all-gather.4.cloned.1.call-done.w_ref
  117.5 12.3 %expert_rows.1 = (bf16[1280,1024]{1,0:T(8,128)(2,1)}, f32[32,128]{1,0:T(8,128)}, f32[2,32,128]{2,1,0:T(8,128)}, f32[2,32,128]{2,1,0:T(8,128)}, f32[2,32,128]{2,1,0:T(8,128)}) custom-call(s32[1]{0:T(128)} %bitcast.host_ref, f32[32,16,128]{2,1,0:T(8,128)} %bitcast.25, bf16[1280,1024]{1,0:T(8,128)(2,1)} %bitcast.18, bf16[1280,1024]{1,0:T(8,128)(2,1)} %bitcast.7.dy_ref, ...), custom_call_target="tpu_custom_call" | custom-call | tf_op jit(solution)/shard_map/expert_rows/pallas_call | solution.py:213
  129.8 0.0 copy-start.3
  129.8 5.2 %all-to-all-start.2 = ((bf16[32,40,1024]{2,1,0:T(8,128)(2,1)}), bf16[32,40,1024]{2,1,0:T(8,128)(2,1)S(1)}, u32[]{:S(2)}, u32[]{:S(2)}) async-start(bf16[32,40,1024]{2,1,0:T(8,128)(2,1)} %bitcast.23), calls=%async_computation.2 | async-start | bytes 5242880 | tf_op jit(solution)/shard_map/all_to_all | solution.py:327
  135.0 0.7 copy.20.ids_ref
  135.8 0.7 copy.21.gates_ref
  136.5 0.0 copy-done.3
  136.5 50.6 %all_gather.21.shares_ref = f32[1024,128]{1,0:T(8,128)} all-gather(f32[32,128]{1,0:T(8,128)S(1)} %copy-done.3), channel_id=1, replica_groups=mesh['dp'=16,'expert'=32] {'expert'}, dimensions={0}, use_global_device_ids=true | all-gather | bytes 540672 | tf_op jit(solution)/shard_map/all_gather | solution.py:347
  187.1 3.3 %router_part.1 = (f32[8,1024]{1,0:T(8,128)}, f32[32,128]{1,0:T(8,128)}) custom-call(f32[1024,128]{1,0:T(8,128)} %all_gather.21.shares_ref, f32[2,32,128]{2,1,0:T(8,128)} %get-tuple-element.10.gg_ref, f32[2,32,128]{2,1,0:T(8,128)} %get-tuple-element.11.gate_ref, f32[2,32,128]{2,1,0:T(8,128)} %get-tuple-element.12.order_ref, ...), custom_call_target="tpu_custom_call" | custom-call | tf_op jit(solution)/shard_map/router_part/pallas_call | solution.py:274
  190.3 0.8 slice.3
  191.1 26.8 %all_gather.22 = f32[16,16,128]{2,1,0:T(8,128)S(1)} all-gather(f32[1,16,128]{2,1,0:T(8,128)S(1)} %all_gather_reshape.3), channel_id=1, replica_groups=mesh['dp'=16,'expert'=32] {'dp'}, dimensions={0}, use_global_device_ids=true | all-gather | bytes 139264 | tf_op jit(solution)/shard_map/all_gather | solution.py:349
  217.9 0.1 constant_dynamic-slice_fusion
  218.0 0.1 reshape.31
  218.1 27.5 %all-gather.1 = f32[32,1,128]{2,1,0:T(1,128)S(1)} all-gather(f32[1,1,128]{2,1,0:T(1,128)S(1)} %reshape.31), channel_id=1, replica_groups=mesh['dp'=16,'expert'=32] {'expert'}, dimensions={0}, use_global_device_ids=true | all-gather | bytes 16896 | tf_op jit(solution)/shard_map/all_gather | solution.py:352
  245.5 0.5 broadcast.3
  246.0 0.7 reduce.3
  246.7 0.1 reshape.29
  246.8 0.7 copy.22
  247.5 0.0 all-to-all-done.2
  247.5 0.0 copy-start.1
  247.5 1.5 copy-done.1
  249.0 4.0 %combine.1 = bf16[128,1024]{1,0:T(8,128)(2,1)} custom-call(s32[1]{0:T(128)} %bitcast.host_ref, s32[128,8]{1,0:T(8,128)} %copy.20.ids_ref, f32[128,8]{1,0:T(8,128)} %copy.21.gates_ref, f32[32,128]{1,0:T(8,128)} %get-tuple-element.13.sum_ref, bf16[64,1280]{1,0:T(8,128)(2,1)} %constant.26.clone.expand_ref, f32[1,1280]{1,0:T(1,128)} %constant.27.clone.rank_ref, ...), custom_call_target="tpu_custom_call" | custom-call | tf_op jit(solution)/shard_map/combine/pallas_call | solution.py:316
  (5 shorter events, 0.1 us)
Async XLA Ops:
  7.2 110.4 %all-gather.4.cloned.1.call-start = ((), (), s32[]{:S(2)}) async-start(), calls=%async_computation.3 | async-start | bytes 5013504 | tf_op jit(solution)/shard_map/all_gather | solution.py:338
  12.9 44.6 %all-to-all-start = ((bf16[32,40,1024]{2,1,0:T(8,128)(2,1)}), bf16[32,40,1024]{2,1,0:T(8,128)(2,1)S(1)}, u32[]{:S(2)}, u32[]{:S(2)}) async-start(bf16[32,40,1024]{2,1,0:T(8,128)(2,1)} %bitcast.22), calls=%async_computation | async-start | bytes 5242880 | tf_op jit(solution)/shard_map/all_to_all | solution.py:327
  57.5 1.5 copy-start
  57.5 6.9 %copy-start.2 = (s32[128,8]{0,1:T(8,128)S(1)}, s32[128,8]{0,1:T(8,128)}, u32[]{:S(2)}) copy-start(s32[128,8]{0,1:T(8,128)} %param.11) | copy-start | bytes 12292
  57.5 6.9 %copy-start.4 = (f32[128,8]{0,1:T(8,128)S(1)}, f32[128,8]{0,1:T(8,128)}, u32[]{:S(2)}) copy-start(f32[128,8]{0,1:T(8,128)} %param.12) | copy-start | bytes 12292
  59.0 58.6 %all-to-all-start.1 = ((bf16[32,40,1024]{2,1,0:T(8,128)(2,1)}), bf16[32,40,1024]{2,1,0:T(8,128)(2,1)}, u32[]{:S(2)}, u32[]{:S(2)}) async-start(bf16[32,40,1024]{2,1,0:T(8,128)(2,1)} %bitcast.21), calls=%async_computation.1 | async-start | bytes 5242880 | tf_op jit(solution)/shard_map/all_to_all | solution.py:327
  129.8 6.7 %copy-start.3 = (f32[32,128]{1,0:T(8,128)S(1)}, f32[32,128]{1,0:T(8,128)}, u32[]{:S(2)}) copy-start(f32[32,128]{1,0:T(8,128)} %get-tuple-element.9) | copy-start | bytes 49156
  129.8 117.7 %all-to-all-start.2 = ((bf16[32,40,1024]{2,1,0:T(8,128)(2,1)}), bf16[32,40,1024]{2,1,0:T(8,128)(2,1)S(1)}, u32[]{:S(2)}, u32[]{:S(2)}) async-start(bf16[32,40,1024]{2,1,0:T(8,128)(2,1)} %bitcast.23), calls=%async_computation.2 | async-start | bytes 5242880 | tf_op jit(solution)/shard_map/all_to_all | solution.py:327
  247.5 1.5 copy-start.1
Sparse Core Ops, SparseCore 0:
  10.1 77.6 all-gather.3

commit v2 on v1

v2 whole, which is shorter than its diff:
```python
import functools

import jax
import jax.numpy as jnp
import numpy as np
from jax import lax
from jax.experimental import pallas as pl
from jax.experimental.pallas import tpu as pltpu
from jax.sharding import PartitionSpec as P

F32 = jnp.float32
BF = jnp.bfloat16
CAP = 20
SLOTS = 2 * CAP
HOSTS = 32
ROWS = HOSTS * SLOTS
BLOCK = 2 * SLOTS + 8
TOKENS = 128


def slot_table():
    which = [0] * 16 + [1] * 16 + [0] * 4 + [1] * 4
    rank = list(range(16)) + list(range(16)) + list(range(16, 20)) + list(range(16, 20))
    return np.array(which), np.array(rank)


WHICH, RANK = slot_table()


def strict(rows, cols, upper):
    a = lax.broadcasted_iota(jnp.int32, (rows, cols), 0)
    b = lax.broadcasted_iota(jnp.int32, (rows, cols), 1)
    return jnp.where((a < b) if upper else (a > b), 1.0, 0.0).astype(BF)


def host_block(first, second):
    width = first.shape[-1]
    row = lax.broadcasted_iota(jnp.int32, (16, width), 0).astype(F32) + 1.0
    row8 = lax.broadcasted_iota(jnp.int32, (8, width), 0)
    mixed = jnp.where(
        row8 < 4, jnp.broadcast_to(first, (8, width)), jnp.broadcast_to(second, (8, width))
    )
    late = (row8 + jnp.where(row8 < 4, 17, 13)).astype(F32)
    return jnp.concatenate(
        [
            jnp.where(jnp.broadcast_to(first, (16, width)) == row, 1.0, 0.0),
            jnp.where(jnp.broadcast_to(second, (16, width)) == row, 1.0, 0.0),
            jnp.where(mixed == late, 1.0, 0.0),
        ],
        axis=0,
    )


def dispatch_kernel(ids_ref, gates_ref, x_ref, dy_ref, out_ref, hot_ref):
    experts, tokens = 2 * HOSTS, x_ref.shape[0]
    top = ids_ref.shape[0]
    column = lax.broadcasted_iota(jnp.int32, (experts, tokens), 0)
    member = jnp.zeros((experts, tokens), F32)
    for k in range(top):
        member += jnp.where(ids_ref[k : k + 1, :] == column, 1.0, 0.0)
    before = jnp.dot(member.astype(BF), strict(tokens, tokens, True), preferred_element_type=F32)
    order = jnp.where(member > 0.0, before + 1.0, 0.0)
    for pair in range(HOSTS // 2):
        blocks = [
            host_block(order[2 * h : 2 * h + 1], order[2 * h + 1 : 2 * h + 2])
            for h in (2 * pair, 2 * pair + 1)
        ]
        hot_ref[80 * pair : 80 * pair + 80, :] = jnp.concatenate(blocks, axis=0).astype(BF)
    line = lambda ref: jnp.concatenate([ref[k : k + 1, :] for k in range(top)], axis=1)
    left = line(gates_ref)
    routes = [line(ids_ref).astype(F32)]
    for _ in range(3):
        high = left.astype(BF).astype(F32)
        routes.append(high)
        left = left - high
    routes = jnp.concatenate(routes + [jnp.zeros((4, top * tokens), F32)], axis=0)

    def step(i, carry):
        hot = hot_ref[pl.ds(pl.multiple_of(i * 320, 320), 320), :]
        xs = jnp.dot(hot, x_ref[...], preferred_element_type=F32)
        ys = jnp.dot(hot, dy_ref[...], preferred_element_type=F32)
        for j in range(8):
            block = jnp.concatenate(
                [xs[40 * j : 40 * j + 40], ys[40 * j : 40 * j + 40], routes], axis=0
            )
            out_ref[8 * i + j] = block.astype(BF)
        return carry

    lax.fori_loop(0, ROWS // 320, step, 0)


def vmem():
    return pl.BlockSpec(memory_space=pltpu.VMEM)


def smem():
    return pl.BlockSpec(memory_space=pltpu.SMEM)


def params(mib):
    return pltpu.CompilerParams(vmem_limit_bytes=mib * 1024 * 1024)


def cost(flops, moved):
    return pl.CostEstimate(flops=flops, bytes_accessed=moved, transcendentals=0)


def dispatch(ids_t, gates_t, tokens, upstream):
    return pl.pallas_call(
        dispatch_kernel,
        out_shape=jax.ShapeDtypeStruct((HOSTS, BLOCK, tokens.shape[1]), BF),
        in_specs=[vmem()] * 4,
        out_specs=vmem(),
        scratch_shapes=[pltpu.VMEM((ROWS, tokens.shape[0]), BF)],
        compiler_params=params(56),
        name="dispatch",
    )(ids_t, gates_t, tokens, upstream)


def pieces(a, b, start, e):
    at = start + 16 * e
    return jnp.concatenate(
        [a[at : at + 16], b[at : at + 16], a[start + 32 : start + 40], b[start + 32 : start + 40]],
        axis=0,
    ).astype(BF)


def forward_kernel(
    host_ref, rows_ref, w_ref,
    xe_ref, hot_ref, gu_ref, add_ref, gg_ref, gate_ref, share_ref,
    dye_ref, ids_ref, gates_ref, wide_ref, gcol_ref,
):
    sources = rows_ref.shape[0]
    pairs = sources // 2
    width = hot_ref.shape[3]
    top = ids_ref.shape[1] // width
    ff = w_ref.shape[2] // 3
    for p in range(pairs):
        a, b = rows_ref[2 * p].astype(F32), rows_ref[2 * p + 1].astype(F32)
        for e in (0, 1):
            xe_ref[0, e, 48 * p : 48 * p + 48, :] = pieces(a, b, 0, e)
            dye_ref[e, 48 * p : 48 * p + 48, :] = pieces(a, b, SLOTS, e)
        for n, block in ((2 * p, a), (2 * p + 1, b)):
            ids_ref[n : n + 1, :] = block[80:81]
            gates_ref[n : n + 1, :] = block[81:82] + block[82:83] + block[83:84]
    upper = strict(width, width, True)
    host = host_ref[0]
    row8 = lax.broadcasted_iota(jnp.int32, (8, width), 0)
    row16 = lax.broadcasted_iota(jnp.int32, (16, width), 0).astype(F32) + 1.0
    total = jnp.zeros((sources, width), F32)
    spread = lambda v, n: jnp.broadcast_to(v, (n, width))
    for e in (0, 1):
        wanted = (2 * host + e).astype(F32)
        member = jnp.zeros((sources, width), F32)
        gate = jnp.zeros((sources, width), F32)
        for k in range(top):
            match = ids_ref[:, width * k : width * k + width] == wanted
            member += jnp.where(match, 1.0, 0.0)
            gate += jnp.where(match, gates_ref[:, width * k : width * k + width], 0.0)
        before = jnp.dot(member.astype(BF), upper, preferred_element_type=F32)
        order = jnp.where(member > 0.0, before + 1.0, 0.0)
        gate_ref[e] = gate
        if e == 0:
            late = jnp.where(row8 < 4, row8 + 17, -1).astype(F32)
        else:
            late = jnp.where(row8 < 4, -1, row8 + 13).astype(F32)
        for p in range(pairs):
            a, b = order[2 * p : 2 * p + 1], order[2 * p + 1 : 2 * p + 2]
            ga, gb = gate[2 * p : 2 * p + 1], gate[2 * p + 1 : 2 * p + 2]
            hot = jnp.concatenate(
                [
                    jnp.where(spread(a, 16) == row16, 1.0, 0.0),
                    jnp.where(spread(b, 16) == row16, 1.0, 0.0),
                    jnp.where(spread(a, 8) == late, 1.0, 0.0),
                    jnp.where(spread(b, 8) == late, 1.0, 0.0),
                ],
                axis=0,
            )
            weight = jnp.concatenate(
                [spread(ga, 16), spread(gb, 16), spread(ga, 8), spread(gb, 8)], axis=0
            )
            wide_ref[48 * p : 48 * p + 48, :] = hot
            hot_ref[0, e, 48 * p : 48 * p + 48, :] = hot.astype(BF)
            gcol_ref[48 * p : 48 * p + 48, :] = jnp.sum(hot * weight, axis=1, keepdims=True)
        pre = jnp.dot(xe_ref[0, e], w_ref[e, :, 0 : 2 * ff], preferred_element_type=F32)
        hidden_grad = jnp.dot(dye_ref[e], w_ref[e, :, 2 * ff :], preferred_element_type=F32)
        pre_gate, pre_up = pre[:, 0:ff], pre[:, ff:]
        sigma = jax.nn.sigmoid(pre_gate)
        active = pre_gate * sigma
        hidden = (active * pre_up).astype(BF).astype(F32)
        gg = jnp.sum(hidden_grad * hidden, axis=1, keepdims=True).astype(BF).astype(F32)
        gcol = gcol_ref[...]
        scaled = hidden_grad * gcol
        gu_ref[0, e, :, 0:ff] = (
            scaled * pre_up * sigma * (1.0 + pre_gate * (1.0 - sigma))
        ).astype(BF)
        gu_ref[0, e, :, ff:] = (scaled * active).astype(BF)
        add_ref[0, e] = gcol * gg
        for p in range(pairs):
            hit = wide_ref[48 * p : 48 * p + 48, :] * gg[48 * p : 48 * p + 48]
            down = lambda v: jnp.sum(v, axis=0, keepdims=True)
            gg_ref[e, 2 * p : 2 * p + 1, :] = down(hit[0:16]) + down(hit[32:40])
            gg_ref[e, 2 * p + 1 : 2 * p + 2, :] = down(hit[16:32]) + down(hit[40:48])
        total = total + gate * gg_ref[e]
    for h in range(HOSTS):
        share_ref[h] = total


def forward(host, blocks, weights):
    halves, sources, width = 2, HOSTS // 2, TOKENS
    model = blocks.shape[2]
    ff = weights.shape[2] // 3
    compact = sources * 24
    shape = lambda last, kind: jax.ShapeDtypeStruct((halves, 2, compact, last), kind)
    spec = lambda last: pl.BlockSpec((1, 2, compact, last), lambda i: (i, 0, 0, 0))
    dense = jax.ShapeDtypeStruct((2, HOSTS, width), F32)
    dense_spec = pl.BlockSpec((2, sources, width), lambda i: (0, i, 0))
    return pl.pallas_call(
        forward_kernel,
        grid=(halves,),
        out_shape=(
            shape(model, BF), shape(width, BF), shape(2 * ff, BF), shape(1, F32),
            dense, dense,
            jax.ShapeDtypeStruct((HOSTS, HOSTS, width), F32),
        ),
        in_specs=[
            smem(),
            pl.BlockSpec((sources, BLOCK, model), lambda i: (i, 0, 0)),
            pl.BlockSpec(weights.shape, lambda i: (0, 0, 0)),
        ],
        out_specs=(
            spec(model), spec(width), spec(2 * ff), spec(1),
            dense_spec, dense_spec,
            pl.BlockSpec((HOSTS, sources, width), lambda i: (0, i, 0)),
        ),
        scratch_shapes=[
            pltpu.VMEM((2, compact, model), BF),
            pltpu.VMEM((sources, blocks.shape[2]), F32),
            pltpu.VMEM((sources, blocks.shape[2]), F32),
            pltpu.VMEM((compact, width), F32),
            pltpu.VMEM((compact, 1), F32),
        ],
        compiler_params=params(56),
        cost_estimate=cost(4 * halves * compact * model * 3 * ff, 20_000_000),
        name="forward",
    )(host, blocks, weights)


def backward_kernel(gu_ref, add_ref, w_ref, rw_ref, out_ref, re_ref):
    ff = w_ref.shape[2] // 3
    compact = gu_ref.shape[2]
    for e in (0, 1):
        row = lax.dot_general(
            gu_ref[0, e], w_ref[e, :, 0 : 2 * ff], (((1,), (1,)), ((), ())),
            preferred_element_type=F32,
        )
        re_ref[e] = (row + add_ref[0, e] * rw_ref[e : e + 1, :]).astype(BF)
    for p in range(compact // 48):
        r0 = re_ref[0, 48 * p : 48 * p + 48, :].astype(F32)
        r1 = re_ref[1, 48 * p : 48 * p + 48, :].astype(F32)
        out_ref[80 * p : 80 * p + 80, :] = jnp.concatenate(
            [
                r0[0:16], r1[0:16], r0[32:40] + r1[32:40],
                r0[16:32], r1[16:32], r0[40:48] + r1[40:48],
            ],
            axis=0,
        ).astype(BF)


def backward(gu, add, weights, rw_rows):
    halves, _, compact, double = gu.shape
    model = weights.shape[1]
    spec = lambda last: pl.BlockSpec((1, 2, compact, last), lambda i: (i, 0, 0, 0))
    return pl.pallas_call(
        backward_kernel,
        grid=(halves,),
        out_shape=jax.ShapeDtypeStruct((ROWS, model), BF),
        in_specs=[
            spec(double), spec(1),
            pl.BlockSpec(weights.shape, lambda i: (0, 0, 0)),
            pl.BlockSpec(rw_rows.shape, lambda i: (0, 0)),
        ],
        out_specs=pl.BlockSpec((ROWS // halves, model), lambda i: (i, 0)),
        scratch_shapes=[pltpu.VMEM((2, compact, model), BF)],
        compiler_params=params(56),
        cost_estimate=cost(4 * halves * compact * model * double, 10_000_000),
        name="backward",
    )(gu, add, weights, rw_rows)


def router_kernel(shares_ref, gg_ref, gate_ref, mask_ref, hot_ref, xe_ref, part_ref, sum_ref):
    total = shares_ref[0]
    for h in range(1, HOSTS):
        total = total + shares_ref[h]
    sum_ref[...] = total
    halves, _, compact, model = xe_ref.shape
    sources = HOSTS // halves
    for e in (0, 1):
        logit = (gate_ref[e] * (gg_ref[e] - total)).astype(BF)
        part = jnp.zeros((8, model), F32)
        for i in range(halves):
            near = lax.dot_general(
                logit[sources * i : sources * i + sources], hot_ref[i, e],
                (((1,), (1,)), ((), ())), preferred_element_type=F32,
            )
            line = jnp.sum(near * mask_ref[...], axis=0, keepdims=True)
            line = jnp.concatenate([line, jnp.zeros((7, compact), F32)], axis=0).astype(BF)
            part = part + jnp.dot(line, xe_ref[i, e], preferred_element_type=F32)
        part_ref[e : e + 1, :] = part[0:1]


def router_part(shares, gg, gate, hot, xe):
    slot = np.arange(xe.shape[2])
    inner = slot % 48
    second = ((inner >= 16) & (inner < 32)) | (inner >= 40)
    source = 2 * (slot // 48) + second
    mask = np.arange(HOSTS // 2)[:, None] == source[None, :]
    return pl.pallas_call(
        router_kernel,
        out_shape=(
            jax.ShapeDtypeStruct((2, xe.shape[3]), F32),
            jax.ShapeDtypeStruct((HOSTS, gg.shape[2]), F32),
        ),
        in_specs=[vmem()] * 6,
        out_specs=(vmem(), vmem()),
        compiler_params=params(16),
        cost_estimate=cost(64 * xe.size, 4_000_000),
        name="router_part",
    )(shares, gg, gate, jnp.asarray(mask.astype(np.float32)), hot, xe)


def combine_kernel(host_ref, ids_ref, gates_ref, sum_ref, expand_ref, rank_ref, rw_ref, rows_ref, out_ref):
    tokens, top = ids_ref.shape
    experts = rw_ref.shape[0]
    column = lax.broadcasted_iota(jnp.int32, (tokens, experts), 1)
    member = jnp.zeros((tokens, experts), F32)
    dense = jnp.zeros((tokens, experts), F32)
    for k in range(top):
        match = ids_ref[:, k : k + 1] == column
        member += jnp.where(match, 1.0, 0.0)
        dense += jnp.where(match, gates_ref[:, k : k + 1], 0.0)
    before = jnp.dot(strict(tokens, tokens, False), member.astype(BF), preferred_element_type=F32)
    order = jnp.where(member > 0.0, before + 1.0, 0.0).astype(BF)
    wide = jnp.dot(order, expand_ref[...], preferred_element_type=F32)
    hot = jnp.where(wide == rank_ref[...], 1.0, 0.0).astype(BF)
    own = jnp.broadcast_to(sum_ref[pl.ds(host_ref[0], 1), :], (tokens, tokens))
    diagonal = lax.broadcasted_iota(jnp.int32, (tokens, tokens), 0) == lax.broadcasted_iota(
        jnp.int32, (tokens, tokens), 1
    )
    own = jnp.sum(jnp.where(diagonal, own, 0.0), axis=1, keepdims=True)
    lost = jnp.dot((dense * own).astype(BF), rw_ref[...], preferred_element_type=F32)
    out_ref[...] = (jnp.dot(hot, rows_ref[...], preferred_element_type=F32) - lost).astype(BF)


def combine(host, ids, gates, sums, rw_t, rows):
    slot = np.arange(ROWS)
    expert = 2 * (slot // SLOTS) + WHICH[slot % SLOTS]
    expand = (np.arange(2 * HOSTS)[:, None] == expert[None, :]).astype(np.float32)
    rank = (RANK[slot % SLOTS] + 1.0).astype(np.float32)[None, :]
    return pl.pallas_call(
        combine_kernel,
        out_shape=jax.ShapeDtypeStruct((ids.shape[0], rows.shape[1]), BF),
        in_specs=[smem()] + [vmem()] * 7,
        out_specs=vmem(),
        compiler_params=params(20),
        name="combine",
    )(host, ids, gates, sums, jnp.asarray(expand, BF), jnp.asarray(rank), rw_t, rows)


def exchange(rows):
    return lax.all_to_all(rows, "expert", split_axis=0, concat_axis=0, tiled=True)


def body(tokens, upstream, expert_ids, gates, expert_weights, router_weight):
    model = tokens.shape[1]
    per_host, _, part, ff = expert_weights.shape
    host = lax.axis_index("expert").astype(jnp.int32)
    group = lax.axis_index("dp").astype(jnp.int32)
    host_arr = host.reshape(1)
    ids_t = expert_ids.T
    shard = expert_weights.transpose(0, 2, 1, 3).reshape(per_host, part, 3 * ff)
    weights = lax.all_gather(shard, "dp", axis=1, tiled=True)
    blocks = exchange(dispatch(ids_t, gates.T, tokens, upstream))
    rw_t = router_weight.T
    rw_rows = lax.dynamic_slice_in_dim(rw_t, per_host * host, per_host, 0).astype(F32)
    xe, hot, gu, add, gg, gate, share = forward(host_arr, blocks, weights)
    shares = exchange(share)
    back = exchange(backward(gu, add, weights, rw_rows))
    piece, sums = router_part(shares, gg, gate, hot, xe)
    everyone = lax.all_gather(piece.reshape(-1, 128), "dp", axis=0, tiled=False)
    column = jnp.sum(everyone, axis=0).reshape(per_host, model)
    column = lax.dynamic_slice_in_dim(column, part * group, part, 1)
    column, back = lax.optimization_barrier((column, back))
    columns = exchange(jnp.broadcast_to(column.reshape(1, -1), (HOSTS, per_host * part)))
    router_grad = columns.reshape(-1, part).T
    token_grad = combine(host_arr, expert_ids, gates, sums, rw_t, back)
    return (token_grad, router_grad)


def solution(mesh):
    in_specs = (
        P(("dp", "expert"), None),
        P(("dp", "expert"), None),
        P(("dp", "expert"), None),
        P(("dp", "expert"), None),
        P("expert", None, "dp", None),
        P(),
    )
    out_specs = (P(("dp", "expert"), None), P("dp", None))
    return jax.shard_map(body, mesh=mesh, in_specs=in_specs, out_specs=out_specs, check_vma=False)
```

time: 261 us -> 199 us (0.76)
  blocking collectives: 157 us -> 29.2 us
  waiting for transfers between devices: 30 us -> 75.5 us
  starting transfers between devices: 21.2 us -> 38.1 us
  local copies, waits for them, and re-layouts: 8.43 us -> 13.3 us
    all_gather x4 -> x1, blocking collectives: 157 us -> 29.2 us  [body(): everyone = lax.all_gather(piece.reshape(-1, 128), 'dp', axis=0, tiled=False)]
    all_to_all x3 -> x4, waiting for transfers between devices: 30 us -> 75.5 us  [exchange(): lax.all_to_all(rows, 'expert', split_axis=0, concat_axis=0, tiled=True)]
    all_to_all x3 -> x4, starting transfers between devices: 21.2 us -> 38.1 us  [exchange(): lax.all_to_all(rows, 'expert', split_axis=0, concat_axis=0, tiled=True)]
    unnamed x13 -> x21, local copies, waits for them, and re-layouts: 4.57 us -> 9.52 us
  transfers between devices with their start and end apart: 4 -> 5, of which waited for: 1 -> 3; matrix products, arithmetic and copies ran while one was open for 2% -> 2% of each run, Pallas kernels for 4% -> 8%
where the time goes in v2:
time: 199 us; the launch traced here: 198 us
  waiting for transfers between devices  75.5 us (38%)
  starting transfers between devices  38.1 us (19%)
  blocking collectives  29.2 us (15%)
  Pallas kernels  25.7 us (13%)
  between operations  14.1 us (7%)
  local copies, waits for them, and re-layouts  13.3 us (7%)
  other arithmetic  2.02 us (1%)
    all_to_all x4, waiting for transfers between devices, exchange(): lax.all_to_all(rows, 'expert', split_axis=0, concat_axis=0, tiled=True)  75.5 us
    all_to_all x4, starting transfers between devices, exchange(): lax.all_to_all(rows, 'expert', split_axis=0, concat_axis=0, tiled=True)  38.1 us
    all_gather x1, blocking collectives, body(): everyone = lax.all_gather(piece.reshape(-1, 128), 'dp', axis=0, tiled=False)  29.2 us
    pallas_call x1, Pallas kernels, forward(): pl.pallas_call(forward_kernel, grid=(halves,), out_shape=(shape(model, BF...  10.3 us
    unnamed x21, local copies, waits for them, and re-layouts  9.52 us
    pallas_call x1, Pallas kernels, backward(): pl.pallas_call(backward_kernel, grid=(halves,), out_shape=jax.ShapeDtypeS...  6.78 us
    pallas_call x1, Pallas kernels, dispatch(): pl.pallas_call(dispatch_kernel, out_shape=jax.ShapeDtypeStruct((HOSTS, BL...  5.79 us
  transfers between devices with their start and end apart: 5, of which 3 were waited for; matrix products, arithmetic and copies ran while one was open for 2% of the time, Pallas kernels for 8%

profile of v2, /device:TPU:1, one launch (start us, length us, event | category | flops | bytes accessed | tf_op | source)
XLA Modules:
  0.0 198.0 jit_solution(10383166671850082718)
XLA Ops:
  7.2 0.0 all-gather.2.cloned.1.call-start
  7.2 1.7 copy.22
  8.9 0.0 all-gather.2.cloned.1.call-update
  9.0 5.8 %dispatch.1 = bf16[32,88,1024]{2,1,0:T(8,128)(2,1)} custom-call(s32[8,128]{1,0:T(8,128)} %bitcast.18, f32[8,128]{1,0:T(8,128)} %bitcast.19, bf16[128,1024]{1,0:T(8,128)(2,1)} %x_ref.1, bf16[128,1024]{1,0:T(8,128)(2,1)} %dy_ref.1), custom_call_target="tpu_custom_call" | custom-call | tf_op jit(solution)/shard_map/dispatch/pallas_call | solution.py:109
  14.8 11.4 %all-to-all-start = ((bf16[32,88,1024]{2,1,0:T(8,128)(2,1)}), bf16[32,88,1024]{2,1,0:T(8,128)(2,1)}, u32[]{:S(2)}, u32[]{:S(2)}) async-start(bf16[32,88,1024]{2,1,0:T(8,128)(2,1)} %dispatch.1), calls=%async_computation | async-start | bytes 11534336 | tf_op jit(solution)/shard_map/all_to_all | solution.py:371
  26.1 71.1 %all-to-all-done.rows_ref = bf16[32,88,1024]{2,1,0:T(8,128)(2,1)} async-done(((bf16[32,88,1024]{2,1,0:T(8,128)(2,1)}), bf16[32,88,1024]{2,1,0:T(8,128)(2,1)}, u32[]{:S(2)}, u32[]{:S(2)}) %all-to-all-start) | async-done | bytes 5767200 | tf_op jit(solution)/shard_map/all_to_all | solution.py:371
  97.2 0.0 all-gather.2.cloned.1.call-done.w_ref
  97.2 10.3 %forward.1 = (bf16[2,2,384,1024]{3,2,1,0:T(8,128)(2,1)}, bf16[2,2,384,128]{3,2,1,0:T(8,128)(2,1)}, bf16[2,2,384,768]{3,2,1,0:T(8,128)(2,1)}, f32[2,2,384,1]{3,2,...) custom-call(s32[1]{0:T(128)} %bitcast.host_ref, ...), custom_call_target="tpu_custom_call" | custom-call | flops 3623878656 | bytes 20000000 | tf_op jit(solution)/shard_map/forward/pallas_call | solution.py:218
  107.6 10.2 %all-to-all-start.1 = ((f32[32,32,128]{2,1,0:T(8,128)}), f32[32,32,128]{2,1,0:T(8,128)S(1)}, u32[]{:S(2)}, u32[]{:S(2)}) async-start(f32[32,32,128]{2,1,0:T(8,128)} %get-tuple-element.13), calls=%async_computation.1 | async-start | bytes 1048576 | tf_op jit(solution)/shard_map/all_to_all | solution.py:371
  117.7 1.3 convert_bitcast_fusion.rw_ref
  119.1 6.8 %backward.1 = bf16[1280,1024]{1,0:T(8,128)(2,1)} custom-call(bf16[2,2,384,768]{3,2,1,0:T(8,128)(2,1)} %get-tuple-element.20.gu_ref, f32[2,2,384,1]{3,2,1,0:T(8,128)} %get-tuple-element.21.add_ref, bf16[2,1024,1152]{2,1,0:T(8,128)(2,1)} %all-gather.2.cloned.1.call-done.w_ref, f32[2,1024]{1,0:T(2,128)} %convert_bitcast_fusion.rw_ref), custom_call_target="tpu_custom_call" | custom-call | flops 2415919104 | bytes 10000000 | tf_op jit(solution)/shard_map/backward/pallas_call | solution.py:274
  125.8 0.0 copy-start.1
  125.8 3.5 %all-to-all-done.1.shares_ref = f32[32,32,128]{2,1,0:T(8,128)S(1)} async-done(((f32[32,32,128]{2,1,0:T(8,128)}), f32[32,32,128]{2,1,0:T(8,128)S(1)}, u32[]{:S(2)}, u32[]{:S(2)}) %all-to-all-start.1) | async-done | bytes 524320 | tf_op jit(solution)/shard_map/all_to_all | solution.py:371
  129.4 4.0 %all-to-all-start.2 = ((bf16[32,40,1024]{2,1,0:T(8,128)(2,1)}), bf16[32,40,1024]{2,1,0:T(8,128)(2,1)S(1)}, u32[]{:S(2)}, u32[]{:S(2)}) async-start(bf16[32,40,1024]{2,1,0:T(8,128)(2,1)} %bitcast.14), calls=%async_computation.2 | async-start | bytes 5242880 | tf_op jit(solution)/shard_map/all_to_all | solution.py:371
  133.4 0.0 copy-done.1
  133.4 0.0 copy-start
  133.4 1.9 copy-done
  135.3 0.0 copy-start.4
  135.3 0.8 copy-done.4
  136.0 0.0 copy-start.5
  136.0 0.8 copy-done.5
  136.8 0.0 copy-start.6
  136.8 0.7 copy-done.6
  137.5 0.8 router_part.1
  138.4 0.0 copy-start.7
  138.4 0.6 copy-done.7
  139.0 0.7 all_gather_reshape.3
  139.7 29.2 %all_gather.7 = f32[16,16,128]{2,1,0:T(8,128)S(1)} all-gather(f32[1,16,128]{2,1,0:T(8,128)S(1)} %all_gather_reshape.3), channel_id=1, replica_groups=mesh['dp'=16,'expert'=32] {'dp'}, dimensions={0}, use_global_device_ids=true | all-gather | bytes 139264 | tf_op jit(solution)/shard_map/all_gather | solution.py:390
  168.9 0.1 constant_dynamic-slice_fusion
  169.0 0.0 all-to-all-done.2
  169.0 0.1 broadcast_in_dim.7
  169.1 0.6 broadcast_in_dim.8
  169.7 12.6 %all-to-all-start.3 = ((f32[32,1,128]{2,1,0:T(1,128)}), f32[32,1,128]{2,1,0:T(1,128)S(1)}, u32[]{:S(2)}, u32[]{:S(2)}) async-start(f32[32,1,128]{2,1,0:T(1,128)} %broadcast_in_dim.8), calls=%async_computation.3 | async-start | bytes 32768 | tf_op jit(solution)/shard_map/all_to_all | solution.py:371
  182.3 0.8 copy.19.ids_ref
  183.1 0.8 copy.20.gates_ref
  183.8 0.0 copy-start.2
  183.8 0.9 copy-done.2
  184.8 0.0 copy-start.3
  184.8 0.9 copy-done.3
  185.7 0.0 copy-start.8
  185.7 0.7 copy-done.8
  186.4 2.0 combine.1
  188.3 0.8 all-to-all-done.3
  189.1 0.5 broadcast.6
  189.6 0.7 reduce.3
  190.3 0.1 reshape.31
  190.4 0.7 copy.21
  (2 shorter events, 0.0 us)
Async XLA Ops:
  7.2 90.1 %all-gather.2.cloned.1.call-start = ((), (), s32[]{:S(2)}) async-start(), calls=%async_computation.4 | async-start | bytes 5013504 | tf_op jit(solution)/shard_map/all_gather | solution.py:382
  14.8 82.5 %all-to-all-start = ((bf16[32,88,1024]{2,1,0:T(8,128)(2,1)}), bf16[32,88,1024]{2,1,0:T(8,128)(2,1)}, u32[]{:S(2)}, u32[]{:S(2)}) async-start(bf16[32,88,1024]{2,1,0:T(8,128)(2,1)} %dispatch.1), calls=%async_computation | async-start | bytes 11534336 | tf_op jit(solution)/shard_map/all_to_all | solution.py:371
  107.6 21.8 %all-to-all-start.1 = ((f32[32,32,128]{2,1,0:T(8,128)}), f32[32,32,128]{2,1,0:T(8,128)S(1)}, u32[]{:S(2)}, u32[]{:S(2)}) async-start(f32[32,32,128]{2,1,0:T(8,128)} %get-tuple-element.13), calls=%async_computation.1 | async-start | bytes 1048576 | tf_op jit(solution)/shard_map/all_to_all | solution.py:371
  125.8 7.5 %copy-start.1 = (bf16[2,2,384,128]{3,2,1,0:T(8,128)(2,1)S(1)}, bf16[2,2,384,128]{3,2,1,0:T(8,128)(2,1)}, u32[]{:S(2)}) copy-start(bf16[2,2,384,128]{3,2,1,0:T(8,128)(2,1)} %get-tuple-element.16.hot_ref) | copy-start | bytes 1179652
  129.4 39.6 %all-to-all-start.2 = ((bf16[32,40,1024]{2,1,0:T(8,128)(2,1)}), bf16[32,40,1024]{2,1,0:T(8,128)(2,1)S(1)}, u32[]{:S(2)}, u32[]{:S(2)}) async-start(bf16[32,40,1024]{2,1,0:T(8,128)(2,1)} %bitcast.14), calls=%async_computation.2 | async-start | bytes 5242880 | tf_op jit(solution)/shard_map/all_to_all | solution.py:371
  133.4 1.9 copy-start
  135.3 0.8 copy-start.4
  136.0 0.8 copy-start.5
  136.8 0.7 copy-start.6
  138.4 0.6 copy-start.7
  169.7 19.4 %all-to-all-start.3 = ((f32[32,1,128]{2,1,0:T(1,128)}), f32[32,1,128]{2,1,0:T(1,128)S(1)}, u32[]{:S(2)}, u32[]{:S(2)}) async-start(f32[32,1,128]{2,1,0:T(1,128)} %broadcast_in_dim.8), calls=%async_computation.3 | async-start | bytes 32768 | tf_op jit(solution)/shard_map/all_to_all | solution.py:371
  183.8 0.9 copy-start.2
  184.8 0.9 copy-start.3
  185.7 0.7 copy-start.8
Sparse Core Ops, SparseCore 0:
  10.1 77.5 all-gather.1

commit v3 on v2

v3 whole, which is shorter than its diff:
```python
import functools

import jax
import jax.numpy as jnp
import numpy as np
from jax import lax
from jax.experimental import pallas as pl
from jax.experimental.pallas import tpu as pltpu
from jax.sharding import PartitionSpec as P

F32 = jnp.float32
BF = jnp.bfloat16
CAP = 20
SLOTS = 2 * CAP
HOSTS = 32
ROWS = HOSTS * SLOTS
BLOCK = 2 * SLOTS
TOKENS = 128


def slot_table():
    which = [0] * 16 + [1] * 16 + [0] * 4 + [1] * 4
    rank = list(range(16)) + list(range(16)) + list(range(16, 20)) + list(range(16, 20))
    return np.array(which), np.array(rank)


WHICH, RANK = slot_table()


def strict(rows, cols, upper):
    a = lax.broadcasted_iota(jnp.int32, (rows, cols), 0)
    b = lax.broadcasted_iota(jnp.int32, (rows, cols), 1)
    return jnp.where((a < b) if upper else (a > b), 1.0, 0.0).astype(BF)


def host_block(first, second):
    width = first.shape[-1]
    row = lax.broadcasted_iota(jnp.int32, (16, width), 0).astype(F32) + 1.0
    row8 = lax.broadcasted_iota(jnp.int32, (8, width), 0)
    mixed = jnp.where(
        row8 < 4, jnp.broadcast_to(first, (8, width)), jnp.broadcast_to(second, (8, width))
    )
    late = (row8 + jnp.where(row8 < 4, 17, 13)).astype(F32)
    return jnp.concatenate(
        [
            jnp.where(jnp.broadcast_to(first, (16, width)) == row, 1.0, 0.0),
            jnp.where(jnp.broadcast_to(second, (16, width)) == row, 1.0, 0.0),
            jnp.where(mixed == late, 1.0, 0.0),
        ],
        axis=0,
    )


def dispatch_kernel(ids_ref, x_ref, dy_ref, out_ref, hot_ref):
    experts, tokens = 2 * HOSTS, x_ref.shape[0]
    hosts = out_ref.shape[0]

    @pl.when(pl.program_id(0) == 0)
    def _():
        column = lax.broadcasted_iota(jnp.int32, (experts, tokens), 0)
        member = jnp.zeros((experts, tokens), F32)
        for k in range(ids_ref.shape[0]):
            member += jnp.where(ids_ref[k : k + 1, :] == column, 1.0, 0.0)
        before = jnp.dot(
            member.astype(BF), strict(tokens, tokens, True), preferred_element_type=F32
        )
        order = jnp.where(member > 0.0, before + 1.0, 0.0)
        for pair in range(HOSTS // 2):
            blocks = [
                host_block(order[2 * h : 2 * h + 1], order[2 * h + 1 : 2 * h + 2])
                for h in (2 * pair, 2 * pair + 1)
            ]
            hot_ref[80 * pair : 80 * pair + 80, :] = jnp.concatenate(blocks, axis=0).astype(BF)

    rows = SLOTS * hosts
    hot = hot_ref[pl.ds(pl.multiple_of(pl.program_id(0) * rows, rows), rows), :]
    xs = jnp.dot(hot, x_ref[...], preferred_element_type=F32)
    ys = jnp.dot(hot, dy_ref[...], preferred_element_type=F32)
    for j in range(hosts):
        at = slice(SLOTS * j, SLOTS * j + SLOTS)
        out_ref[j] = jnp.concatenate([xs[at], ys[at]], axis=0).astype(BF)


def vmem():
    return pl.BlockSpec(memory_space=pltpu.VMEM)


def smem():
    return pl.BlockSpec(memory_space=pltpu.SMEM)


def params(mib):
    return pltpu.CompilerParams(vmem_limit_bytes=mib * 1024 * 1024)


def cost(flops, moved):
    return pl.CostEstimate(flops=flops, bytes_accessed=moved, transcendentals=0)


def dispatch(ids_t, tokens, upstream):
    steps = 4
    whole = lambda v: pl.BlockSpec(v.shape, lambda i: (0, 0))
    return pl.pallas_call(
        dispatch_kernel,
        grid=(steps,),
        out_shape=jax.ShapeDtypeStruct((HOSTS, BLOCK, tokens.shape[1]), BF),
        in_specs=[whole(ids_t), whole(tokens), whole(upstream)],
        out_specs=pl.BlockSpec((HOSTS // steps, BLOCK, tokens.shape[1]), lambda i: (i, 0, 0)),
        scratch_shapes=[pltpu.VMEM((ROWS, tokens.shape[0]), BF)],
        compiler_params=params(56),
        name="dispatch",
    )(ids_t, tokens, upstream)


def pieces(a, b, start, e):
    at = start + 16 * e
    return jnp.concatenate(
        [a[at : at + 16], b[at : at + 16], a[start + 32 : start + 40], b[start + 32 : start + 40]],
        axis=0,
    ).astype(BF)


def load_weights(w_ref, held_ref, sems, count):
    ff = w_ref.shape[3]
    return [
        [
            pltpu.make_async_copy(
                w_ref.at[e, j], held_ref.at[e, :, pl.ds(ff * j, ff)], sems.at[e, j]
            )
            for j in range(count)
        ]
        for e in (0, 1)
    ]


def forward_kernel(
    host_ref, route_ref, rows_ref, w_hbm,
    xe_ref, hot_ref, gu_ref, add_ref, gg_ref, share_ref,
    dye_ref, wide_ref, gcol_ref, w_ref, sems,
):
    sources = rows_ref.shape[0]
    pairs = sources // 2
    width = hot_ref.shape[3]
    ff = w_ref.shape[2] // 3
    first = pl.program_id(0) == 0
    copies = load_weights(w_hbm, w_ref, sems, 3)

    @pl.when(first)
    def _():
        for group in copies:
            for copy in group:
                copy.start()

    for p in range(pairs):
        a, b = rows_ref[2 * p].astype(F32), rows_ref[2 * p + 1].astype(F32)
        for e in (0, 1):
            xe_ref[0, e, 48 * p : 48 * p + 48, :] = pieces(a, b, 0, e)
            dye_ref[e, 48 * p : 48 * p + 48, :] = pieces(a, b, SLOTS, e)
    ids = route_ref[:, 0:8, :]
    gates = route_ref[:, 8:16, :]
    upper = strict(width, width, True)
    host = host_ref[0]
    row8 = lax.broadcasted_iota(jnp.int32, (8, width), 0)
    row16 = lax.broadcasted_iota(jnp.int32, (16, width), 0).astype(F32) + 1.0
    total = jnp.zeros((sources, width), F32)
    spread = lambda v, n: jnp.broadcast_to(v, (n, width))
    for e in (0, 1):
        wanted = (2 * host + e).astype(F32)
        match = ids == wanted
        member = jnp.sum(jnp.where(match, 1.0, 0.0), axis=1)
        gate = jnp.sum(jnp.where(match, gates, 0.0), axis=1)
        before = jnp.dot(member.astype(BF), upper, preferred_element_type=F32)
        order = jnp.where(member > 0.0, before + 1.0, 0.0)
        gg_ref[2 + e] = gate
        if e == 0:
            late = jnp.where(row8 < 4, row8 + 17, -1).astype(F32)
        else:
            late = jnp.where(row8 < 4, -1, row8 + 13).astype(F32)
        for p in range(pairs):
            a, b = order[2 * p : 2 * p + 1], order[2 * p + 1 : 2 * p + 2]
            ga, gb = gate[2 * p : 2 * p + 1], gate[2 * p + 1 : 2 * p + 2]
            hot = jnp.concatenate(
                [
                    jnp.where(spread(a, 16) == row16, 1.0, 0.0),
                    jnp.where(spread(b, 16) == row16, 1.0, 0.0),
                    jnp.where(spread(a, 8) == late, 1.0, 0.0),
                    jnp.where(spread(b, 8) == late, 1.0, 0.0),
                ],
                axis=0,
            )
            weight = jnp.concatenate(
                [spread(ga, 16), spread(gb, 16), spread(ga, 8), spread(gb, 8)], axis=0
            )
            wide_ref[48 * p : 48 * p + 48, :] = hot
            hot_ref[0, e, 48 * p : 48 * p + 48, :] = hot.astype(BF)
            gcol_ref[48 * p : 48 * p + 48, :] = jnp.sum(hot * weight, axis=1, keepdims=True)

        @pl.when(first)
        def _(e=e):
            for copy in copies[e]:
                copy.wait()

        pre = jnp.dot(xe_ref[0, e], w_ref[e, :, 0 : 2 * ff], preferred_element_type=F32)
        hidden_grad = jnp.dot(dye_ref[e], w_ref[e, :, 2 * ff :], preferred_element_type=F32)
        pre_gate, pre_up = pre[:, 0:ff], pre[:, ff:]
        sigma = jax.nn.sigmoid(pre_gate)
        active = pre_gate * sigma
        hidden = (active * pre_up).astype(BF).astype(F32)
        gg = jnp.sum(hidden_grad * hidden, axis=1, keepdims=True).astype(BF).astype(F32)
        gcol = gcol_ref[...]
        scaled = hidden_grad * gcol
        gu_ref[0, e, :, 0:ff] = (
            scaled * pre_up * sigma * (1.0 + pre_gate * (1.0 - sigma))
        ).astype(BF)
        gu_ref[0, e, :, ff:] = (scaled * active).astype(BF)
        add_ref[0, e] = gcol * gg
        for p in range(pairs):
            hit = wide_ref[48 * p : 48 * p + 48, :] * gg[48 * p : 48 * p + 48]
            down = lambda v: jnp.sum(v, axis=0, keepdims=True)
            gg_ref[e, 2 * p : 2 * p + 1, :] = down(hit[0:16]) + down(hit[32:40])
            gg_ref[e, 2 * p + 1 : 2 * p + 2, :] = down(hit[16:32]) + down(hit[40:48])
        total = total + gate * gg_ref[e]
    for h in range(HOSTS):
        share_ref[h] = total


def forward(host, route, blocks, weights):
    halves, sources, width = 2, HOSTS // 2, TOKENS
    model, ff = weights.shape[2:]
    compact = sources * 24
    shape = lambda last, kind: jax.ShapeDtypeStruct((halves, 2, compact, last), kind)
    spec = lambda last: pl.BlockSpec((1, 2, compact, last), lambda i: (i, 0, 0, 0))
    return pl.pallas_call(
        forward_kernel,
        grid=(halves,),
        out_shape=(
            shape(model, BF), shape(width, BF), shape(2 * ff, BF), shape(1, F32),
            jax.ShapeDtypeStruct((4, HOSTS, width), F32),
            jax.ShapeDtypeStruct((HOSTS, HOSTS, width), F32),
        ),
        in_specs=[
            smem(),
            pl.BlockSpec((sources, 16, width), lambda i: (i, 0, 0)),
            pl.BlockSpec((sources, BLOCK, model), lambda i: (i, 0, 0)),
            pl.BlockSpec(memory_space=pl.ANY),
        ],
        out_specs=(
            spec(model), spec(width), spec(2 * ff), spec(1),
            pl.BlockSpec((4, sources, width), lambda i: (0, i, 0)),
            pl.BlockSpec((HOSTS, sources, width), lambda i: (0, i, 0)),
        ),
        scratch_shapes=[
            pltpu.VMEM((2, compact, model), BF),
            pltpu.VMEM((compact, width), F32),
            pltpu.VMEM((compact, 1), F32),
            pltpu.VMEM((2, model, 3 * ff), BF),
            pltpu.SemaphoreType.DMA((2, 3)),
        ],
        compiler_params=params(56),
        cost_estimate=cost(4 * halves * compact * model * 3 * ff, 20_000_000),
        name="forward",
    )(host, route, blocks, weights)


def backward_kernel(host_ref, gu_ref, add_ref, rw_ref, w_hbm, out_ref, re_ref, w_ref, sems):
    compact = gu_ref.shape[2]
    first = pl.program_id(0) == 0
    copies = load_weights(w_hbm, w_ref, sems, 2)

    @pl.when(first)
    def _():
        for group in copies:
            for copy in group:
                copy.start()

    experts = rw_ref.shape[0]
    mine = lax.broadcasted_iota(jnp.int32, (8, experts), 0) + 2 * host_ref[0]
    pick = jnp.where(lax.broadcasted_iota(jnp.int32, (8, experts), 1) == mine, 1.0, 0.0)
    router = jnp.dot(pick.astype(BF), rw_ref[...], preferred_element_type=F32)
    for e in (0, 1):

        @pl.when(first)
        def _(e=e):
            for copy in copies[e]:
                copy.wait()

        row = lax.dot_general(
            gu_ref[0, e], w_ref[e], (((1,), (1,)), ((), ())), preferred_element_type=F32
        )
        re_ref[e] = (row + add_ref[0, e] * router[e : e + 1]).astype(BF)
    for p in range(compact // 48):
        r0 = re_ref[0, 48 * p : 48 * p + 48, :].astype(F32)
        r1 = re_ref[1, 48 * p : 48 * p + 48, :].astype(F32)
        out_ref[80 * p : 80 * p + 80, :] = jnp.concatenate(
            [
                r0[0:16], r1[0:16], r0[32:40] + r1[32:40],
                r0[16:32], r1[16:32], r0[40:48] + r1[40:48],
            ],
            axis=0,
        ).astype(BF)


def backward(host, gu, add, rw_t, weights):
    halves, _, compact, double = gu.shape
    model = weights.shape[2]
    spec = lambda last: pl.BlockSpec((1, 2, compact, last), lambda i: (i, 0, 0, 0))
    return pl.pallas_call(
        backward_kernel,
        grid=(halves,),
        out_shape=jax.ShapeDtypeStruct((ROWS, model), BF),
        in_specs=[
            smem(), spec(double), spec(1),
            pl.BlockSpec(rw_t.shape, lambda i: (0, 0)),
            pl.BlockSpec(memory_space=pl.ANY),
        ],
        out_specs=pl.BlockSpec((ROWS // halves, model), lambda i: (i, 0)),
        scratch_shapes=[
            pltpu.VMEM((2, compact, model), BF),
            pltpu.VMEM((2, model, double), BF),
            pltpu.SemaphoreType.DMA((2, 2)),
        ],
        compiler_params=params(56),
        cost_estimate=cost(4 * halves * compact * model * double, 10_000_000),
        name="backward",
    )(host, gu, add, rw_t, weights)


def router_kernel(shares_ref, gg_ref, hot_hbm, xe_hbm, part_ref, sum_ref, hot_ref, xe_ref, sems):
    copies = [
        pltpu.make_async_copy(hot_hbm, hot_ref, sems.at[0]),
        pltpu.make_async_copy(xe_hbm, xe_ref, sems.at[1]),
    ]
    for copy in copies:
        copy.start()
    total = shares_ref[0]
    for h in range(1, HOSTS):
        total = total + shares_ref[h]
    sum_ref[...] = total
    halves, _, compact, model = xe_ref.shape
    sources = HOSTS // halves
    source = lax.broadcasted_iota(jnp.int32, (sources, compact), 0)
    slot = lax.broadcasted_iota(jnp.int32, (sources, compact), 1) - 48 * (source >> 1)
    even = ((slot >= 0) & (slot < 16)) | ((slot >= 32) & (slot < 40))
    odd = ((slot >= 16) & (slot < 32)) | ((slot >= 40) & (slot < 48))
    own = ((source & 1) == 0) & even | ((source & 1) == 1) & odd
    for copy in copies:
        copy.wait()
    for e in (0, 1):
        logit = (gg_ref[2 + e] * (gg_ref[e] - total)).astype(BF)
        part = jnp.zeros((8, model), F32)
        for i in range(halves):
            near = lax.dot_general(
                logit[sources * i : sources * i + sources], hot_ref[i, e],
                (((1,), (1,)), ((), ())), preferred_element_type=F32,
            )
            line = jnp.sum(jnp.where(own, near, 0.0), axis=0, keepdims=True)
            line = jnp.concatenate([line, jnp.zeros((7, compact), F32)], axis=0).astype(BF)
            part = part + jnp.dot(line, xe_ref[i, e], preferred_element_type=F32)
        part_ref[e : e + 1, :] = part[0:1]


def router_part(shares, gg, hot, xe):
    return pl.pallas_call(
        router_kernel,
        out_shape=(
            jax.ShapeDtypeStruct((2, xe.shape[3]), F32),
            jax.ShapeDtypeStruct((HOSTS, gg.shape[2]), F32),
        ),
        in_specs=[vmem(), vmem()] + [pl.BlockSpec(memory_space=pl.ANY)] * 2,
        out_specs=(vmem(), vmem()),
        scratch_shapes=[
            pltpu.VMEM(hot.shape, BF), pltpu.VMEM(xe.shape, BF), pltpu.SemaphoreType.DMA((2,)),
        ],
        compiler_params=params(16),
        cost_estimate=cost(64 * xe.size, 4_000_000),
        name="router_part",
    )(shares, gg, hot, xe)


def lookup_kernel(ids_ref, gates_ref, expand_ref, rank_ref, hot_ref, dense_ref):
    tokens, top = ids_ref.shape
    experts = expand_ref.shape[0]
    column = lax.broadcasted_iota(jnp.int32, (tokens, experts), 1)
    member = jnp.zeros((tokens, experts), F32)
    dense = jnp.zeros((tokens, experts), F32)
    for k in range(top):
        match = ids_ref[:, k : k + 1] == column
        member += jnp.where(match, 1.0, 0.0)
        dense += jnp.where(match, gates_ref[:, k : k + 1], 0.0)
    before = jnp.dot(strict(tokens, tokens, False), member.astype(BF), preferred_element_type=F32)
    order = jnp.where(member > 0.0, before + 1.0, 0.0).astype(BF)
    wide = jnp.dot(order, expand_ref[...], preferred_element_type=F32)
    hot_ref[...] = jnp.where(wide == rank_ref[...], 1.0, 0.0).astype(BF)
    dense_ref[...] = dense


def lookup(ids, gates):
    slot = np.arange(ROWS)
    expert = 2 * (slot // SLOTS) + WHICH[slot % SLOTS]
    expand = (np.arange(2 * HOSTS)[:, None] == expert[None, :]).astype(np.float32)
    rank = (RANK[slot % SLOTS] + 1.0).astype(np.float32)[None, :]
    return pl.pallas_call(
        lookup_kernel,
        out_shape=(
            jax.ShapeDtypeStruct((ids.shape[0], ROWS), BF),
            jax.ShapeDtypeStruct((ids.shape[0], 2 * HOSTS), F32),
        ),
        in_specs=[vmem()] * 4,
        out_specs=(vmem(), vmem()),
        compiler_params=params(56),
        name="lookup",
    )(ids, gates, jnp.asarray(expand, BF), jnp.asarray(rank))


def combine_kernel(host_ref, hot_ref, dense_ref, sum_ref, rw_ref, rows_ref, out_ref):
    tokens = hot_ref.shape[0]
    own = jnp.broadcast_to(sum_ref[pl.ds(host_ref[0], 1), :], (tokens, tokens))
    diagonal = lax.broadcasted_iota(jnp.int32, (tokens, tokens), 0) == lax.broadcasted_iota(
        jnp.int32, (tokens, tokens), 1
    )
    own = jnp.sum(jnp.where(diagonal, own, 0.0), axis=1, keepdims=True)
    lost = jnp.dot((dense_ref[...] * own).astype(BF), rw_ref[...], preferred_element_type=F32)
    out = jnp.dot(hot_ref[...], rows_ref[...], preferred_element_type=F32)
    out_ref[...] = (out - lost).astype(BF)


def combine(host, hot, dense, sums, rw_t, rows):
    return pl.pallas_call(
        combine_kernel,
        out_shape=jax.ShapeDtypeStruct((hot.shape[0], rows.shape[1]), BF),
        in_specs=[smem()] + [vmem()] * 5,
        out_specs=vmem(),
        compiler_params=params(20),
        name="combine",
    )(host, hot, dense, sums, rw_t, rows)


def exchange(rows):
    return lax.all_to_all(rows, "expert", split_axis=0, concat_axis=0, tiled=True)


def body(tokens, upstream, expert_ids, gates, expert_weights, router_weight):
    model = tokens.shape[1]
    per_host, _, part, ff = expert_weights.shape
    host = lax.axis_index("expert").astype(jnp.int32)
    group = lax.axis_index("dp").astype(jnp.int32)
    host_arr = host.reshape(1)
    ids_t = expert_ids.T
    weights = lax.all_gather(expert_weights, "dp", axis=2, tiled=True)
    blocks = exchange(dispatch(ids_t, tokens, upstream))
    route = jnp.concatenate([ids_t.astype(F32), gates.T], axis=0)
    route = lax.all_gather(route, "expert", axis=0, tiled=False)
    places, dense = lookup(expert_ids, gates)
    route, places, dense = lax.optimization_barrier((route, places, dense))
    rw_t = router_weight.T
    xe, hot, gu, add, gg, share = forward(host_arr, route, blocks, weights)
    shares = exchange(share)
    rows = backward(host_arr, gu, add, rw_t, weights)
    piece, sums = router_part(shares, gg, hot, xe)
    piece, rows = lax.optimization_barrier((piece, rows))
    back = exchange(rows)
    everyone = lax.all_gather(piece.reshape(-1, 128), "dp", axis=0, tiled=False)
    column = jnp.sum(everyone, axis=0).reshape(per_host, model)
    column = lax.dynamic_slice_in_dim(column, part * group, part, 1)
    column, back = lax.optimization_barrier((column, back))
    columns = exchange(jnp.broadcast_to(column.reshape(1, -1), (HOSTS, per_host * part)))
    router_grad = columns.reshape(-1, part).T
    token_grad = combine(host_arr, places, dense, sums, rw_t, back)
    return (token_grad, router_grad)


def solution(mesh):
    in_specs = (
        P(("dp", "expert"), None),
        P(("dp", "expert"), None),
        P(("dp", "expert"), None),
        P(("dp", "expert"), None),
        P("expert", None, "dp", None),
        P(),
    )
    out_specs = (P(("dp", "expert"), None), P("dp", None))
    return jax.shard_map(body, mesh=mesh, in_specs=in_specs, out_specs=out_specs, check_vma=False)
```

time: 199 us -> 207 us (1.040)
  blocking collectives: 29.2 us -> 111 us
  waiting for transfers between devices: 75.5 us -> 14.2 us
  local copies, waits for them, and re-layouts: 13.3 us -> 5 us
  starting transfers between devices: 38.1 us -> 30.4 us
  Pallas kernels: 25.7 us -> 30.7 us
    all_gather x0 -> x1, blocking collectives: none -> 82.2 us  [body(): route = lax.all_gather(route, 'expert', axis=0, tiled=False)]
    all_to_all x4, waiting for transfers between devices: 75.5 us -> 13.5 us  [exchange(): lax.all_to_all(rows, 'expert', split_axis=0, concat_axis=0, tiled=True)]
    all_to_all x4, starting transfers between devices: 38.1 us -> 30.4 us  [exchange(): lax.all_to_all(rows, 'expert', split_axis=0, concat_axis=0, tiled=True)]
    unnamed x21 -> x23, local copies, waits for them, and re-layouts: 9.52 us -> 3.61 us
    pallas_call x2 -> x3, Pallas kernels: 7.74 us -> 8.64 us  [the longest x1 4.94 us: dispatch(): pl.pallas_call(dispatch_kernel, grid=(steps,), out_shape=jax.ShapeDtypeSt...]
  transfers between devices with their start and end apart: 5 -> 5, of which waited for: 3 -> 3; matrix products, arithmetic and copies ran while one was open for 2% -> 1% of each run, Pallas kernels for 8% -> 8%
where the time goes in v3:
time: 207 us
  blocking collectives  111 us (54%)
  Pallas kernels  30.7 us (15%)
  starting transfers between devices  30.4 us (15%)
  waiting for transfers between devices  14.2 us (7%)
  between operations  14.2 us (7%)
  local copies, waits for them, and re-layouts  5 us (2%)
    all_gather x1, blocking collectives, body(): route = lax.all_gather(route, 'expert', axis=0, tiled=False)  82.2 us
    all_to_all x4, starting transfers between devices, exchange(): lax.all_to_all(rows, 'expert', split_axis=0, concat_axis=0, tiled=True)  30.4 us
    all_gather x1, blocking collectives, body(): everyone = lax.all_gather(piece.reshape(-1, 128), 'dp', axis=0, tiled=False)  29.3 us
    all_to_all x4, waiting for transfers between devices, exchange(): lax.all_to_all(rows, 'expert', split_axis=0, concat_axis=0, tiled=True)  13.5 us
    pallas_call x1, Pallas kernels, forward(): pl.pallas_call(forward_kernel, grid=(halves,), out_shape=(shape(model, BF...  11.7 us
    pallas_call x1, Pallas kernels, backward(): pl.pallas_call(backward_kernel, grid=(halves,), out_shape=jax.ShapeDtypeS...  8.03 us
    pallas_call x1, Pallas kernels, dispatch(): pl.pallas_call(dispatch_kernel, grid=(steps,), out_shape=jax.ShapeDtypeSt...  4.94 us
  transfers between devices with their start and end apart: 5, of which 3 were waited for; matrix products, arithmetic and copies ran while one was open for 1% of the time, Pallas kernels for 8%

profile of v3, /device:TPU:1, one launch (start us, length us, event | category | flops | bytes accessed | tf_op | source)
XLA Modules:
  0.0 206.7 jit_solution(6522924428960153360)
XLA Ops:
  7.2 0.0 all-gather.3.cloned.1.call-start
  7.2 0.7 all-gather.3.cloned.1.call-update
  7.9 4.9 %dispatch.1 = bf16[32,80,1024]{2,1,0:T(8,128)(2,1)} custom-call(s32[8,128]{1,0:T(8,128)} %bitcast.15, bf16[128,1024]{1,0:T(8,128)(2,1)} %x_ref.1, bf16[128,1024]{1,0:T(8,128)(2,1)} %dy_ref.1), custom_call_target="tpu_custom_call" | custom-call | tf_op jit(solution)/shard_map/dispatch/pallas_call | solution.py:103
  12.8 0.0 copy-start.8
  12.8 0.0 copy-start.9
  12.8 11.5 %all-to-all-start = ((bf16[32,80,1024]{2,1,0:T(8,128)(2,1)}), bf16[32,80,1024]{2,1,0:T(8,128)(2,1)}, u32[]{:S(2)}, u32[]{:S(2)}) async-start(bf16[32,80,1024]{2,1,0:T(8,128)(2,1)} %dispatch.1), calls=%async_computation | async-start | bytes 10485760 | tf_op jit(solution)/shard_map/all_to_all | solution.py:439
  24.3 0.0 copy-done.8
  24.3 0.7 copy.15.ids_ref
  25.1 0.0 copy-done.9
  25.1 0.7 copy.16.gates_ref
  25.8 2.4 %lookup.1 = (bf16[128,1280]{1,0:T(8,128)(2,1)}, f32[128,64]{1,0:T(8,128)}) custom-call(s32[128,8]{1,0:T(8,128)} %copy.15.ids_ref, f32[128,8]{1,0:T(8,128)} %copy.16.gates_ref, bf16[64,1280]{1,0:T(8,128)(2,1)} %constant.21.clone.expand_ref, f32[1,1280]{1,0:T(1,128)} %constant.22.clone.rank_ref), custom_call_target="tpu_custom_call" | custom-call | tf_op jit(solution)/shard_map/lookup/pallas_call | solution.py:402
  28.2 82.2 %all-gather = f32[512,128]{1,0:T(8,128)} all-gather(f32[16,128]{1,0:T(8,128)S(1)} %pad_maximum_fusion), channel_id=2, replica_groups=mesh['dp'=16,'expert'=32] {'expert'}, dimensions={0}, use_global_device_ids=true | all-gather | bytes 270336 | tf_op jit(solution)/shard_map/all_gather | solution.py:452
  110.3 0.0 all-to-all-done.rows_ref
  110.3 0.0 all-gather.3.cloned.1.call-done.w_hbm
  110.3 11.7 %forward.1 = (bf16[2,2,384,1024]{3,2,1,0:T(8,128)(2,1)}, bf16[2,2,384,128]{3,2,1,0:T(8,128)(2,1)}, bf16[2,2,384,768]{3,2,1,0:T(8,128)(2,1)}, f32[2,2,384,1]{3,2,...) custom-call(s32[1]{0:T(128)} %bitcast.host_ref, f32[32,16,128]{2,1,0:T(8,128)} %bitcast.13, ...), custom_call_target="tpu_custom_call" | custom-call | flops 3623878656 | bytes 20000000 | tf_op jit(solution)/shard_map/forward/pallas_call | solution.py:233
  122.1 7.1 %all-to-all-start.1 = ((f32[32,32,128]{2,1,0:T(8,128)}), f32[32,32,128]{2,1,0:T(8,128)}, u32[]{:S(2)}, u32[]{:S(2)}) async-start(f32[32,32,128]{2,1,0:T(8,128)} %get-tuple-element.24), calls=%async_computation.1 | async-start | bytes 1048576 | tf_op jit(solution)/shard_map/all_to_all | solution.py:439
  129.2 0.0 copy-start
  129.2 0.0 copy-start.2
  129.2 8.0 %backward.1 = bf16[1280,1024]{1,0:T(8,128)(2,1)} custom-call(s32[1]{0:T(128)} %bitcast.host_ref, bf16[2,2,384,768]{3,2,1,0:T(8,128)(2,1)} %get-tuple-element.30.gu_ref, f32[2,2,384,1]{3,2,1,0:T(8,128)} %get-tuple-element.31.add_ref, bf16[64,1024]{1,0:T(8,128)(2,1)} %bitcast.10, bf16[2,3,1024,384]{3,2,1,0:T(8,128)(2,1)} %all-gather.3.cloned.1.call-done.w_hbm), custom_call_target="tpu_custom_call" | custom-call | flops 2415919104 | bytes 10000000 | tf_op jit(solution)/shard_map/backward/pallas_call | solution.py:307
  137.2 3.6 %all-to-all-done.1.shares_ref = f32[32,32,128]{2,1,0:T(8,128)} async-done(((f32[32,32,128]{2,1,0:T(8,128)}), f32[32,32,128]{2,1,0:T(8,128)}, u32[]{:S(2)}, u32[]{:S(2)}) %all-to-all-start.1) | async-done | bytes 524320 | tf_op jit(solution)/shard_map/all_to_all | solution.py:439
  140.8 0.0 copy-done
  140.8 0.0 copy-done.2
  140.8 0.0 copy-start.4
  140.8 0.8 copy-done.4
  141.7 2.4 %router_part.1 = (f32[2,1024]{1,0:T(2,128)S(1)}, f32[32,128]{1,0:T(8,128)S(1)}) custom-call(f32[32,32,128]{2,1,0:T(8,128)} %all-to-all-done.1.shares_ref, f32[4,32,128]{2,1,0:T(8,128)S(1)} %copy-done.4, bf16[2,2,384,128]{3,2,1,0:T(8,128)(2,1)S(1)} %copy-done.2, bf16[2,2,384,1024]{3,2,1,0:T(8,128)(2,1)S(1)} %copy-done), custom_call_target="tpu_custom_call" | custom-call | flops 100663296 | bytes 4000000 | tf_op jit(solution)/shard_map/router_part/pallas_call | solution.py:363
  144.0 0.0 copy-start.6
  144.1 0.6 copy-done.6
  144.6 0.0 copy-start.1
  144.6 0.0 copy-start.3
  144.6 0.0 copy-start.5
  144.6 0.0 copy-start.7
  144.7 4.0 %all-to-all-start.2 = ((bf16[32,40,1024]{2,1,0:T(8,128)(2,1)}), bf16[32,40,1024]{2,1,0:T(8,128)(2,1)S(1)}, u32[]{:S(2)}, u32[]{:S(2)}) async-start(bf16[32,40,1024]{2,1,0:T(8,128)(2,1)} %bitcast.12), calls=%async_computation.2 | async-start | bytes 5242880 | tf_op jit(solution)/shard_map/all_to_all | solution.py:439
  148.7 0.0 copy-done.7
  148.7 29.3 %all_gather.15 = f32[16,16,128]{2,1,0:T(8,128)S(1)} all-gather(f32[1,16,128]{2,1,0:T(8,128)S(1)} %all_gather_reshape.3), channel_id=1, replica_groups=mesh['dp'=16,'expert'=32] {'dp'}, dimensions={0}, use_global_device_ids=true | all-gather | bytes 139264 | tf_op jit(solution)/shard_map/all_gather | solution.py:462
  178.0 0.1 constant_dynamic-slice_fusion
  178.1 4.4 %all-to-all-done.2 = bf16[32,40,1024]{2,1,0:T(8,128)(2,1)S(1)} async-done(((bf16[32,40,1024]{2,1,0:T(8,128)(2,1)}), bf16[32,40,1024]{2,1,0:T(8,128)(2,1)S(1)}, u32[]{:S(2)}, u32[]{:S(2)}) %all-to-all-start.2) | async-done | bytes 2621472 | tf_op jit(solution)/shard_map/all_to_all | solution.py:439
  182.5 0.1 broadcast_in_dim.7
  182.6 0.6 broadcast_in_dim.8
  183.2 7.8 %all-to-all-start.3 = ((f32[32,1,128]{2,1,0:T(1,128)}), f32[32,1,128]{2,1,0:T(1,128)S(1)}, u32[]{:S(2)}, u32[]{:S(2)}) async-start(f32[32,1,128]{2,1,0:T(1,128)} %broadcast_in_dim.8), calls=%async_computation.3 | async-start | bytes 32768 | tf_op jit(solution)/shard_map/all_to_all | solution.py:439
  191.0 0.0 copy-done.1
  191.0 0.0 copy-done.3
  191.0 0.0 copy-done.5
  191.0 1.3 combine.1
  192.4 5.5 %all-to-all-done.3 = f32[32,1,128]{2,1,0:T(1,128)S(1)} async-done(((f32[32,1,128]{2,1,0:T(1,128)}), f32[32,1,128]{2,1,0:T(1,128)S(1)}, u32[]{:S(2)}, u32[]{:S(2)}) %all-to-all-start.3) | async-done | bytes 16416 | tf_op jit(solution)/shard_map/all_to_all | solution.py:439
  197.9 0.5 broadcast.6
  198.4 0.7 reduce.3
  199.1 0.1 reshape.27
  199.1 0.7 copy.17
  (5 shorter events, 0.0 us)
Async XLA Ops:
  7.2 103.2 %all-gather.3.cloned.1.call-start = ((), (), s32[]{:S(2)}) async-start(), calls=%async_computation.4 | async-start | bytes 5013504 | tf_op jit(solution)/shard_map/all_gather | solution.py:449
  12.8 11.5 %copy-start.8 = (s32[128,8]{0,1:T(8,128)S(1)}, s32[128,8]{0,1:T(8,128)}, u32[]{:S(2)}) copy-start(s32[128,8]{0,1:T(8,128)} %param.10) | copy-start | bytes 12292
  12.8 12.2 %copy-start.9 = (f32[128,8]{0,1:T(8,128)S(1)}, f32[128,8]{0,1:T(8,128)}, u32[]{:S(2)}) copy-start(f32[128,8]{0,1:T(8,128)} %param.11) | copy-start | bytes 12292
  12.8 97.5 %all-to-all-start = ((bf16[32,80,1024]{2,1,0:T(8,128)(2,1)}), bf16[32,80,1024]{2,1,0:T(8,128)(2,1)}, u32[]{:S(2)}, u32[]{:S(2)}) async-start(bf16[32,80,1024]{2,1,0:T(8,128)(2,1)} %dispatch.1), calls=%async_computation | async-start | bytes 10485760 | tf_op jit(solution)/shard_map/all_to_all | solution.py:439
  122.1 18.8 %all-to-all-start.1 = ((f32[32,32,128]{2,1,0:T(8,128)}), f32[32,32,128]{2,1,0:T(8,128)}, u32[]{:S(2)}, u32[]{:S(2)}) async-start(f32[32,32,128]{2,1,0:T(8,128)} %get-tuple-element.24), calls=%async_computation.1 | async-start | bytes 1048576 | tf_op jit(solution)/shard_map/all_to_all | solution.py:439
  129.2 11.7 %copy-start = (bf16[2,2,384,1024]{3,2,1,0:T(8,128)(2,1)S(1)}, bf16[2,2,384,1024]{3,2,1,0:T(8,128)(2,1)}, u32[]{:S(2)}) copy-start(bf16[2,2,384,1024]{3,2,1,0:T(8,128)(2,1)} %get-tuple-element.27.xe_hbm) | copy-start | bytes 9437188
  129.2 11.7 %copy-start.2 = (bf16[2,2,384,128]{3,2,1,0:T(8,128)(2,1)S(1)}, bf16[2,2,384,128]{3,2,1,0:T(8,128)(2,1)}, u32[]{:S(2)}) copy-start(bf16[2,2,384,128]{3,2,1,0:T(8,128)(2,1)} %get-tuple-element.26.hot_hbm) | copy-start | bytes 1179652
  140.8 0.8 copy-start.4
  144.0 0.6 copy-start.6
  144.6 46.4 %copy-start.1 = (bf16[1024,64]{0,1:T(8,128)(2,1)S(1)}, bf16[1024,64]{0,1:T(8,128)(2,1)}, u32[]{:S(2)}) copy-start(bf16[1024,64]{0,1:T(8,128)(2,1)} %param.13) | copy-start | bytes 393220
  144.6 46.4 %copy-start.3 = (bf16[128,1280]{1,0:T(8,128)(2,1)S(1)}, bf16[128,1280]{1,0:T(8,128)(2,1)}, u32[]{:S(2)}) copy-start(bf16[128,1280]{1,0:T(8,128)(2,1)} %get-tuple-element.21.hot_ref) | copy-start | bytes 983044
  144.6 46.4 %copy-start.5 = (f32[128,64]{1,0:T(8,128)S(1)}, f32[128,64]{1,0:T(8,128)}, u32[]{:S(2)}) copy-start(f32[128,64]{1,0:T(8,128)} %get-tuple-element.22.dense_ref) | copy-start | bytes 98308
  144.6 4.0 %copy-start.7 = (f32[2,1024]{1,0:T(2,128)S(1)}, f32[2,1024]{1,0:T(2,128)}, u32[]{:S(2)}) copy-start(f32[2,1024]{1,0:T(2,128)} %copy-done.6) | copy-start | bytes 24580
  144.7 37.8 %all-to-all-start.2 = ((bf16[32,40,1024]{2,1,0:T(8,128)(2,1)}), bf16[32,40,1024]{2,1,0:T(8,128)(2,1)S(1)}, u32[]{:S(2)}, u32[]{:S(2)}) async-start(bf16[32,40,1024]{2,1,0:T(8,128)(2,1)} %bitcast.12), calls=%async_computation.2 | async-start | bytes 5242880 | tf_op jit(solution)/shard_map/all_to_all | solution.py:439
  183.2 14.7 %all-to-all-start.3 = ((f32[32,1,128]{2,1,0:T(1,128)}), f32[32,1,128]{2,1,0:T(1,128)S(1)}, u32[]{:S(2)}, u32[]{:S(2)}) async-start(f32[32,1,128]{2,1,0:T(1,128)} %broadcast_in_dim.8), calls=%async_computation.3 | async-start | bytes 32768 | tf_op jit(solution)/shard_map/all_to_all | solution.py:439
Sparse Core Ops, SparseCore 0:
  10.1 77.5 all-gather.2

commit v4 on v3

--- a/solution.py
+++ b/solution.py
@@ -112,6 +112,24 @@
     )(ids_t, tokens, upstream)
 
 
+def route_kernel(ids_ref, gates_ref, out_ref):
+    route = jnp.concatenate([ids_ref[...].astype(F32), gates_ref[...]], axis=0)
+    for h in range(out_ref.shape[0]):
+        out_ref[h] = route
+
+
+def routes(ids_t, gates_t):
+    top, tokens = ids_t.shape
+    return pl.pallas_call(
+        route_kernel,
+        out_shape=jax.ShapeDtypeStruct((HOSTS, 2 * top, tokens), F32),
+        in_specs=[vmem(), vmem()],
+        out_specs=vmem(),
+        compiler_params=params(56),
+        name="routes",
+    )(ids_t, gates_t)
+
+
 def pieces(a, b, start, e):
     at = start + 16 * e
     return jnp.concatenate(
@@ -120,58 +138,29 @@
     ).astype(BF)
 
 
-def load_weights(w_ref, held_ref, sems, count):
-    ff = w_ref.shape[3]
-    return [
-        [
-            pltpu.make_async_copy(
-                w_ref.at[e, j], held_ref.at[e, :, pl.ds(ff * j, ff)], sems.at[e, j]
-            )
-            for j in range(count)
-        ]
-        for e in (0, 1)
-    ]
-
-
-def forward_kernel(
-    host_ref, route_ref, rows_ref, w_hbm,
-    xe_ref, hot_ref, gu_ref, add_ref, gg_ref, share_ref,
-    dye_ref, wide_ref, gcol_ref, w_ref, sems,
-):
+def prep_kernel(host_ref, route_ref, rows_ref, xe_ref, dye_ref, hot_ref, gcol_ref, gate_ref):
     sources = rows_ref.shape[0]
     pairs = sources // 2
     width = hot_ref.shape[3]
-    ff = w_ref.shape[2] // 3
-    first = pl.program_id(0) == 0
-    copies = load_weights(w_hbm, w_ref, sems, 3)
-
-    @pl.when(first)
-    def _():
-        for group in copies:
-            for copy in group:
-                copy.start()
-
     for p in range(pairs):
         a, b = rows_ref[2 * p].astype(F32), rows_ref[2 * p + 1].astype(F32)
         for e in (0, 1):
             xe_ref[0, e, 48 * p : 48 * p + 48, :] = pieces(a, b, 0, e)
-            dye_ref[e, 48 * p : 48 * p + 48, :] = pieces(a, b, SLOTS, e)
+            dye_ref[0, e, 48 * p : 48 * p + 48, :] = pieces(a, b, SLOTS, e)
     ids = route_ref[:, 0:8, :]
     gates = route_ref[:, 8:16, :]
     upper = strict(width, width, True)
     host = host_ref[0]
     row8 = lax.broadcasted_iota(jnp.int32, (8, width), 0)
     row16 = lax.broadcasted_iota(jnp.int32, (16, width), 0).astype(F32) + 1.0
-    total = jnp.zeros((sources, width), F32)
     spread = lambda v, n: jnp.broadcast_to(v, (n, width))
     for e in (0, 1):
-        wanted = (2 * host + e).astype(F32)
-        match = ids == wanted
+        match = ids == (2 * host + e).astype(F32)
         member = jnp.sum(jnp.where(match, 1.0, 0.0), axis=1)
         gate = jnp.sum(jnp.where(match, gates, 0.0), axis=1)
         before = jnp.dot(member.astype(BF), upper, preferred_element_type=F32)
         order = jnp.where(member > 0.0, before + 1.0, 0.0)
-        gg_ref[2 + e] = gate
+        gate_ref[e] = gate
         if e == 0:
             late = jnp.where(row8 < 4, row8 + 17, -1).astype(F32)
         else:
@@ -191,23 +180,71 @@
             weight = jnp.concatenate(
                 [spread(ga, 16), spread(gb, 16), spread(ga, 8), spread(gb, 8)], axis=0
             )
-            wide_ref[48 * p : 48 * p + 48, :] = hot
             hot_ref[0, e, 48 * p : 48 * p + 48, :] = hot.astype(BF)
-            gcol_ref[48 * p : 48 * p + 48, :] = jnp.sum(hot * weight, axis=1, keepdims=True)
-
-        @pl.when(first)
-        def _(e=e):
-            for copy in copies[e]:
-                copy.wait()
-
+            gcol_ref[0, e, 48 * p : 48 * p + 48, :] = jnp.sum(hot * weight, axis=1, keepdims=True)
+
+
+HALVES = 2
+SOURCES = HOSTS // HALVES
+COMPACT = SOURCES * 24
+
+
+def compact_shape(last, kind):
+    return jax.ShapeDtypeStruct((HALVES, 2, COMPACT, last), kind)
+
+
+def compact_spec(last):
+    return pl.BlockSpec((1, 2, COMPACT, last), lambda i: (i, 0, 0, 0))
+
+
+def dense_shape():
+    return jax.ShapeDtypeStruct((2, HOSTS, TOKENS), F32)
+
+
+def dense_spec():
+    return pl.BlockSpec((2, SOURCES, TOKENS), lambda i: (0, i, 0))
+
+
+def prep(host, route, blocks):
+    model = blocks.shape[2]
+    return pl.pallas_call(
+        prep_kernel,
+        grid=(HALVES,),
+        out_shape=(
+            compact_shape(model, BF), compact_shape(model, BF), compact_shape(TOKENS, BF),
+            compact_shape(1, F32), dense_shape(),
+        ),
+        in_specs=[
+            smem(),
+            pl.BlockSpec((SOURCES, 16, TOKENS), lambda i: (i, 0, 0)),
+            pl.BlockSpec((SOURCES, BLOCK, model), lambda i: (i, 0, 0)),
+        ],
+        out_specs=(
+            compact_spec(model), compact_spec(model), compact_spec(TOKENS),
+            compact_spec(1), dense_spec(),
+        ),
+        compiler_params=params(56),
+        cost_estimate=cost(1_000_000, 14_000_000),
+        name="prep",
+    )(host, route, blocks)
+
+
+def forward_kernel(
+    xe_ref, dye_ref, hot_ref, gcol_ref, gate_ref, w_ref, gu_ref, add_ref, gg_ref, share_ref,
+):
+    pairs = COMPACT // 48
+    ff = w_ref.shape[2] // 3
+    total = jnp.zeros(share_ref.shape[1:], F32)
+    down = lambda v: jnp.sum(v, axis=0, keepdims=True)
+    for e in (0, 1):
         pre = jnp.dot(xe_ref[0, e], w_ref[e, :, 0 : 2 * ff], preferred_element_type=F32)
-        hidden_grad = jnp.dot(dye_ref[e], w_ref[e, :, 2 * ff :], preferred_element_type=F32)
+        hidden_grad = jnp.dot(dye_ref[0, e], w_ref[e, :, 2 * ff :], preferred_element_type=F32)
         pre_gate, pre_up = pre[:, 0:ff], pre[:, ff:]
         sigma = jax.nn.sigmoid(pre_gate)
         active = pre_gate * sigma
         hidden = (active * pre_up).astype(BF).astype(F32)
         gg = jnp.sum(hidden_grad * hidden, axis=1, keepdims=True).astype(BF).astype(F32)
-        gcol = gcol_ref[...]
+        gcol = gcol_ref[0, e]
         scaled = hidden_grad * gcol
         gu_ref[0, e, :, 0:ff] = (
             scaled * pre_up * sigma * (1.0 + pre_gate * (1.0 - sigma))
@@ -215,80 +252,50 @@
         gu_ref[0, e, :, ff:] = (scaled * active).astype(BF)
         add_ref[0, e] = gcol * gg
         for p in range(pairs):
-            hit = wide_ref[48 * p : 48 * p + 48, :] * gg[48 * p : 48 * p + 48]
-            down = lambda v: jnp.sum(v, axis=0, keepdims=True)
+            hit = hot_ref[0, e, 48 * p : 48 * p + 48, :].astype(F32) * gg[48 * p : 48 * p + 48]
             gg_ref[e, 2 * p : 2 * p + 1, :] = down(hit[0:16]) + down(hit[32:40])
             gg_ref[e, 2 * p + 1 : 2 * p + 2, :] = down(hit[16:32]) + down(hit[40:48])
-        total = total + gate * gg_ref[e]
+        total = total + gate_ref[e] * gg_ref[e]
+    total = total.astype(BF)
     for h in range(HOSTS):
         share_ref[h] = total
 
 
-def forward(host, route, blocks, weights):
-    halves, sources, width = 2, HOSTS // 2, TOKENS
-    model, ff = weights.shape[2:]
-    compact = sources * 24
-    shape = lambda last, kind: jax.ShapeDtypeStruct((halves, 2, compact, last), kind)
-    spec = lambda last: pl.BlockSpec((1, 2, compact, last), lambda i: (i, 0, 0, 0))
+def forward(xe, dye, hot, gcol, gate, weights):
+    _, model, triple = weights.shape
     return pl.pallas_call(
         forward_kernel,
-        grid=(halves,),
+        grid=(HALVES,),
         out_shape=(
-            shape(model, BF), shape(width, BF), shape(2 * ff, BF), shape(1, F32),
-            jax.ShapeDtypeStruct((4, HOSTS, width), F32),
-            jax.ShapeDtypeStruct((HOSTS, HOSTS, width), F32),
+            compact_shape(triple // 3 * 2, BF), compact_shape(1, F32), dense_shape(),
+            jax.ShapeDtypeStruct((HOSTS, HOSTS, TOKENS), BF),
         ),
         in_specs=[
-            smem(),
-            pl.BlockSpec((sources, 16, width), lambda i: (i, 0, 0)),
-            pl.BlockSpec((sources, BLOCK, model), lambda i: (i, 0, 0)),
-            pl.BlockSpec(memory_space=pl.ANY),
+            compact_spec(model), compact_spec(model), compact_spec(TOKENS),
+            compact_spec(1), dense_spec(),
+            pl.BlockSpec(weights.shape, lambda i: (0, 0, 0)),
         ],
         out_specs=(
-            spec(model), spec(width), spec(2 * ff), spec(1),
-            pl.BlockSpec((4, sources, width), lambda i: (0, i, 0)),
-            pl.BlockSpec((HOSTS, sources, width), lambda i: (0, i, 0)),
-        ),
-        scratch_shapes=[
-            pltpu.VMEM((2, compact, model), BF),
-            pltpu.VMEM((compact, width), F32),
-            pltpu.VMEM((compact, 1), F32),
-            pltpu.VMEM((2, model, 3 * ff), BF),
-            pltpu.SemaphoreType.DMA((2, 3)),
-        ],
-        compiler_params=params(56),
-        cost_estimate=cost(4 * halves * compact * model * 3 * ff, 20_000_000),
+            compact_spec(triple // 3 * 2), compact_spec(1), dense_spec(),
+            pl.BlockSpec((HOSTS, SOURCES, TOKENS), lambda i: (0, i, 0)),
+        ),
+        compiler_params=params(56),
+        cost_estimate=cost(4 * HALVES * COMPACT * model * triple, 20_000_000),
         name="forward",
-    )(host, route, blocks, weights)
-
-
-def backward_kernel(host_ref, gu_ref, add_ref, rw_ref, w_hbm, out_ref, re_ref, w_ref, sems):
-    compact = gu_ref.shape[2]
-    first = pl.program_id(0) == 0
-    copies = load_weights(w_hbm, w_ref, sems, 2)
-
-    @pl.when(first)
-    def _():
-        for group in copies:
-            for copy in group:
-                copy.start()
-
+    )(xe, dye, hot, gcol, gate, weights)
+
+
+def backward_kernel(host_ref, gu_ref, add_ref, rw_ref, w_ref, out_ref, re_ref):
     experts = rw_ref.shape[0]
     mine = lax.broadcasted_iota(jnp.int32, (8, experts), 0) + 2 * host_ref[0]
     pick = jnp.where(lax.broadcasted_iota(jnp.int32, (8, experts), 1) == mine, 1.0, 0.0)
     router = jnp.dot(pick.astype(BF), rw_ref[...], preferred_element_type=F32)
     for e in (0, 1):
-
-        @pl.when(first)
-        def _(e=e):
-            for copy in copies[e]:
-                copy.wait()
-
         row = lax.dot_general(
             gu_ref[0, e], w_ref[e], (((1,), (1,)), ((), ())), preferred_element_type=F32
         )
         re_ref[e] = (row + add_ref[0, e] * router[e : e + 1]).astype(BF)
-    for p in range(compact // 48):
+    for p in range(COMPACT // 48):
         r0 = re_ref[0, 48 * p : 48 * p + 48, :].astype(F32)
         r1 = re_ref[1, 48 * p : 48 * p + 48, :].astype(F32)
         out_ref[80 * p : 80 * p + 80, :] = jnp.concatenate(
@@ -301,40 +308,35 @@
 
 
 def backward(host, gu, add, rw_t, weights):
-    halves, _, compact, double = gu.shape
-    model = weights.shape[2]
-    spec = lambda last: pl.BlockSpec((1, 2, compact, last), lambda i: (i, 0, 0, 0))
+    double = gu.shape[3]
+    model = weights.shape[1]
     return pl.pallas_call(
         backward_kernel,
-        grid=(halves,),
+        grid=(HALVES,),
         out_shape=jax.ShapeDtypeStruct((ROWS, model), BF),
         in_specs=[
-            smem(), spec(double), spec(1),
+            smem(), compact_spec(double), compact_spec(1),
             pl.BlockSpec(rw_t.shape, lambda i: (0, 0)),
-            pl.BlockSpec(memory_space=pl.ANY),
+            pl.BlockSpec((2, model, double), lambda i: (0, 0, 0)),
         ],
-        out_specs=pl.BlockSpec((ROWS // halves, model), lambda i: (i, 0)),
-        scratch_shapes=[
-            pltpu.VMEM((2, compact, model), BF),
-            pltpu.VMEM((2, model, double), BF),
-            pltpu.SemaphoreType.DMA((2, 2)),
-        ],
-        compiler_params=params(56),
-        cost_estimate=cost(4 * halves * compact * model * double, 10_000_000),
+        out_specs=pl.BlockSpec((ROWS // HALVES, model), lambda i: (i, 0)),
+        scratch_shapes=[pltpu.VMEM((2, COMPACT, model), BF)],
+        compiler_params=params(56),
+        cost_estimate=cost(4 * HALVES * COMPACT * model * double, 10_000_000),
         name="backward",
     )(host, gu, add, rw_t, weights)
 
 
-def router_kernel(shares_ref, gg_ref, hot_hbm, xe_hbm, part_ref, sum_ref, hot_ref, xe_ref, sems):
+def router_kernel(shares_ref, gg_ref, gate_ref, hot_hbm, xe_hbm, part_ref, sum_ref, hot_ref, xe_ref, sems):
     copies = [
         pltpu.make_async_copy(hot_hbm, hot_ref, sems.at[0]),
         pltpu.make_async_copy(xe_hbm, xe_ref, sems.at[1]),
     ]
     for copy in copies:
         copy.start()
-    total = shares_ref[0]
+    total = shares_ref[0].astype(F32)
     for h in range(1, HOSTS):
-        total = total + shares_ref[h]
+        total = total + shares_ref[h].astype(F32)
     sum_ref[...] = total
     halves, _, compact, model = xe_ref.shape
     sources = HOSTS // halves
@@ -346,7 +348,7 @@
     for copy in copies:
         copy.wait()
     for e in (0, 1):
-        logit = (gg_ref[2 + e] * (gg_ref[e] - total)).astype(BF)
+        logit = (gate_ref[e] * (gg_ref[e] - total)).astype(BF)
         part = jnp.zeros((8, model), F32)
         for i in range(halves):
             near = lax.dot_general(
@@ -359,14 +361,14 @@
         part_ref[e : e + 1, :] = part[0:1]
 
 
-def router_part(shares, gg, hot, xe):
+def router_part(shares, gg, gate, hot, xe):
     return pl.pallas_call(
         router_kernel,
         out_shape=(
             jax.ShapeDtypeStruct((2, xe.shape[3]), F32),
             jax.ShapeDtypeStruct((HOSTS, gg.shape[2]), F32),
         ),
-        in_specs=[vmem(), vmem()] + [pl.BlockSpec(memory_space=pl.ANY)] * 2,
+        in_specs=[vmem()] * 3 + [pl.BlockSpec(memory_space=pl.ANY)] * 2,
         out_specs=(vmem(), vmem()),
         scratch_shapes=[
             pltpu.VMEM(hot.shape, BF), pltpu.VMEM(xe.shape, BF), pltpu.SemaphoreType.DMA((2,)),
@@ -374,7 +376,7 @@
         compiler_params=params(16),
         cost_estimate=cost(64 * xe.size, 4_000_000),
         name="router_part",
-    )(shares, gg, hot, xe)
+    )(shares, gg, gate, hot, xe)
 
 
 def lookup_kernel(ids_ref, gates_ref, expand_ref, rank_ref, hot_ref, dense_ref):
@@ -446,17 +448,20 @@
     group = lax.axis_index("dp").astype(jnp.int32)
     host_arr = host.reshape(1)
     ids_t = expert_ids.T
-    weights = lax.all_gather(expert_weights, "dp", axis=2, tiled=True)
-    blocks = exchange(dispatch(ids_t, tokens, upstream))
-    route = jnp.concatenate([ids_t.astype(F32), gates.T], axis=0)
-    route = lax.all_gather(route, "expert", axis=0, tiled=False)
+    shard = expert_weights.transpose(0, 2, 1, 3).reshape(per_host, part, 3 * ff)
+    weights = lax.all_gather(shard, "dp", axis=1, tiled=True)
+    route = exchange(routes(ids_t, gates.T))
+    sent = dispatch(ids_t, tokens, upstream)
+    route, sent = lax.optimization_barrier((route, sent))
+    blocks = exchange(sent)
     places, dense = lookup(expert_ids, gates)
-    route, places, dense = lax.optimization_barrier((route, places, dense))
+    blocks, places, dense = lax.optimization_barrier((blocks, places, dense))
     rw_t = router_weight.T
-    xe, hot, gu, add, gg, share = forward(host_arr, route, blocks, weights)
+    xe, dye, hot, gcol, gate = prep(host_arr, route, blocks)
+    gu, add, gg, share = forward(xe, dye, hot, gcol, gate, weights)
     shares = exchange(share)
     rows = backward(host_arr, gu, add, rw_t, weights)
-    piece, sums = router_part(shares, gg, hot, xe)
+    piece, sums = router_part(shares, gg, gate, hot, xe)
     piece, rows = lax.optimization_barrier((piece, rows))
     back = exchange(rows)
     everyone = lax.all_gather(piece.reshape(-1, 128), "dp", axis=0, tiled=False)

time: 207 us -> 199 us (0.961)
  blocking collectives: 111 us -> 29.3 us
  waiting for transfers between devices: 14.2 us -> 77.2 us
  starting transfers between devices: 30.4 us -> 37.1 us
  Pallas kernels: 30.7 us -> 33.1 us
    all_gather x1 -> x0, blocking collectives: 82.2 us -> none  [body(): route = lax.all_gather(route, 'expert', axis=0, tiled=False)]
    all_to_all x4 -> x5, waiting for transfers between devices: 13.5 us -> 77.2 us  [exchange(): lax.all_to_all(rows, 'expert', split_axis=0, concat_axis=0, tiled=True)]
    all_to_all x4 -> x5, starting transfers between devices: 30.4 us -> 37 us  [exchange(): lax.all_to_all(rows, 'expert', split_axis=0, concat_axis=0, tiled=True)]
    pallas_call x2 -> x4, Pallas kernels: 19.8 us -> 23.1 us  [the longest x1 9.81 us: forward(): pl.pallas_call(forward_kernel, grid=(HALVES,), out_shape=(compact_shape(t...]
  transfers between devices with their start and end apart: 5 -> 6, of which waited for: 3 -> 5; matrix products, arithmetic and copies ran while one was open for 1% -> 1% of each run, Pallas kernels for 8% -> 11%
where the time goes in v4:
time: 199 us
  waiting for transfers between devices  77.2 us (39%)
  starting transfers between devices  37.1 us (19%)
  Pallas kernels  33.1 us (17%)
  blocking collectives  29.3 us (15%)
  between operations  14.2 us (7%)
  local copies, waits for them, and re-layouts  6.99 us (4%)
    all_to_all x5, waiting for transfers between devices, exchange(): lax.all_to_all(rows, 'expert', split_axis=0, concat_axis=0, tiled=True)  77.2 us
    all_to_all x5, starting transfers between devices, exchange(): lax.all_to_all(rows, 'expert', split_axis=0, concat_axis=0, tiled=True)  37 us
    all_gather x1, blocking collectives, body(): everyone = lax.all_gather(piece.reshape(-1, 128), 'dp', axis=0, tiled=False)  29.3 us
    pallas_call x1, Pallas kernels, forward(): pl.pallas_call(forward_kernel, grid=(HALVES,), out_shape=(compact_shape(t...  9.81 us
    pallas_call x1, Pallas kernels, backward(): pl.pallas_call(backward_kernel, grid=(HALVES,), out_shape=jax.ShapeDtypeS...  6.66 us
    pallas_call x1, Pallas kernels, prep(): pl.pallas_call(prep_kernel, grid=(HALVES,), out_shape=(compact_shape(mode...  5.21 us
    pallas_call x1, Pallas kernels, dispatch(): pl.pallas_call(dispatch_kernel, grid=(steps,), out_shape=jax.ShapeDtypeSt...  4.98 us
  transfers between devices with their start and end apart: 6, of which 5 were waited for; matrix products, arithmetic and copies ran while one was open for 1% of the time, Pallas kernels for 11%

profile of v4, /device:TPU:1, one launch (start us, length us, event | category | flops | bytes accessed | tf_op | source)
XLA Modules:
  0.0 198.6 jit_solution(4147127088543919464)
XLA Ops:
  7.2 0.0 all-gather.2.cloned.1.call-start
  7.2 1.7 copy.21
  8.9 0.0 all-gather.2.cloned.1.call-update
  8.9 1.4 routes.1
  10.4 10.4 %all-to-all-start = ((f32[32,16,128]{2,1,0:T(8,128)}), f32[32,16,128]{2,1,0:T(8,128)S(1)}, u32[]{:S(2)}, u32[]{:S(2)}) async-start(f32[32,16,128]{2,1,0:T(8,128)} %routes.1), calls=%async_computation | async-start | bytes 524288 | tf_op jit(solution)/shard_map/all_to_all | solution.py:441
  20.8 5.0 %dispatch.1 = bf16[32,80,1024]{2,1,0:T(8,128)(2,1)} custom-call(s32[8,128]{1,0:T(8,128)} %bitcast.18, bf16[128,1024]{1,0:T(8,128)(2,1)} %x_ref.1, bf16[128,1024]{1,0:T(8,128)(2,1)} %dy_ref.1), custom_call_target="tpu_custom_call" | custom-call | tf_op jit(solution)/shard_map/dispatch/pallas_call | solution.py:103
  25.8 0.0 copy-start.8
  25.8 0.0 copy-start.9
  25.8 4.1 %all-to-all-done.route_ref = f32[32,16,128]{2,1,0:T(8,128)S(1)} async-done(((f32[32,16,128]{2,1,0:T(8,128)}), f32[32,16,128]{2,1,0:T(8,128)S(1)}, u32[]{:S(2)}, u32[]{:S(2)}) %all-to-all-start) | async-done | bytes 262176 | tf_op jit(solution)/shard_map/all_to_all | solution.py:441
  29.9 0.0 copy-start.7
  29.9 0.7 copy-done.7
  30.6 4.7 %all-to-all-start.1 = ((bf16[32,80,1024]{2,1,0:T(8,128)(2,1)}), bf16[32,80,1024]{2,1,0:T(8,128)(2,1)}, u32[]{:S(2)}, u32[]{:S(2)}) async-start(bf16[32,80,1024]{2,1,0:T(8,128)(2,1)} %dispatch.1), calls=%async_computation.1 | async-start | bytes 10485760 | tf_op jit(solution)/shard_map/all_to_all | solution.py:441
  35.3 0.0 copy-done.8
  35.3 0.7 copy.17.ids_ref
  36.0 0.0 copy-done.9
  36.0 0.7 copy.18.gates_ref
  36.8 2.4 %lookup.1 = (bf16[128,1280]{1,0:T(8,128)(2,1)}, f32[128,64]{1,0:T(8,128)}) custom-call(s32[128,8]{1,0:T(8,128)} %copy.17.ids_ref, f32[128,8]{1,0:T(8,128)} %copy.18.gates_ref, bf16[64,1280]{1,0:T(8,128)(2,1)} %constant.21.clone.expand_ref, f32[1,1280]{1,0:T(1,128)} %constant.22.clone.rank_ref), custom_call_target="tpu_custom_call" | custom-call | tf_op jit(solution)/shard_map/lookup/pallas_call | solution.py:404
  39.1 60.8 %all-to-all-done.1.rows_ref = bf16[32,80,1024]{2,1,0:T(8,128)(2,1)} async-done(((bf16[32,80,1024]{2,1,0:T(8,128)(2,1)}), bf16[32,80,1024]{2,1,0:T(8,128)(2,1)}, u32[]{:S(2)}, u32[]{:S(2)}) %all-to-all-start.1) | async-done | bytes 5242912 | tf_op jit(solution)/shard_map/all_to_all | solution.py:441
  99.9 5.2 %prep.1 = (bf16[2,2,384,1024]{3,2,1,0:T(8,128)(2,1)}, bf16[2,2,384,1024]{3,2,1,0:T(8,128)(2,1)}, bf16[2,2,384,128]{3,2,1,0:T(8,128)(2,1)}, f32[2,2,384,1]{3,2,1,0:T(8,128)}, f32[2,32,128]{2,1,0:T(8,128)}) custom-call(s32[1]{0:T(128)} %bitcast.host_ref, f32[32,16,128]{2,1,0:T(8,128)} %copy-done.7, bf16[32,80,1024]{2,1,0:T(8,128)(2,1)} %all-to-all-done.1.rows_ref), custom_call_target="tpu_custom_call" | custom-call | flops 1000000 | bytes 14000000 | tf_op jit(solution)/shard_map/prep/pallas_call | solution.py:210
  105.1 0.0 all-gather.2.cloned.1.call-done.w_ref
  105.1 9.8 %forward.1 = (bf16[2,2,384,768]{3,2,1,0:T(8,128)(2,1)}, f32[2,2,384,1]{3,2,1,0:T(8,128)}, f32[2,32,128]{2,1,0:T(8,128)}, bf16[32,32,128]{2,1,0:T(8,128)(2,1)}) custom-call(bf16[2,2,384,1024]{3,2,1,0:T(8,128)(2,1)} %get-tuple-element.31.xe_ref.xe_hbm, bf16[2,2,384,1024]{3,2,1,0:T(8,128)(2,1)} %get-tuple-element.32.dye_ref, ...), custom_call_target="tpu_custom_call" | custom-call | flops 3623878656 | bytes 20000000 | tf_op jit(solution)/shard_map/forward/pallas_call | solution.py:266
  115.0 8.9 %all-to-all-start.2 = ((bf16[32,32,128]{2,1,0:T(8,128)(2,1)}), bf16[32,32,128]{2,1,0:T(8,128)(2,1)S(1)}, u32[]{:S(2)}, u32[]{:S(2)}) async-start(bf16[32,32,128]{2,1,0:T(8,128)(2,1)} %get-tuple-element.36), calls=%async_computation.2 | async-start | bytes 524288 | tf_op jit(solution)/shard_map/all_to_all | solution.py:441
  123.9 0.0 copy-start
  123.9 0.0 copy-start.5
  123.9 0.0 copy-start.6
  123.9 6.7 %backward.1 = bf16[1280,1024]{1,0:T(8,128)(2,1)} custom-call(s32[1]{0:T(128)} %bitcast.host_ref, bf16[2,2,384,768]{3,2,1,0:T(8,128)(2,1)} %get-tuple-element.40.gu_ref, f32[2,2,384,1]{3,2,1,0:T(8,128)} %get-tuple-element.41.add_ref, bf16[64,1024]{1,0:T(8,128)(2,1)} %bitcast.11, bf16[2,1024,1152]{2,1,0:T(8,128)(2,1)} %all-gather.2.cloned.1.call-done.w_ref), custom_call_target="tpu_custom_call" | custom-call | flops 2415919104 | bytes 10000000 | tf_op jit(solution)/shard_map/backward/pallas_call | solution.py:313
  130.6 2.3 %all-to-all-done.2.shares_ref = bf16[32,32,128]{2,1,0:T(8,128)(2,1)S(1)} async-done(((bf16[32,32,128]{2,1,0:T(8,128)(2,1)}), bf16[32,32,128]{2,1,0:T(8,128)(2,1)S(1)}, u32[]{:S(2)}, u32[]{:S(2)}) %all-to-all-start.2) | async-done | bytes 262176 | tf_op jit(solution)/shard_map/all_to_all | solution.py:441
  132.9 0.0 copy-done
  132.9 0.0 copy-done.5
  132.9 0.0 copy-done.6
  132.9 0.0 copy-start.2
  132.9 1.0 copy-done.2
  133.9 1.3 router_part.1
  135.2 0.0 copy-start.1
  135.2 0.0 copy-start.3
  135.2 0.0 copy-start.4
  135.2 5.3 %all-to-all-start.3 = ((bf16[32,40,1024]{2,1,0:T(8,128)(2,1)}), bf16[32,40,1024]{2,1,0:T(8,128)(2,1)S(1)}, u32[]{:S(2)}, u32[]{:S(2)}) async-start(bf16[32,40,1024]{2,1,0:T(8,128)(2,1)} %bitcast.13), calls=%async_computation.3 | async-start | bytes 5242880 | tf_op jit(solution)/shard_map/all_to_all | solution.py:441
  140.5 29.3 %all_gather.7 = f32[16,16,128]{2,1,0:T(8,128)S(1)} all-gather(f32[1,16,128]{2,1,0:T(8,128)S(1)} %all_gather_reshape.3), channel_id=1, replica_groups=mesh['dp'=16,'expert'=32] {'dp'}, dimensions={0}, use_global_device_ids=true | all-gather | bytes 139264 | tf_op jit(solution)/shard_map/all_gather | solution.py:467
  169.8 0.1 constant_dynamic-slice_fusion
  169.9 4.5 %all-to-all-done.3 = bf16[32,40,1024]{2,1,0:T(8,128)(2,1)S(1)} async-done(((bf16[32,40,1024]{2,1,0:T(8,128)(2,1)}), bf16[32,40,1024]{2,1,0:T(8,128)(2,1)S(1)}, u32[]{:S(2)}, u32[]{:S(2)}) %all-to-all-start.3) | async-done | bytes 2621472 | tf_op jit(solution)/shard_map/all_to_all | solution.py:441
  174.4 0.1 broadcast_in_dim.7
  174.5 0.6 broadcast_in_dim.8
  175.1 7.8 %all-to-all-start.4 = ((f32[32,1,128]{2,1,0:T(1,128)}), f32[32,1,128]{2,1,0:T(1,128)S(1)}, u32[]{:S(2)}, u32[]{:S(2)}) async-start(f32[32,1,128]{2,1,0:T(1,128)} %broadcast_in_dim.8), calls=%async_computation.4 | async-start | bytes 32768 | tf_op jit(solution)/shard_map/all_to_all | solution.py:441
  182.9 0.0 copy-done.1
  182.9 0.0 copy-done.3
  182.9 0.0 copy-done.4
  182.9 1.4 combine.1
  184.3 5.5 %all-to-all-done.4 = f32[32,1,128]{2,1,0:T(1,128)S(1)} async-done(((f32[32,1,128]{2,1,0:T(1,128)}), f32[32,1,128]{2,1,0:T(1,128)S(1)}, u32[]{:S(2)}, u32[]{:S(2)}) %all-to-all-start.4) | async-done | bytes 16416 | tf_op jit(solution)/shard_map/all_to_all | solution.py:441
  189.8 0.5 broadcast.6
  190.3 0.7 reduce.3
  191.0 0.1 reshape.31
  191.0 0.7 copy.20
  (3 shorter events, 0.0 us)
Async XLA Ops:
  7.2 98.0 %all-gather.2.cloned.1.call-start = ((), (), s32[]{:S(2)}) async-start(), calls=%async_computation.5 | async-start | bytes 5013504 | tf_op jit(solution)/shard_map/all_gather | solution.py:452
  10.4 19.5 %all-to-all-start = ((f32[32,16,128]{2,1,0:T(8,128)}), f32[32,16,128]{2,1,0:T(8,128)S(1)}, u32[]{:S(2)}, u32[]{:S(2)}) async-start(f32[32,16,128]{2,1,0:T(8,128)} %routes.1), calls=%async_computation | async-start | bytes 524288 | tf_op jit(solution)/shard_map/all_to_all | solution.py:441
  25.8 9.5 %copy-start.8 = (s32[128,8]{0,1:T(8,128)S(1)}, s32[128,8]{0,1:T(8,128)}, u32[]{:S(2)}) copy-start(s32[128,8]{0,1:T(8,128)} %param.10) | copy-start | bytes 12292
  25.8 10.3 %copy-start.9 = (f32[128,8]{0,1:T(8,128)S(1)}, f32[128,8]{0,1:T(8,128)}, u32[]{:S(2)}) copy-start(f32[128,8]{0,1:T(8,128)} %param.11) | copy-start | bytes 12292
  29.9 0.7 copy-start.7
  30.6 69.3 %all-to-all-start.1 = ((bf16[32,80,1024]{2,1,0:T(8,128)(2,1)}), bf16[32,80,1024]{2,1,0:T(8,128)(2,1)}, u32[]{:S(2)}, u32[]{:S(2)}) async-start(bf16[32,80,1024]{2,1,0:T(8,128)(2,1)} %dispatch.1), calls=%async_computation.1 | async-start | bytes 10485760 | tf_op jit(solution)/shard_map/all_to_all | solution.py:441
  115.0 17.9 %all-to-all-start.2 = ((bf16[32,32,128]{2,1,0:T(8,128)(2,1)}), bf16[32,32,128]{2,1,0:T(8,128)(2,1)S(1)}, u32[]{:S(2)}, u32[]{:S(2)}) async-start(bf16[32,32,128]{2,1,0:T(8,128)(2,1)} %get-tuple-element.36), calls=%async_computation.2 | async-start | bytes 524288 | tf_op jit(solution)/shard_map/all_to_all | solution.py:441
  123.9 9.0 %copy-start = (bf16[2,2,384,1024]{3,2,1,0:T(8,128)(2,1)S(1)}, bf16[2,2,384,1024]{3,2,1,0:T(8,128)(2,1)}, u32[]{:S(2)}) copy-start(bf16[2,2,384,1024]{3,2,1,0:T(8,128)(2,1)} %get-tuple-element.31.xe_ref.xe_hbm) | copy-start | bytes 9437188
  123.9 9.0 %copy-start.5 = (f32[2,32,128]{2,1,0:T(8,128)S(1)}, f32[2,32,128]{2,1,0:T(8,128)}, u32[]{:S(2)}) copy-start(f32[2,32,128]{2,1,0:T(8,128)} %get-tuple-element.35.gate_ref) | copy-start | bytes 98308
  123.9 9.0 %copy-start.6 = (f32[2,32,128]{2,1,0:T(8,128)S(1)}, f32[2,32,128]{2,1,0:T(8,128)}, u32[]{:S(2)}) copy-start(f32[2,32,128]{2,1,0:T(8,128)} %get-tuple-element.37.gg_ref) | copy-start | bytes 98308
  132.9 1.0 copy-start.2
  135.2 47.7 %copy-start.1 = (bf16[1024,64]{0,1:T(8,128)(2,1)S(1)}, bf16[1024,64]{0,1:T(8,128)(2,1)}, u32[]{:S(2)}) copy-start(bf16[1024,64]{0,1:T(8,128)(2,1)} %param.13) | copy-start | bytes 393220
  135.2 47.7 %copy-start.3 = (bf16[128,1280]{1,0:T(8,128)(2,1)S(1)}, bf16[128,1280]{1,0:T(8,128)(2,1)}, u32[]{:S(2)}) copy-start(bf16[128,1280]{1,0:T(8,128)(2,1)} %get-tuple-element.27.hot_ref) | copy-start | bytes 983044
  135.2 47.7 %copy-start.4 = (f32[128,64]{1,0:T(8,128)S(1)}, f32[128,64]{1,0:T(8,128)}, u32[]{:S(2)}) copy-start(f32[128,64]{1,0:T(8,128)} %get-tuple-element.28.dense_ref) | copy-start | bytes 98308
  135.2 39.2 %all-to-all-start.3 = ((bf16[32,40,1024]{2,1,0:T(8,128)(2,1)}), bf16[32,40,1024]{2,1,0:T(8,128)(2,1)S(1)}, u32[]{:S(2)}, u32[]{:S(2)}) async-start(bf16[32,40,1024]{2,1,0:T(8,128)(2,1)} %bitcast.13), calls=%async_computation.3 | async-start | bytes 5242880 | tf_op jit(solution)/shard_map/all_to_all | solution.py:441
  175.1 14.7 %all-to-all-start.4 = ((f32[32,1,128]{2,1,0:T(1,128)}), f32[32,1,128]{2,1,0:T(1,128)S(1)}, u32[]{:S(2)}, u32[]{:S(2)}) async-start(f32[32,1,128]{2,1,0:T(1,128)} %broadcast_in_dim.8), calls=%async_computation.4 | async-start | bytes 32768 | tf_op jit(solution)/shard_map/all_to_all | solution.py:441
Sparse Core Ops, SparseCore 0:
  10.1 77.5 all-gather.1

commit v5 on v4

--- a/solution.py
+++ b/solution.py
@@ -14,7 +14,9 @@
 SLOTS = 2 * CAP
 HOSTS = 32
 ROWS = HOSTS * SLOTS
-BLOCK = 2 * SLOTS
+TILES = 8
+SPAN = SLOTS * TILES
+BLOCK = 2 * SPAN + 32
 TOKENS = 128
 
 
@@ -51,7 +53,20 @@
     )
 
 
-def dispatch_kernel(ids_ref, x_ref, dy_ref, out_ref, hot_ref):
+def to_tiles(rows):
+    return [
+        rows[8 * i : 8 * i + 8, 128 * j : 128 * j + 128]
+        for i in range(rows.shape[0] // 8)
+        for j in range(TILES)
+    ]
+
+
+def from_tiles(block, start, i):
+    at = start + 64 * i
+    return jnp.concatenate([block[at + 8 * j : at + 8 * j + 8] for j in range(TILES)], axis=1)
+
+
+def dispatch_kernel(ids_ref, gates_ref, x_ref, dy_ref, out_ref, hot_ref):
     experts, tokens = 2 * HOSTS, x_ref.shape[0]
     hosts = out_ref.shape[0]
 
@@ -76,9 +91,15 @@
     hot = hot_ref[pl.ds(pl.multiple_of(pl.program_id(0) * rows, rows), rows), :]
     xs = jnp.dot(hot, x_ref[...], preferred_element_type=F32)
     ys = jnp.dot(hot, dy_ref[...], preferred_element_type=F32)
+    left = gates_ref[...]
+    route = [ids_ref[...].astype(F32)]
+    for _ in range(3):
+        high = left.astype(BF).astype(F32)
+        route.append(high)
+        left = left - high
     for j in range(hosts):
         at = slice(SLOTS * j, SLOTS * j + SLOTS)
-        out_ref[j] = jnp.concatenate([xs[at], ys[at]], axis=0).astype(BF)
+        out_ref[j] = jnp.concatenate(to_tiles(xs[at]) + to_tiles(ys[at]) + route, axis=0).astype(BF)
 
 
 def vmem():
@@ -97,63 +118,74 @@
     return pl.CostEstimate(flops=flops, bytes_accessed=moved, transcendentals=0)
 
 
-def dispatch(ids_t, tokens, upstream):
+def dispatch(ids_t, gates_t, tokens, upstream):
     steps = 4
     whole = lambda v: pl.BlockSpec(v.shape, lambda i: (0, 0))
     return pl.pallas_call(
         dispatch_kernel,
         grid=(steps,),
-        out_shape=jax.ShapeDtypeStruct((HOSTS, BLOCK, tokens.shape[1]), BF),
-        in_specs=[whole(ids_t), whole(tokens), whole(upstream)],
-        out_specs=pl.BlockSpec((HOSTS // steps, BLOCK, tokens.shape[1]), lambda i: (i, 0, 0)),
+        out_shape=jax.ShapeDtypeStruct((HOSTS, BLOCK, 128), BF),
+        in_specs=[whole(ids_t), whole(gates_t), whole(tokens), whole(upstream)],
+        out_specs=pl.BlockSpec((HOSTS // steps, BLOCK, 128), lambda i: (i, 0, 0)),
         scratch_shapes=[pltpu.VMEM((ROWS, tokens.shape[0]), BF)],
         compiler_params=params(56),
         name="dispatch",
-    )(ids_t, tokens, upstream)
-
-
-def route_kernel(ids_ref, gates_ref, out_ref):
-    route = jnp.concatenate([ids_ref[...].astype(F32), gates_ref[...]], axis=0)
-    for h in range(out_ref.shape[0]):
-        out_ref[h] = route
-
-
-def routes(ids_t, gates_t):
-    top, tokens = ids_t.shape
-    return pl.pallas_call(
-        route_kernel,
-        out_shape=jax.ShapeDtypeStruct((HOSTS, 2 * top, tokens), F32),
-        in_specs=[vmem(), vmem()],
-        out_specs=vmem(),
-        compiler_params=params(56),
-        name="routes",
-    )(ids_t, gates_t)
+    )(ids_t, gates_t, tokens, upstream)
 
 
 def pieces(a, b, start, e):
-    at = start + 16 * e
-    return jnp.concatenate(
-        [a[at : at + 16], b[at : at + 16], a[start + 32 : start + 40], b[start + 32 : start + 40]],
-        axis=0,
-    ).astype(BF)
-
-
-def prep_kernel(host_ref, route_ref, rows_ref, xe_ref, dye_ref, hot_ref, gcol_ref, gate_ref):
+    rows = [from_tiles(v, start, i) for v in (a, b) for i in (2 * e, 2 * e + 1)]
+    rows += [from_tiles(v, start, 4) for v in (a, b)]
+    return jnp.concatenate(rows, axis=0).astype(BF)
+
+
+HALVES = 2
+SOURCES = HOSTS // HALVES
+COMPACT = SOURCES * 24
+
+
+def compact_shape(last, kind):
+    return jax.ShapeDtypeStruct((HALVES, 2, COMPACT, last), kind)
+
+
+def compact_spec(last):
+    return pl.BlockSpec((1, 2, COMPACT, last), lambda i: (i, 0, 0, 0))
+
+
+def dense_shape():
+    return jax.ShapeDtypeStruct((2, HOSTS, TOKENS), F32)
+
+
+def dense_spec():
+    return pl.BlockSpec((2, SOURCES, TOKENS), lambda i: (0, i, 0))
+
+
+def forward_kernel(
+    host_ref, rows_ref, w_ref,
+    xe_ref, hot_ref, gu_ref, add_ref, gg_ref, gate_ref, share_ref,
+    dye_ref, ids_ref, gates_ref, gcol_ref,
+):
     sources = rows_ref.shape[0]
     pairs = sources // 2
     width = hot_ref.shape[3]
+    ff = w_ref.shape[2] // 3
     for p in range(pairs):
         a, b = rows_ref[2 * p].astype(F32), rows_ref[2 * p + 1].astype(F32)
         for e in (0, 1):
             xe_ref[0, e, 48 * p : 48 * p + 48, :] = pieces(a, b, 0, e)
-            dye_ref[0, e, 48 * p : 48 * p + 48, :] = pieces(a, b, SLOTS, e)
-    ids = route_ref[:, 0:8, :]
-    gates = route_ref[:, 8:16, :]
+            dye_ref[e, 48 * p : 48 * p + 48, :] = pieces(a, b, SPAN, e)
+        for n, v in ((2 * p, a), (2 * p + 1, b)):
+            at = 2 * SPAN
+            ids_ref[n] = v[at : at + 8]
+            gates_ref[n] = v[at + 8 : at + 16] + v[at + 16 : at + 24] + v[at + 24 : at + 32]
+    ids, gates = ids_ref[...], gates_ref[...]
     upper = strict(width, width, True)
     host = host_ref[0]
     row8 = lax.broadcasted_iota(jnp.int32, (8, width), 0)
     row16 = lax.broadcasted_iota(jnp.int32, (16, width), 0).astype(F32) + 1.0
     spread = lambda v, n: jnp.broadcast_to(v, (n, width))
+    down = lambda v: jnp.sum(v, axis=0, keepdims=True)
+    total = jnp.zeros((sources, width), F32)
     for e in (0, 1):
         match = ids == (2 * host + e).astype(F32)
         member = jnp.sum(jnp.where(match, 1.0, 0.0), axis=1)
@@ -181,70 +213,15 @@
                 [spread(ga, 16), spread(gb, 16), spread(ga, 8), spread(gb, 8)], axis=0
             )
             hot_ref[0, e, 48 * p : 48 * p + 48, :] = hot.astype(BF)
-            gcol_ref[0, e, 48 * p : 48 * p + 48, :] = jnp.sum(hot * weight, axis=1, keepdims=True)
-
-
-HALVES = 2
-SOURCES = HOSTS // HALVES
-COMPACT = SOURCES * 24
-
-
-def compact_shape(last, kind):
-    return jax.ShapeDtypeStruct((HALVES, 2, COMPACT, last), kind)
-
-
-def compact_spec(last):
-    return pl.BlockSpec((1, 2, COMPACT, last), lambda i: (i, 0, 0, 0))
-
-
-def dense_shape():
-    return jax.ShapeDtypeStruct((2, HOSTS, TOKENS), F32)
-
-
-def dense_spec():
-    return pl.BlockSpec((2, SOURCES, TOKENS), lambda i: (0, i, 0))
-
-
-def prep(host, route, blocks):
-    model = blocks.shape[2]
-    return pl.pallas_call(
-        prep_kernel,
-        grid=(HALVES,),
-        out_shape=(
-            compact_shape(model, BF), compact_shape(model, BF), compact_shape(TOKENS, BF),
-            compact_shape(1, F32), dense_shape(),
-        ),
-        in_specs=[
-            smem(),
-            pl.BlockSpec((SOURCES, 16, TOKENS), lambda i: (i, 0, 0)),
-            pl.BlockSpec((SOURCES, BLOCK, model), lambda i: (i, 0, 0)),
-        ],
-        out_specs=(
-            compact_spec(model), compact_spec(model), compact_spec(TOKENS),
-            compact_spec(1), dense_spec(),
-        ),
-        compiler_params=params(56),
-        cost_estimate=cost(1_000_000, 14_000_000),
-        name="prep",
-    )(host, route, blocks)
-
-
-def forward_kernel(
-    xe_ref, dye_ref, hot_ref, gcol_ref, gate_ref, w_ref, gu_ref, add_ref, gg_ref, share_ref,
-):
-    pairs = COMPACT // 48
-    ff = w_ref.shape[2] // 3
-    total = jnp.zeros(share_ref.shape[1:], F32)
-    down = lambda v: jnp.sum(v, axis=0, keepdims=True)
-    for e in (0, 1):
+            gcol_ref[e, 48 * p : 48 * p + 48, :] = jnp.sum(hot * weight, axis=1, keepdims=True)
         pre = jnp.dot(xe_ref[0, e], w_ref[e, :, 0 : 2 * ff], preferred_element_type=F32)
-        hidden_grad = jnp.dot(dye_ref[0, e], w_ref[e, :, 2 * ff :], preferred_element_type=F32)
+        hidden_grad = jnp.dot(dye_ref[e], w_ref[e, :, 2 * ff :], preferred_element_type=F32)
         pre_gate, pre_up = pre[:, 0:ff], pre[:, ff:]
         sigma = jax.nn.sigmoid(pre_gate)
         active = pre_gate * sigma
         hidden = (active * pre_up).astype(BF).astype(F32)
         gg = jnp.sum(hidden_grad * hidden, axis=1, keepdims=True).astype(BF).astype(F32)
-        gcol = gcol_ref[0, e]
+        gcol = gcol_ref[e]
         scaled = hidden_grad * gcol
         gu_ref[0, e, :, 0:ff] = (
             scaled * pre_up * sigma * (1.0 + pre_gate * (1.0 - sigma))
@@ -255,34 +232,43 @@
             hit = hot_ref[0, e, 48 * p : 48 * p + 48, :].astype(F32) * gg[48 * p : 48 * p + 48]
             gg_ref[e, 2 * p : 2 * p + 1, :] = down(hit[0:16]) + down(hit[32:40])
             gg_ref[e, 2 * p + 1 : 2 * p + 2, :] = down(hit[16:32]) + down(hit[40:48])
-        total = total + gate_ref[e] * gg_ref[e]
+        total = total + gate * gg_ref[e]
     total = total.astype(BF)
     for h in range(HOSTS):
         share_ref[h] = total
 
 
-def forward(xe, dye, hot, gcol, gate, weights):
+def forward(host, blocks, weights):
     _, model, triple = weights.shape
+    double = triple // 3 * 2
     return pl.pallas_call(
         forward_kernel,
         grid=(HALVES,),
         out_shape=(
-            compact_shape(triple // 3 * 2, BF), compact_shape(1, F32), dense_shape(),
+            compact_shape(model, BF), compact_shape(TOKENS, BF), compact_shape(double, BF),
+            compact_shape(1, F32), dense_shape(), dense_shape(),
             jax.ShapeDtypeStruct((HOSTS, HOSTS, TOKENS), BF),
         ),
         in_specs=[
-            compact_spec(model), compact_spec(model), compact_spec(TOKENS),
-            compact_spec(1), dense_spec(),
+            smem(),
+            pl.BlockSpec((SOURCES, BLOCK, 128), lambda i: (i, 0, 0)),
             pl.BlockSpec(weights.shape, lambda i: (0, 0, 0)),
         ],
         out_specs=(
-            compact_spec(triple // 3 * 2), compact_spec(1), dense_spec(),
+            compact_spec(model), compact_spec(TOKENS), compact_spec(double),
+            compact_spec(1), dense_spec(), dense_spec(),
             pl.BlockSpec((HOSTS, SOURCES, TOKENS), lambda i: (0, i, 0)),
         ),
+        scratch_shapes=[
+            pltpu.VMEM((2, COMPACT, model), BF),
+            pltpu.VMEM((SOURCES, 8, TOKENS), F32),
+            pltpu.VMEM((SOURCES, 8, TOKENS), F32),
+            pltpu.VMEM((2, COMPACT, 1), F32),
+        ],
         compiler_params=params(56),
         cost_estimate=cost(4 * HALVES * COMPACT * model * triple, 20_000_000),
         name="forward",
-    )(xe, dye, hot, gcol, gate, weights)
+    )(host, blocks, weights)
 
 
 def backward_kernel(host_ref, gu_ref, add_ref, rw_ref, w_ref, out_ref, re_ref):
@@ -450,15 +436,11 @@
     ids_t = expert_ids.T
     shard = expert_weights.transpose(0, 2, 1, 3).reshape(per_host, part, 3 * ff)
     weights = lax.all_gather(shard, "dp", axis=1, tiled=True)
-    route = exchange(routes(ids_t, gates.T))
-    sent = dispatch(ids_t, tokens, upstream)
-    route, sent = lax.optimization_barrier((route, sent))
-    blocks = exchange(sent)
+    blocks = exchange(dispatch(ids_t, gates.T, tokens, upstream))
     places, dense = lookup(expert_ids, gates)
     blocks, places, dense = lax.optimization_barrier((blocks, places, dense))
     rw_t = router_weight.T
-    xe, dye, hot, gcol, gate = prep(host_arr, route, blocks)
-    gu, add, gg, share = forward(xe, dye, hot, gcol, gate, weights)
+    xe, hot, gu, add, gg, gate, share = forward(host_arr, blocks, weights)
     shares = exchange(share)
     rows = backward(host_arr, gu, add, rw_t, weights)
     piece, sums = router_part(shares, gg, gate, hot, xe)

time: 199 us -> 188 us (0.945)
  Pallas kernels: 33.1 us -> 26.5 us
  starting transfers between devices: 37.1 us -> 34.5 us
    pallas_call x3 -> x1, Pallas kernels: 16.4 us -> 9.91 us  [forward(): pl.pallas_call(forward_kernel, grid=(HALVES,), out_shape=(compact_shape(m...]
    all_to_all x5 -> x4, starting transfers between devices: 37 us -> 34.5 us  [exchange(): lax.all_to_all(rows, 'expert', split_axis=0, concat_axis=0, tiled=True)]
    all_to_all x5 -> x4, waiting for transfers between devices: 77.2 us -> 76 us  [exchange(): lax.all_to_all(rows, 'expert', split_axis=0, concat_axis=0, tiled=True)]
  transfers between devices with their start and end apart: 6 -> 5, of which waited for: 5 -> 4; matrix products, arithmetic and copies ran while one was open for 1% -> 1% of each run, Pallas kernels for 11% -> 8%
where the time goes in v5:
time: 188 us
  waiting for transfers between devices  76.1 us (40%)
  starting transfers between devices  34.5 us (18%)
  blocking collectives  29.6 us (16%)
  Pallas kernels  26.5 us (14%)
  between operations  14.2 us (8%)
  local copies, waits for them, and re-layouts  6.26 us (3%)
    all_to_all x4, waiting for transfers between devices, exchange(): lax.all_to_all(rows, 'expert', split_axis=0, concat_axis=0, tiled=True)  76 us
    all_to_all x4, starting transfers between devices, exchange(): lax.all_to_all(rows, 'expert', split_axis=0, concat_axis=0, tiled=True)  34.5 us
    all_gather x1, blocking collectives, body(): everyone = lax.all_gather(piece.reshape(-1, 128), 'dp', axis=0, tiled=False)  29.6 us
    pallas_call x1, Pallas kernels, forward(): pl.pallas_call(forward_kernel, grid=(HALVES,), out_shape=(compact_shape(m...  9.91 us
    pallas_call x1, Pallas kernels, backward(): pl.pallas_call(backward_kernel, grid=(HALVES,), out_shape=jax.ShapeDtypeS...  6.59 us
    pallas_call x1, Pallas kernels, dispatch(): pl.pallas_call(dispatch_kernel, grid=(steps,), out_shape=jax.ShapeDtypeSt...  4.98 us
  transfers between devices with their start and end apart: 5, of which 4 were waited for; matrix products, arithmetic and copies ran while one was open for 1% of the time, Pallas kernels for 8%

profile of v5, /device:TPU:1, one launch (start us, length us, event | category | flops | bytes accessed | tf_op | source)
XLA Modules:
  0.0 187.8 jit_solution(17578647522835069682)
XLA Ops:
  7.2 0.0 all-gather.2.cloned.1.call-start
  7.2 1.7 copy.21
  8.9 0.0 all-gather.2.cloned.1.call-update
  8.9 5.0 %dispatch.1 = bf16[32,672,128]{2,1,0:T(8,128)(2,1)} custom-call(s32[8,128]{1,0:T(8,128)} %bitcast.17, f32[8,128]{1,0:T(8,128)} %bitcast.18, bf16[128,1024]{1,0:T(8,128)(2,1)} %x_ref.1, bf16[128,1024]{1,0:T(8,128)(2,1)} %dy_ref.1), custom_call_target="tpu_custom_call" | custom-call | tf_op jit(solution)/shard_map/dispatch/pallas_call | solution.py:124
  13.9 0.0 copy-start.7
  13.9 0.0 copy-start.8
  13.9 11.5 %all-to-all-start = ((bf16[32,672,128]{2,1,0:T(8,128)(2,1)}), bf16[32,672,128]{2,1,0:T(8,128)(2,1)}, u32[]{:S(2)}, u32[]{:S(2)}) async-start(bf16[32,672,128]{2,1,0:T(8,128)(2,1)} %dispatch.1), calls=%async_computation | async-start | bytes 11010048 | tf_op jit(solution)/shard_map/all_to_all | solution.py:427
  25.4 0.0 copy-done.7
  25.4 0.7 copy.17.ids_ref
  26.2 0.0 copy-done.8
  26.2 0.7 copy.18.gates_ref
  26.9 2.4 %lookup.1 = (bf16[128,1280]{1,0:T(8,128)(2,1)}, f32[128,64]{1,0:T(8,128)}) custom-call(s32[128,8]{1,0:T(8,128)} %copy.17.ids_ref, f32[128,8]{1,0:T(8,128)} %copy.18.gates_ref, bf16[64,1280]{1,0:T(8,128)(2,1)} %constant.21.clone.expand_ref, f32[1,1280]{1,0:T(1,128)} %constant.22.clone.rank_ref), custom_call_target="tpu_custom_call" | custom-call | tf_op jit(solution)/shard_map/lookup/pallas_call | solution.py:390
  29.2 64.0 %all-to-all-done.rows_ref = bf16[32,672,128]{2,1,0:T(8,128)(2,1)} async-done(((bf16[32,672,128]{2,1,0:T(8,128)(2,1)}), bf16[32,672,128]{2,1,0:T(8,128)(2,1)}, u32[]{:S(2)}, u32[]{:S(2)}) %all-to-all-start) | async-done | bytes 5505056 | tf_op jit(solution)/shard_map/all_to_all | solution.py:427
  93.3 0.0 all-gather.2.cloned.1.call-done.w_ref
  93.3 9.9 %forward.1 = (bf16[2,2,384,1024]{3,2,1,0:T(8,128)(2,1)}, bf16[2,2,384,128]{3,2,1,0:T(8,128)(2,1)}, bf16[2,2,384,768]{3,2,1,0:T(8,128)(2,1)}, f32[2,2,384,1]{3,2,...) custom-call(s32[1]{0:T(128)} %bitcast.host_ref, ...), custom_call_target="tpu_custom_call" | custom-call | flops 3623878656 | bytes 20000000 | tf_op jit(solution)/shard_map/forward/pallas_call | solution.py:244
  103.2 9.6 %all-to-all-start.1 = ((bf16[32,32,128]{2,1,0:T(8,128)(2,1)}), bf16[32,32,128]{2,1,0:T(8,128)(2,1)S(1)}, u32[]{:S(2)}, u32[]{:S(2)}) async-start(bf16[32,32,128]{2,1,0:T(8,128)(2,1)} %get-tuple-element.25), calls=%async_computation.1 | async-start | bytes 524288 | tf_op jit(solution)/shard_map/all_to_all | solution.py:427
  112.8 0.0 copy-start
  112.8 0.0 copy-start.5
  112.9 0.0 copy-start.6
  112.9 6.6 %backward.1 = bf16[1280,1024]{1,0:T(8,128)(2,1)} custom-call(s32[1]{0:T(128)} %bitcast.host_ref, bf16[2,2,384,768]{3,2,1,0:T(8,128)(2,1)} %get-tuple-element.32.gu_ref, f32[2,2,384,1]{3,2,1,0:T(8,128)} %get-tuple-element.33.add_ref, bf16[64,1024]{1,0:T(8,128)(2,1)} %bitcast.11, bf16[2,1024,1152]{2,1,0:T(8,128)(2,1)} %all-gather.2.cloned.1.call-done.w_ref), custom_call_target="tpu_custom_call" | custom-call | flops 2415919104 | bytes 10000000 | tf_op jit(solution)/shard_map/backward/pallas_call | solution.py:299
  119.5 2.4 %all-to-all-done.1.shares_ref = bf16[32,32,128]{2,1,0:T(8,128)(2,1)S(1)} async-done(((bf16[32,32,128]{2,1,0:T(8,128)(2,1)}), bf16[32,32,128]{2,1,0:T(8,128)(2,1)S(1)}, u32[]{:S(2)}, u32[]{:S(2)}) %all-to-all-start.1) | async-done | bytes 262176 | tf_op jit(solution)/shard_map/all_to_all | solution.py:427
  121.8 0.0 copy-done
  121.8 0.0 copy-done.5
  121.8 0.0 copy-done.6
  121.8 0.0 copy-start.2
  121.8 1.0 copy-done.2
  122.8 1.3 router_part.1
  124.2 0.0 copy-start.1
  124.2 0.0 copy-start.3
  124.2 0.0 copy-start.4
  124.2 5.2 %all-to-all-start.2 = ((bf16[32,40,1024]{2,1,0:T(8,128)(2,1)}), bf16[32,40,1024]{2,1,0:T(8,128)(2,1)S(1)}, u32[]{:S(2)}, u32[]{:S(2)}) async-start(bf16[32,40,1024]{2,1,0:T(8,128)(2,1)} %bitcast.13), calls=%async_computation.2 | async-start | bytes 5242880 | tf_op jit(solution)/shard_map/all_to_all | solution.py:427
  129.4 29.6 %all_gather.7 = f32[16,16,128]{2,1,0:T(8,128)S(1)} all-gather(f32[1,16,128]{2,1,0:T(8,128)S(1)} %all_gather_reshape.3), channel_id=1, replica_groups=mesh['dp'=16,'expert'=32] {'dp'}, dimensions={0}, use_global_device_ids=true | all-gather | bytes 139264 | tf_op jit(solution)/shard_map/all_gather | solution.py:449
  159.1 0.1 constant_dynamic-slice_fusion
  159.2 4.1 %all-to-all-done.2 = bf16[32,40,1024]{2,1,0:T(8,128)(2,1)S(1)} async-done(((bf16[32,40,1024]{2,1,0:T(8,128)(2,1)}), bf16[32,40,1024]{2,1,0:T(8,128)(2,1)S(1)}, u32[]{:S(2)}, u32[]{:S(2)}) %all-to-all-start.2) | async-done | bytes 2621472 | tf_op jit(solution)/shard_map/all_to_all | solution.py:427
  163.3 0.1 broadcast_in_dim.7
  163.4 0.6 broadcast_in_dim.8
  164.0 8.1 %all-to-all-start.3 = ((f32[32,1,128]{2,1,0:T(1,128)}), f32[32,1,128]{2,1,0:T(1,128)S(1)}, u32[]{:S(2)}, u32[]{:S(2)}) async-start(f32[32,1,128]{2,1,0:T(1,128)} %broadcast_in_dim.8), calls=%async_computation.3 | async-start | bytes 32768 | tf_op jit(solution)/shard_map/all_to_all | solution.py:427
  172.1 0.0 copy-done.1
  172.1 0.0 copy-done.3
  172.1 0.0 copy-done.4
  172.2 1.3 combine.1
  173.5 5.5 %all-to-all-done.3 = f32[32,1,128]{2,1,0:T(1,128)S(1)} async-done(((f32[32,1,128]{2,1,0:T(1,128)}), f32[32,1,128]{2,1,0:T(1,128)S(1)}, u32[]{:S(2)}, u32[]{:S(2)}) %all-to-all-start.3) | async-done | bytes 16416 | tf_op jit(solution)/shard_map/all_to_all | solution.py:427
  179.0 0.5 broadcast.6
  179.5 0.7 reduce.3
  180.2 0.1 reshape.31
  180.3 0.7 copy.20
  (3 shorter events, 0.0 us)
Async XLA Ops:
  7.2 86.1 %all-gather.2.cloned.1.call-start = ((), (), s32[]{:S(2)}) async-start(), calls=%async_computation.4 | async-start | bytes 5013504 | tf_op jit(solution)/shard_map/all_gather | solution.py:438
  13.9 11.5 %copy-start.7 = (s32[128,8]{0,1:T(8,128)S(1)}, s32[128,8]{0,1:T(8,128)}, u32[]{:S(2)}) copy-start(s32[128,8]{0,1:T(8,128)} %param.10) | copy-start | bytes 12292
  13.9 12.2 %copy-start.8 = (f32[128,8]{0,1:T(8,128)S(1)}, f32[128,8]{0,1:T(8,128)}, u32[]{:S(2)}) copy-start(f32[128,8]{0,1:T(8,128)} %param.11) | copy-start | bytes 12292
  13.9 79.3 %all-to-all-start = ((bf16[32,672,128]{2,1,0:T(8,128)(2,1)}), bf16[32,672,128]{2,1,0:T(8,128)(2,1)}, u32[]{:S(2)}, u32[]{:S(2)}) async-start(bf16[32,672,128]{2,1,0:T(8,128)(2,1)} %dispatch.1), calls=%async_computation | async-start | bytes 11010048 | tf_op jit(solution)/shard_map/all_to_all | solution.py:427
  103.2 18.6 %all-to-all-start.1 = ((bf16[32,32,128]{2,1,0:T(8,128)(2,1)}), bf16[32,32,128]{2,1,0:T(8,128)(2,1)S(1)}, u32[]{:S(2)}, u32[]{:S(2)}) async-start(bf16[32,32,128]{2,1,0:T(8,128)(2,1)} %get-tuple-element.25), calls=%async_computation.1 | async-start | bytes 524288 | tf_op jit(solution)/shard_map/all_to_all | solution.py:427
  112.8 9.0 %copy-start = (bf16[2,2,384,1024]{3,2,1,0:T(8,128)(2,1)S(1)}, bf16[2,2,384,1024]{3,2,1,0:T(8,128)(2,1)}, u32[]{:S(2)}) copy-start(bf16[2,2,384,1024]{3,2,1,0:T(8,128)(2,1)} %get-tuple-element.29.xe_hbm) | copy-start | bytes 9437188
  112.8 9.0 %copy-start.5 = (f32[2,32,128]{2,1,0:T(8,128)S(1)}, f32[2,32,128]{2,1,0:T(8,128)}, u32[]{:S(2)}) copy-start(f32[2,32,128]{2,1,0:T(8,128)} %get-tuple-element.26.gg_ref) | copy-start | bytes 98308
  112.9 9.0 %copy-start.6 = (f32[2,32,128]{2,1,0:T(8,128)S(1)}, f32[2,32,128]{2,1,0:T(8,128)}, u32[]{:S(2)}) copy-start(f32[2,32,128]{2,1,0:T(8,128)} %get-tuple-element.27.gate_ref) | copy-start | bytes 98308
  121.8 1.0 copy-start.2
  124.2 48.0 %copy-start.1 = (bf16[1024,64]{0,1:T(8,128)(2,1)S(1)}, bf16[1024,64]{0,1:T(8,128)(2,1)}, u32[]{:S(2)}) copy-start(bf16[1024,64]{0,1:T(8,128)(2,1)} %param.13) | copy-start | bytes 393220
  124.2 48.0 %copy-start.3 = (bf16[128,1280]{1,0:T(8,128)(2,1)S(1)}, bf16[128,1280]{1,0:T(8,128)(2,1)}, u32[]{:S(2)}) copy-start(bf16[128,1280]{1,0:T(8,128)(2,1)} %get-tuple-element.22.hot_ref) | copy-start | bytes 983044
  124.2 48.0 %copy-start.4 = (f32[128,64]{1,0:T(8,128)S(1)}, f32[128,64]{1,0:T(8,128)}, u32[]{:S(2)}) copy-start(f32[128,64]{1,0:T(8,128)} %get-tuple-element.23.dense_ref) | copy-start | bytes 98308
  124.2 39.1 %all-to-all-start.2 = ((bf16[32,40,1024]{2,1,0:T(8,128)(2,1)}), bf16[32,40,1024]{2,1,0:T(8,128)(2,1)S(1)}, u32[]{:S(2)}, u32[]{:S(2)}) async-start(bf16[32,40,1024]{2,1,0:T(8,128)(2,1)} %bitcast.13), calls=%async_computation.2 | async-start | bytes 5242880 | tf_op jit(solution)/shard_map/all_to_all | solution.py:427
  164.0 15.0 %all-to-all-start.3 = ((f32[32,1,128]{2,1,0:T(1,128)}), f32[32,1,128]{2,1,0:T(1,128)S(1)}, u32[]{:S(2)}, u32[]{:S(2)}) async-start(f32[32,1,128]{2,1,0:T(1,128)} %broadcast_in_dim.8), calls=%async_computation.3 | async-start | bytes 32768 | tf_op jit(solution)/shard_map/all_to_all | solution.py:427
Sparse Core Ops, SparseCore 0:
  10.1 77.5 all-gather.1

commit v6 on v5

--- a/solution.py
+++ b/solution.py
@@ -1,4 +1,4 @@
-import functools
+import math
 
 import jax
 import jax.numpy as jnp
@@ -444,10 +444,12 @@
     shares = exchange(share)
     rows = backward(host_arr, gu, add, rw_t, weights)
     piece, sums = router_part(shares, gg, gate, hot, xe)
-    piece, rows = lax.optimization_barrier((piece, rows))
     back = exchange(rows)
-    everyone = lax.all_gather(piece.reshape(-1, 128), "dp", axis=0, tiled=False)
-    column = jnp.sum(everyone, axis=0).reshape(per_host, model)
+    side = math.isqrt(lax.axis_size("dp"))
+    near = [[side * h + l for l in range(side)] for h in range(side)]
+    far = [[side * h + l for h in range(side)] for l in range(side)]
+    column = lax.psum(piece.reshape(-1, 128), "dp", axis_index_groups=near)
+    column = lax.psum(column, "dp", axis_index_groups=far).reshape(per_host, model)
     column = lax.dynamic_slice_in_dim(column, part * group, part, 1)
     column, back = lax.optimization_barrier((column, back))
     columns = exchange(jnp.broadcast_to(column.reshape(1, -1), (HOSTS, per_host * part)))

time: 188 us -> 186 us (0.989)
  local copies, waits for them, and re-layouts: 6.26 us -> 9.39 us
  waiting for transfers between devices: 76.1 us -> 73.3 us
  blocking collectives: 29.6 us -> 27.1 us
    all_gather x1 -> x0, blocking collectives: 29.6 us -> none  [body(): everyone = lax.all_gather(piece.reshape(-1, 128), 'dp', axis=0, tiled=False)]
    psum x0 -> x2, blocking collectives: none -> 27.1 us  [the longest x1 17 us: body(): lax.psum(column, 'dp', axis_index_groups=far).reshape(per_host, model)]
    all_to_all x4, waiting for transfers between devices: 76 us -> 73.2 us  [exchange(): lax.all_to_all(rows, 'expert', split_axis=0, concat_axis=0, tiled=True)]
    unnamed x21 -> x23, local copies, waits for them, and re-layouts: 3.16 us -> 5.61 us
  transfers between devices with their start and end apart: 5 -> 5, of which waited for: 4 -> 4; matrix products, arithmetic and copies ran while one was open for 1% -> 1% of each run, Pallas kernels for 8% -> 9%
where the time goes in v6:
time: 186 us
  waiting for transfers between devices  73.3 us (39%)
  starting transfers between devices  34.6 us (19%)
  blocking collectives  27.1 us (15%)
  Pallas kernels  26.4 us (14%)
  between operations  14.2 us (8%)
  local copies, waits for them, and re-layouts  9.39 us (5%)
    all_to_all x4, waiting for transfers between devices, exchange(): lax.all_to_all(rows, 'expert', split_axis=0, concat_axis=0, tiled=True)  73.2 us
    all_to_all x4, starting transfers between devices, exchange(): lax.all_to_all(rows, 'expert', split_axis=0, concat_axis=0, tiled=True)  34.5 us
    psum x1, blocking collectives, body(): lax.psum(column, 'dp', axis_index_groups=far).reshape(per_host, model)  17 us
    psum x1, blocking collectives, body(): column = lax.psum(piece.reshape(-1, 128), 'dp', axis_index_groups=near)  10.1 us
    pallas_call x1, Pallas kernels, forward(): pl.pallas_call(forward_kernel, grid=(HALVES,), out_shape=(compact_shape(m...  9.91 us
    pallas_call x1, Pallas kernels, backward(): pl.pallas_call(backward_kernel, grid=(HALVES,), out_shape=jax.ShapeDtypeS...  6.47 us
    unnamed x23, local copies, waits for them, and re-layouts  5.61 us
    pallas_call x1, Pallas kernels, dispatch(): pl.pallas_call(dispatch_kernel, grid=(steps,), out_shape=jax.ShapeDtypeSt...  4.96 us
  transfers between devices with their start and end apart: 5, of which 4 were waited for; matrix products, arithmetic and copies ran while one was open for 1% of the time, Pallas kernels for 9%

profile of v6, /device:TPU:1, one launch (start us, length us, event | category | flops | bytes accessed | tf_op | source)
XLA Modules:
  0.0 185.5 jit_solution(4599686955477103658)
XLA Ops:
  7.2 0.0 all-gather.2.cloned.1.call-start
  7.2 1.7 copy.21
  8.9 0.0 all-gather.2.cloned.1.call-update
  8.9 5.0 %dispatch.1 = bf16[32,672,128]{2,1,0:T(8,128)(2,1)} custom-call(s32[8,128]{1,0:T(8,128)} %bitcast.17, f32[8,128]{1,0:T(8,128)} %bitcast.18, bf16[128,1024]{1,0:T(8,128)(2,1)} %x_ref.1, bf16[128,1024]{1,0:T(8,128)(2,1)} %dy_ref.1), custom_call_target="tpu_custom_call" | custom-call | tf_op jit(solution)/shard_map/dispatch/pallas_call | solution.py:124
  13.9 0.0 copy-start.8
  13.9 0.0 copy-start.9
  13.9 11.5 %all-to-all-start = ((bf16[32,672,128]{2,1,0:T(8,128)(2,1)}), bf16[32,672,128]{2,1,0:T(8,128)(2,1)}, u32[]{:S(2)}, u32[]{:S(2)}) async-start(bf16[32,672,128]{2,1,0:T(8,128)(2,1)} %dispatch.1), calls=%async_computation | async-start | bytes 11010048 | tf_op jit(solution)/shard_map/all_to_all | solution.py:427
  25.4 0.0 copy-done.8
  25.4 0.7 copy.17.ids_ref
  26.1 0.0 copy-done.9
  26.1 0.7 copy.18.gates_ref
  26.9 2.4 %lookup.1 = (bf16[128,1280]{1,0:T(8,128)(2,1)}, f32[128,64]{1,0:T(8,128)}) custom-call(s32[128,8]{1,0:T(8,128)} %copy.17.ids_ref, f32[128,8]{1,0:T(8,128)} %copy.18.gates_ref, bf16[64,1280]{1,0:T(8,128)(2,1)} %constant.19.clone.expand_ref, f32[1,1280]{1,0:T(1,128)} %constant.20.clone.rank_ref), custom_call_target="tpu_custom_call" | custom-call | tf_op jit(solution)/shard_map/lookup/pallas_call | solution.py:390
  29.2 64.0 %all-to-all-done.rows_ref = bf16[32,672,128]{2,1,0:T(8,128)(2,1)} async-done(((bf16[32,672,128]{2,1,0:T(8,128)(2,1)}), bf16[32,672,128]{2,1,0:T(8,128)(2,1)}, u32[]{:S(2)}, u32[]{:S(2)}) %all-to-all-start) | async-done | bytes 5505056 | tf_op jit(solution)/shard_map/all_to_all | solution.py:427
  93.3 0.0 all-gather.2.cloned.1.call-done.w_ref
  93.3 9.9 %forward.1 = (bf16[2,2,384,1024]{3,2,1,0:T(8,128)(2,1)}, bf16[2,2,384,128]{3,2,1,0:T(8,128)(2,1)}, bf16[2,2,384,768]{3,2,1,0:T(8,128)(2,1)}, f32[2,2,384,1]{3,2,...) custom-call(s32[1]{0:T(128)} %bitcast.host_ref, ...), custom_call_target="tpu_custom_call" | custom-call | flops 3623878656 | bytes 20000000 | tf_op jit(solution)/shard_map/forward/pallas_call | solution.py:244
  103.2 9.6 %all-to-all-start.1 = ((bf16[32,32,128]{2,1,0:T(8,128)(2,1)}), bf16[32,32,128]{2,1,0:T(8,128)(2,1)S(1)}, u32[]{:S(2)}, u32[]{:S(2)}) async-start(bf16[32,32,128]{2,1,0:T(8,128)(2,1)} %get-tuple-element.23), calls=%async_computation.1 | async-start | bytes 524288 | tf_op jit(solution)/shard_map/all_to_all | solution.py:427
  112.8 6.5 %backward.1 = bf16[1280,1024]{1,0:T(8,128)(2,1)} custom-call(s32[1]{0:T(128)} %bitcast.host_ref, bf16[2,2,384,768]{3,2,1,0:T(8,128)(2,1)} %get-tuple-element.30.gu_ref, f32[2,2,384,1]{3,2,1,0:T(8,128)} %get-tuple-element.31.add_ref, bf16[64,1024]{1,0:T(8,128)(2,1)} %bitcast.11, bf16[2,1024,1152]{2,1,0:T(8,128)(2,1)} %all-gather.2.cloned.1.call-done.w_ref), custom_call_target="tpu_custom_call" | custom-call | flops 2415919104 | bytes 10000000 | tf_op jit(solution)/shard_map/backward/pallas_call | solution.py:299
  119.3 0.0 copy-start.2
  119.3 0.0 copy-start.5
  119.3 0.0 copy-start.6
  119.3 2.5 %all-to-all-done.1.shares_ref = bf16[32,32,128]{2,1,0:T(8,128)(2,1)S(1)} async-done(((bf16[32,32,128]{2,1,0:T(8,128)(2,1)}), bf16[32,32,128]{2,1,0:T(8,128)(2,1)S(1)}, u32[]{:S(2)}, u32[]{:S(2)}) %all-to-all-start.1) | async-done | bytes 262176 | tf_op jit(solution)/shard_map/all_to_all | solution.py:427
  121.8 0.0 copy-start.1
  121.8 0.0 copy-start.4
  121.8 5.0 %all-to-all-start.2 = ((bf16[32,40,1024]{2,1,0:T(8,128)(2,1)}), bf16[32,40,1024]{2,1,0:T(8,128)(2,1)S(1)}, u32[]{:S(2)}, u32[]{:S(2)}) async-start(bf16[32,40,1024]{2,1,0:T(8,128)(2,1)} %bitcast.13), calls=%async_computation.2 | async-start | bytes 5242880 | tf_op jit(solution)/shard_map/all_to_all | solution.py:427
  126.9 0.0 copy-done.2
  126.9 0.0 copy-done.5
  126.9 0.0 copy-done.6
  126.9 0.0 copy-start
  126.9 1.9 %copy-done = bf16[2,2,384,1024]{3,2,1,0:T(8,128)(2,1)S(1)} copy-done((bf16[2,2,384,1024]{3,2,1,0:T(8,128)(2,1)S(1)}, bf16[2,2,384,1024]{3,2,1,0:T(8,128)(2,1)}, u32[]{:S(2)}) %copy-start) | copy-done | bytes 3145752
  128.8 1.3 router_part.1
  130.1 0.0 copy-start.7
  130.1 0.6 copy-done.7
  130.7 0.7 reshape.33
  131.4 10.1 %psum.14 = f32[16,128]{1,0:T(8,128)S(1)} all-reduce(f32[16,128]{1,0:T(8,128)S(1)} %reshape.33), channel_id=1, replica_groups={{0,32,64,96},{128,160,192,224},{256,288,320,352},{384,416,448,480},{1,3..., use_global_device_ids=true, to_apply=%region_0.0 | all-reduce | flops 2048 | bytes 16384 | tf_op jit(solution)/shard_map/psum | solution.py:451
  141.5 17.0 %psum.15 = f32[2,1024]{1,0:T(2,128)S(1)} all-reduce(f32[2,1024]{1,0:T(2,128)S(1)} %reshape.34), channel_id=1, replica_groups={{0,128,256,384},{32,160,288,416},{64,192,320,448},{96,224,352,480},{1,1..., use_global_device_ids=true, to_apply=%region_1.0 | all-reduce | flops 2048 | bytes 16384 | tf_op jit(solution)/shard_map/psum | solution.py:452
  158.5 0.1 constant_dynamic-slice_fusion
  158.6 2.1 %all-to-all-done.2 = bf16[32,40,1024]{2,1,0:T(8,128)(2,1)S(1)} async-done(((bf16[32,40,1024]{2,1,0:T(8,128)(2,1)}), bf16[32,40,1024]{2,1,0:T(8,128)(2,1)S(1)}, u32[]{:S(2)}, u32[]{:S(2)}) %all-to-all-start.2) | async-done | bytes 2621472 | tf_op jit(solution)/shard_map/all_to_all | solution.py:427
  160.7 0.1 broadcast_in_dim.7
  160.8 0.6 broadcast_in_dim.8
  161.4 8.4 %all-to-all-start.3 = ((f32[32,1,128]{2,1,0:T(1,128)}), f32[32,1,128]{2,1,0:T(1,128)S(1)}, u32[]{:S(2)}, u32[]{:S(2)}) async-start(f32[32,1,128]{2,1,0:T(1,128)} %broadcast_in_dim.8), calls=%async_computation.3 | async-start | bytes 32768 | tf_op jit(solution)/shard_map/all_to_all | solution.py:427
  169.8 0.0 copy-done.1
  169.8 0.0 copy-done.4
  169.9 0.0 copy-start.3
  169.9 1.0 copy-done.3
  170.8 1.3 combine.1
  172.2 4.5 %all-to-all-done.3 = f32[32,1,128]{2,1,0:T(1,128)S(1)} async-done(((f32[32,1,128]{2,1,0:T(1,128)}), f32[32,1,128]{2,1,0:T(1,128)S(1)}, u32[]{:S(2)}, u32[]{:S(2)}) %all-to-all-start.3) | async-done | bytes 16416 | tf_op jit(solution)/shard_map/all_to_all | solution.py:427
  176.7 0.5 broadcast.6
  177.2 0.7 reduce.3
  177.9 0.1 reshape.35
  178.0 0.7 copy.20
  (1 shorter events, 0.0 us)
Async XLA Ops:
  7.2 86.1 %all-gather.2.cloned.1.call-start = ((), (), s32[]{:S(2)}) async-start(), calls=%async_computation.4 | async-start | bytes 5013504 | tf_op jit(solution)/shard_map/all_gather | solution.py:438
  13.9 11.5 %copy-start.8 = (s32[128,8]{0,1:T(8,128)S(1)}, s32[128,8]{0,1:T(8,128)}, u32[]{:S(2)}) copy-start(s32[128,8]{0,1:T(8,128)} %param.10) | copy-start | bytes 12292
  13.9 12.2 %copy-start.9 = (f32[128,8]{0,1:T(8,128)S(1)}, f32[128,8]{0,1:T(8,128)}, u32[]{:S(2)}) copy-start(f32[128,8]{0,1:T(8,128)} %param.11) | copy-start | bytes 12292
  13.9 79.4 %all-to-all-start = ((bf16[32,672,128]{2,1,0:T(8,128)(2,1)}), bf16[32,672,128]{2,1,0:T(8,128)(2,1)}, u32[]{:S(2)}, u32[]{:S(2)}) async-start(bf16[32,672,128]{2,1,0:T(8,128)(2,1)} %dispatch.1), calls=%async_computation | async-start | bytes 11010048 | tf_op jit(solution)/shard_map/all_to_all | solution.py:427
  103.2 18.6 %all-to-all-start.1 = ((bf16[32,32,128]{2,1,0:T(8,128)(2,1)}), bf16[32,32,128]{2,1,0:T(8,128)(2,1)S(1)}, u32[]{:S(2)}, u32[]{:S(2)}) async-start(bf16[32,32,128]{2,1,0:T(8,128)(2,1)} %get-tuple-element.23), calls=%async_computation.1 | async-start | bytes 524288 | tf_op jit(solution)/shard_map/all_to_all | solution.py:427
  119.3 7.6 %copy-start.2 = (bf16[2,2,384,128]{3,2,1,0:T(8,128)(2,1)S(1)}, bf16[2,2,384,128]{3,2,1,0:T(8,128)(2,1)}, u32[]{:S(2)}) copy-start(bf16[2,2,384,128]{3,2,1,0:T(8,128)(2,1)} %get-tuple-element.26.hot_hbm) | copy-start | bytes 1179652
  119.3 7.6 %copy-start.5 = (f32[2,32,128]{2,1,0:T(8,128)S(1)}, f32[2,32,128]{2,1,0:T(8,128)}, u32[]{:S(2)}) copy-start(f32[2,32,128]{2,1,0:T(8,128)} %get-tuple-element.24.gg_ref) | copy-start | bytes 98308
  119.3 7.6 %copy-start.6 = (f32[2,32,128]{2,1,0:T(8,128)S(1)}, f32[2,32,128]{2,1,0:T(8,128)}, u32[]{:S(2)}) copy-start(f32[2,32,128]{2,1,0:T(8,128)} %get-tuple-element.25.gate_ref) | copy-start | bytes 98308
  121.8 48.0 %copy-start.1 = (bf16[1024,64]{0,1:T(8,128)(2,1)S(1)}, bf16[1024,64]{0,1:T(8,128)(2,1)}, u32[]{:S(2)}) copy-start(bf16[1024,64]{0,1:T(8,128)(2,1)} %param.13) | copy-start | bytes 393220
  121.8 48.0 %copy-start.4 = (f32[128,64]{1,0:T(8,128)S(1)}, f32[128,64]{1,0:T(8,128)}, u32[]{:S(2)}) copy-start(f32[128,64]{1,0:T(8,128)} %get-tuple-element.21.dense_ref) | copy-start | bytes 98308
  121.8 38.9 %all-to-all-start.2 = ((bf16[32,40,1024]{2,1,0:T(8,128)(2,1)}), bf16[32,40,1024]{2,1,0:T(8,128)(2,1)S(1)}, u32[]{:S(2)}, u32[]{:S(2)}) async-start(bf16[32,40,1024]{2,1,0:T(8,128)(2,1)} %bitcast.13), calls=%async_computation.2 | async-start | bytes 5242880 | tf_op jit(solution)/shard_map/all_to_all | solution.py:427
  126.9 1.9 %copy-start = (bf16[2,2,384,1024]{3,2,1,0:T(8,128)(2,1)S(1)}, bf16[2,2,384,1024]{3,2,1,0:T(8,128)(2,1)}, u32[]{:S(2)}) copy-start(bf16[2,2,384,1024]{3,2,1,0:T(8,128)(2,1)} %get-tuple-element.27.xe_hbm) | copy-start | bytes 9437188
  130.1 0.6 copy-start.7
  161.4 15.3 %all-to-all-start.3 = ((f32[32,1,128]{2,1,0:T(1,128)}), f32[32,1,128]{2,1,0:T(1,128)S(1)}, u32[]{:S(2)}, u32[]{:S(2)}) async-start(f32[32,1,128]{2,1,0:T(1,128)} %broadcast_in_dim.8), calls=%async_computation.3 | async-start | bytes 32768 | tf_op jit(solution)/shard_map/all_to_all | solution.py:427
  169.9 1.0 copy-start.3
Sparse Core Ops, SparseCore 0:
  10.1 77.5 all-gather.1

commit v7 on v6

--- a/solution.py
+++ b/solution.py
@@ -16,7 +16,7 @@
 ROWS = HOSTS * SLOTS
 TILES = 8
 SPAN = SLOTS * TILES
-BLOCK = 2 * SPAN + 32
+BLOCK = 2 * SPAN + 16
 TOKENS = 128
 
 
@@ -91,12 +91,7 @@
     hot = hot_ref[pl.ds(pl.multiple_of(pl.program_id(0) * rows, rows), rows), :]
     xs = jnp.dot(hot, x_ref[...], preferred_element_type=F32)
     ys = jnp.dot(hot, dy_ref[...], preferred_element_type=F32)
-    left = gates_ref[...]
-    route = [ids_ref[...].astype(F32)]
-    for _ in range(3):
-        high = left.astype(BF).astype(F32)
-        route.append(high)
-        left = left - high
+    route = [ids_ref[...].astype(F32), gates_ref[...]]
     for j in range(hosts):
         at = slice(SLOTS * j, SLOTS * j + SLOTS)
         out_ref[j] = jnp.concatenate(to_tiles(xs[at]) + to_tiles(ys[at]) + route, axis=0).astype(BF)
@@ -177,7 +172,7 @@
         for n, v in ((2 * p, a), (2 * p + 1, b)):
             at = 2 * SPAN
             ids_ref[n] = v[at : at + 8]
-            gates_ref[n] = v[at + 8 : at + 16] + v[at + 16 : at + 24] + v[at + 24 : at + 32]
+            gates_ref[n] = v[at + 8 : at + 16]
     ids, gates = ids_ref[...], gates_ref[...]
     upper = strict(width, width, True)
     host = host_ref[0]
@@ -423,6 +418,35 @@
     )(host, hot, dense, sums, rw_t, rows)
 
 
+def layout_kernel(columns_ref, out_ref):
+    hosts, both = columns_ref.shape
+    part = both // 2
+    turned = columns_ref[...].T
+    row = lax.broadcasted_iota(jnp.int32, (hosts, 2 * hosts), 0)
+    column = lax.broadcasted_iota(jnp.int32, (hosts, 2 * hosts), 1)
+    out = jnp.zeros(out_ref.shape, F32)
+    for e in (0, 1):
+        out = out + jnp.dot(
+            turned[part * e : part * e + part],
+            jnp.where(column == 2 * row + e, 1.0, 0.0),
+            precision=lax.Precision.HIGHEST,
+            preferred_element_type=F32,
+        )
+    out_ref[...] = out
+
+
+def layout(columns):
+    hosts, both = columns.shape
+    return pl.pallas_call(
+        layout_kernel,
+        out_shape=jax.ShapeDtypeStruct((both // 2, 2 * hosts), F32),
+        in_specs=[vmem()],
+        out_specs=vmem(),
+        compiler_params=params(16),
+        name="layout",
+    )(columns)
+
+
 def exchange(rows):
     return lax.all_to_all(rows, "expert", split_axis=0, concat_axis=0, tiled=True)
 
@@ -453,7 +477,7 @@
     column = lax.dynamic_slice_in_dim(column, part * group, part, 1)
     column, back = lax.optimization_barrier((column, back))
     columns = exchange(jnp.broadcast_to(column.reshape(1, -1), (HOSTS, per_host * part)))
-    router_grad = columns.reshape(-1, part).T
+    router_grad = layout(columns)
     token_grad = combine(host_arr, places, dense, sums, rw_t, back)
     return (token_grad, router_grad)
 

time: 186 us -> 183 us (0.984)
  blocking collectives: 27.1 us -> 24.6 us
    unnamed x23 -> x22, local copies, waits for them, and re-layouts: 5.61 us -> 4.92 us
where the time goes in v7:
time: 183 us; the launch traced here: 182 us
  waiting for transfers between devices  74.1 us (40%)
  starting transfers between devices  33.9 us (19%)
  Pallas kernels  27.3 us (15%)
  blocking collectives  24.6 us (13%)
  between operations  14.2 us (8%)
  local copies, waits for them, and re-layouts  8.12 us (4%)
    all_to_all x4, waiting for transfers between devices, exchange(): lax.all_to_all(rows, 'expert', split_axis=0, concat_axis=0, tiled=True)  74.1 us
    all_to_all x4, starting transfers between devices, exchange(): lax.all_to_all(rows, 'expert', split_axis=0, concat_axis=0, tiled=True)  33.9 us
    psum x1, blocking collectives, body(): lax.psum(column, 'dp', axis_index_groups=far).reshape(per_host, model)  15.3 us
    pallas_call x1, Pallas kernels, forward(): pl.pallas_call(forward_kernel, grid=(HALVES,), out_shape=(compact_shape(m...  9.89 us
    psum x1, blocking collectives, body(): column = lax.psum(piece.reshape(-1, 128), 'dp', axis_index_groups=near)  9.32 us
    pallas_call x1, Pallas kernels, backward(): pl.pallas_call(backward_kernel, grid=(HALVES,), out_shape=jax.ShapeDtypeS...  6.45 us
    pallas_call x1, Pallas kernels, dispatch(): pl.pallas_call(dispatch_kernel, grid=(steps,), out_shape=jax.ShapeDtypeSt...  5.04 us
    unnamed x22, local copies, waits for them, and re-layouts  4.92 us
  transfers between devices with their start and end apart: 5, of which 4 were waited for; matrix products, arithmetic and copies ran while one was open for 1% of the time, Pallas kernels for 9%

profile of v7, /device:TPU:1, one launch (start us, length us, event | category | flops | bytes accessed | tf_op | source)
XLA Modules:
  0.0 182.3 jit_solution(11146428864296247485)
XLA Ops:
  7.2 0.0 all-gather.2.cloned.1.call-start
  7.2 1.7 copy.19
  8.9 0.0 all-gather.2.cloned.1.call-update
  8.9 5.0 %dispatch.1 = bf16[32,656,128]{2,1,0:T(8,128)(2,1)} custom-call(s32[8,128]{1,0:T(8,128)} %bitcast.17, f32[8,128]{1,0:T(8,128)} %bitcast.18, bf16[128,1024]{1,0:T(8,128)(2,1)} %x_ref.1, bf16[128,1024]{1,0:T(8,128)(2,1)} %dy_ref.1), custom_call_target="tpu_custom_call" | custom-call | tf_op jit(solution)/shard_map/dispatch/pallas_call | solution.py:119
  14.0 0.0 copy-start.8
  14.0 0.0 copy-start.9
  14.0 11.5 %all-to-all-start = ((bf16[32,656,128]{2,1,0:T(8,128)(2,1)}), bf16[32,656,128]{2,1,0:T(8,128)(2,1)}, u32[]{:S(2)}, u32[]{:S(2)}) async-start(bf16[32,656,128]{2,1,0:T(8,128)(2,1)} %dispatch.1), calls=%async_computation | async-start | bytes 10747904 | tf_op jit(solution)/shard_map/all_to_all | solution.py:451
  25.5 0.0 copy-done.8
  25.5 0.7 copy.16.ids_ref
  26.2 0.0 copy-done.9
  26.2 0.7 copy.17.gates_ref
  27.0 2.4 %lookup.1 = (bf16[128,1280]{1,0:T(8,128)(2,1)}, f32[128,64]{1,0:T(8,128)}) custom-call(s32[128,8]{1,0:T(8,128)} %copy.16.ids_ref, f32[128,8]{1,0:T(8,128)} %copy.17.gates_ref, bf16[64,1280]{1,0:T(8,128)(2,1)} %constant.19.clone.expand_ref, f32[1,1280]{1,0:T(1,128)} %constant.20.clone.rank_ref), custom_call_target="tpu_custom_call" | custom-call | tf_op jit(solution)/shard_map/lookup/pallas_call | solution.py:385
  29.3 62.5 %all-to-all-done.rows_ref = bf16[32,656,128]{2,1,0:T(8,128)(2,1)} async-done(((bf16[32,656,128]{2,1,0:T(8,128)(2,1)}), bf16[32,656,128]{2,1,0:T(8,128)(2,1)}, u32[]{:S(2)}, u32[]{:S(2)}) %all-to-all-start) | async-done | bytes 5373984 | tf_op jit(solution)/shard_map/all_to_all | solution.py:451
  91.8 0.0 all-gather.2.cloned.1.call-done.w_ref
  91.8 9.9 %forward.1 = (bf16[2,2,384,1024]{3,2,1,0:T(8,128)(2,1)}, bf16[2,2,384,128]{3,2,1,0:T(8,128)(2,1)}, bf16[2,2,384,768]{3,2,1,0:T(8,128)(2,1)}, f32[2,2,384,1]{3,2,...) custom-call(s32[1]{0:T(128)} %bitcast.host_ref, ...), custom_call_target="tpu_custom_call" | custom-call | flops 3623878656 | bytes 20000000 | tf_op jit(solution)/shard_map/forward/pallas_call | solution.py:239
  101.7 11.1 %all-to-all-start.1 = ((bf16[32,32,128]{2,1,0:T(8,128)(2,1)}), bf16[32,32,128]{2,1,0:T(8,128)(2,1)S(1)}, u32[]{:S(2)}, u32[]{:S(2)}) async-start(bf16[32,32,128]{2,1,0:T(8,128)(2,1)} %get-tuple-element.23), calls=%async_computation.1 | async-start | bytes 524288 | tf_op jit(solution)/shard_map/all_to_all | solution.py:451
  112.8 6.4 %backward.1 = bf16[1280,1024]{1,0:T(8,128)(2,1)} custom-call(s32[1]{0:T(128)} %bitcast.host_ref, bf16[2,2,384,768]{3,2,1,0:T(8,128)(2,1)} %get-tuple-element.30.gu_ref, f32[2,2,384,1]{3,2,1,0:T(8,128)} %get-tuple-element.31.add_ref, bf16[64,1024]{1,0:T(8,128)(2,1)} %bitcast.11, bf16[2,1024,1152]{2,1,0:T(8,128)(2,1)} %all-gather.2.cloned.1.call-done.w_ref), custom_call_target="tpu_custom_call" | custom-call | flops 2415919104 | bytes 10000000 | tf_op jit(solution)/shard_map/backward/pallas_call | solution.py:294
  119.3 0.0 copy-start.2
  119.3 0.0 copy-start.5
  119.3 0.0 copy-start.6
  119.3 2.5 %all-to-all-done.1.shares_ref = bf16[32,32,128]{2,1,0:T(8,128)(2,1)S(1)} async-done(((bf16[32,32,128]{2,1,0:T(8,128)(2,1)}), bf16[32,32,128]{2,1,0:T(8,128)(2,1)S(1)}, u32[]{:S(2)}, u32[]{:S(2)}) %all-to-all-start.1) | async-done | bytes 262176 | tf_op jit(solution)/shard_map/all_to_all | solution.py:451
  121.8 0.0 copy-start.1
  121.8 0.0 copy-start.4
  121.8 5.0 %all-to-all-start.2 = ((bf16[32,40,1024]{2,1,0:T(8,128)(2,1)}), bf16[32,40,1024]{2,1,0:T(8,128)(2,1)S(1)}, u32[]{:S(2)}, u32[]{:S(2)}) async-start(bf16[32,40,1024]{2,1,0:T(8,128)(2,1)} %bitcast.14), calls=%async_computation.2 | async-start | bytes 5242880 | tf_op jit(solution)/shard_map/all_to_all | solution.py:451
  126.8 0.0 copy-done.2
  126.9 0.0 copy-done.5
  126.9 0.0 copy-done.6
  126.9 0.0 copy-start
  126.9 1.9 %copy-done = bf16[2,2,384,1024]{3,2,1,0:T(8,128)(2,1)S(1)} copy-done((bf16[2,2,384,1024]{3,2,1,0:T(8,128)(2,1)S(1)}, bf16[2,2,384,1024]{3,2,1,0:T(8,128)(2,1)}, u32[]{:S(2)}) %copy-start) | copy-done | bytes 3145752
  128.8 1.3 router_part.1
  130.1 0.0 copy-start.7
  130.1 0.6 copy-done.7
  130.7 0.7 reshape.29
  131.4 9.3 %psum.14 = f32[16,128]{1,0:T(8,128)S(1)} all-reduce(f32[16,128]{1,0:T(8,128)S(1)} %reshape.29), channel_id=1, replica_groups={{0,32,64,96},{128,160,192,224},{256,288,320,352},{384,416,448,480},{1,3..., use_global_device_ids=true, to_apply=%region_0.0 | all-reduce | flops 2048 | bytes 16384 | tf_op jit(solution)/shard_map/psum | solution.py:475
  140.7 15.3 %psum.15 = f32[2,1024]{1,0:T(2,128)S(1)} all-reduce(f32[2,1024]{1,0:T(2,128)S(1)} %reshape.30), channel_id=1, replica_groups={{0,128,256,384},{32,160,288,416},{64,192,320,448},{96,224,352,480},{1,1..., use_global_device_ids=true, to_apply=%region_1.0 | all-reduce | flops 2048 | bytes 16384 | tf_op jit(solution)/shard_map/psum | solution.py:476
  156.1 0.1 constant_dynamic-slice_fusion
  156.2 4.6 %all-to-all-done.2 = bf16[32,40,1024]{2,1,0:T(8,128)(2,1)S(1)} async-done(((bf16[32,40,1024]{2,1,0:T(8,128)(2,1)}), bf16[32,40,1024]{2,1,0:T(8,128)(2,1)S(1)}, u32[]{:S(2)}, u32[]{:S(2)}) %all-to-all-start.2) | async-done | bytes 2621472 | tf_op jit(solution)/shard_map/all_to_all | solution.py:451
  160.7 0.1 broadcast_in_dim.7
  160.8 0.6 broadcast_in_dim.8
  161.4 6.3 %all-to-all-start.3 = ((f32[32,1,128]{2,1,0:T(1,128)}), f32[32,1,128]{2,1,0:T(1,128)S(1)}, u32[]{:S(2)}, u32[]{:S(2)}) async-start(f32[32,1,128]{2,1,0:T(1,128)} %broadcast_in_dim.8), calls=%async_computation.3 | async-start | bytes 32768 | tf_op jit(solution)/shard_map/all_to_all | solution.py:451
  167.7 0.0 copy-done.1
  167.7 0.0 copy-done.4
  167.7 0.0 copy-start.3
  167.7 1.0 copy-done.3
  168.7 1.3 combine.1
  170.0 4.5 %all-to-all-done.3 = f32[32,1,128]{2,1,0:T(1,128)S(1)} async-done(((f32[32,1,128]{2,1,0:T(1,128)}), f32[32,1,128]{2,1,0:T(1,128)S(1)}, u32[]{:S(2)}, u32[]{:S(2)}) %all-to-all-start.3) | async-done | bytes 16416 | tf_op jit(solution)/shard_map/all_to_all | solution.py:451
  174.6 0.9 layout.1
  (1 shorter events, 0.0 us)
Async XLA Ops:
  7.2 84.6 %all-gather.2.cloned.1.call-start = ((), (), s32[]{:S(2)}) async-start(), calls=%async_computation.4 | async-start | bytes 5013504 | tf_op jit(solution)/shard_map/all_gather | solution.py:462
  14.0 11.5 %copy-start.8 = (s32[128,8]{0,1:T(8,128)S(1)}, s32[128,8]{0,1:T(8,128)}, u32[]{:S(2)}) copy-start(s32[128,8]{0,1:T(8,128)} %param.10) | copy-start | bytes 12292
  14.0 12.3 %copy-start.9 = (f32[128,8]{0,1:T(8,128)S(1)}, f32[128,8]{0,1:T(8,128)}, u32[]{:S(2)}) copy-start(f32[128,8]{0,1:T(8,128)} %param.11) | copy-start | bytes 12292
  14.0 77.8 %all-to-all-start = ((bf16[32,656,128]{2,1,0:T(8,128)(2,1)}), bf16[32,656,128]{2,1,0:T(8,128)(2,1)}, u32[]{:S(2)}, u32[]{:S(2)}) async-start(bf16[32,656,128]{2,1,0:T(8,128)(2,1)} %dispatch.1), calls=%async_computation | async-start | bytes 10747904 | tf_op jit(solution)/shard_map/all_to_all | solution.py:451
  101.7 20.1 %all-to-all-start.1 = ((bf16[32,32,128]{2,1,0:T(8,128)(2,1)}), bf16[32,32,128]{2,1,0:T(8,128)(2,1)S(1)}, u32[]{:S(2)}, u32[]{:S(2)}) async-start(bf16[32,32,128]{2,1,0:T(8,128)(2,1)} %get-tuple-element.23), calls=%async_computation.1 | async-start | bytes 524288 | tf_op jit(solution)/shard_map/all_to_all | solution.py:451
  119.3 7.6 %copy-start.2 = (bf16[2,2,384,128]{3,2,1,0:T(8,128)(2,1)S(1)}, bf16[2,2,384,128]{3,2,1,0:T(8,128)(2,1)}, u32[]{:S(2)}) copy-start(bf16[2,2,384,128]{3,2,1,0:T(8,128)(2,1)} %get-tuple-element.26.hot_hbm) | copy-start | bytes 1179652
  119.3 7.6 %copy-start.5 = (f32[2,32,128]{2,1,0:T(8,128)S(1)}, f32[2,32,128]{2,1,0:T(8,128)}, u32[]{:S(2)}) copy-start(f32[2,32,128]{2,1,0:T(8,128)} %get-tuple-element.24.gg_ref) | copy-start | bytes 98308
  119.3 7.6 %copy-start.6 = (f32[2,32,128]{2,1,0:T(8,128)S(1)}, f32[2,32,128]{2,1,0:T(8,128)}, u32[]{:S(2)}) copy-start(f32[2,32,128]{2,1,0:T(8,128)} %get-tuple-element.25.gate_ref) | copy-start | bytes 98308
  121.8 45.9 %copy-start.1 = (bf16[1024,64]{0,1:T(8,128)(2,1)S(1)}, bf16[1024,64]{0,1:T(8,128)(2,1)}, u32[]{:S(2)}) copy-start(bf16[1024,64]{0,1:T(8,128)(2,1)} %param.13) | copy-start | bytes 393220
  121.8 45.9 %copy-start.4 = (f32[128,64]{1,0:T(8,128)S(1)}, f32[128,64]{1,0:T(8,128)}, u32[]{:S(2)}) copy-start(f32[128,64]{1,0:T(8,128)} %get-tuple-element.21.dense_ref) | copy-start | bytes 98308
  121.8 38.9 %all-to-all-start.2 = ((bf16[32,40,1024]{2,1,0:T(8,128)(2,1)}), bf16[32,40,1024]{2,1,0:T(8,128)(2,1)S(1)}, u32[]{:S(2)}, u32[]{:S(2)}) async-start(bf16[32,40,1024]{2,1,0:T(8,128)(2,1)} %bitcast.14), calls=%async_computation.2 | async-start | bytes 5242880 | tf_op jit(solution)/shard_map/all_to_all | solution.py:451
  126.9 1.9 %copy-start = (bf16[2,2,384,1024]{3,2,1,0:T(8,128)(2,1)S(1)}, bf16[2,2,384,1024]{3,2,1,0:T(8,128)(2,1)}, u32[]{:S(2)}) copy-start(bf16[2,2,384,1024]{3,2,1,0:T(8,128)(2,1)} %get-tuple-element.27.xe_hbm) | copy-start | bytes 9437188
  130.1 0.6 copy-start.7
  161.4 13.1 %all-to-all-start.3 = ((f32[32,1,128]{2,1,0:T(1,128)}), f32[32,1,128]{2,1,0:T(1,128)S(1)}, u32[]{:S(2)}, u32[]{:S(2)}) async-start(f32[32,1,128]{2,1,0:T(1,128)} %broadcast_in_dim.8), calls=%async_computation.3 | async-start | bytes 32768 | tf_op jit(solution)/shard_map/all_to_all | solution.py:451
  167.7 1.0 copy-start.3
Sparse Core Ops, SparseCore 0:
  10.1 77.4 all-gather.1

commit v8 on v7

--- a/solution.py
+++ b/solution.py
@@ -266,42 +266,61 @@
     )(host, blocks, weights)
 
 
-def backward_kernel(host_ref, gu_ref, add_ref, rw_ref, w_ref, out_ref, re_ref):
+def backward_kernel(host_ref, gu_ref, add_ref, rw_ref, w_ref, out_hbm, re_ref, out_ref, sems):
+    expert = pl.program_id(0)
     experts = rw_ref.shape[0]
-    mine = lax.broadcasted_iota(jnp.int32, (8, experts), 0) + 2 * host_ref[0]
+    mine = 2 * host_ref[0] + expert
     pick = jnp.where(lax.broadcasted_iota(jnp.int32, (8, experts), 1) == mine, 1.0, 0.0)
     router = jnp.dot(pick.astype(BF), rw_ref[...], preferred_element_type=F32)
-    for e in (0, 1):
-        row = lax.dot_general(
-            gu_ref[0, e], w_ref[e], (((1,), (1,)), ((), ())), preferred_element_type=F32
-        )
-        re_ref[e] = (row + add_ref[0, e] * router[e : e + 1]).astype(BF)
-    for p in range(COMPACT // 48):
-        r0 = re_ref[0, 48 * p : 48 * p + 48, :].astype(F32)
-        r1 = re_ref[1, 48 * p : 48 * p + 48, :].astype(F32)
-        out_ref[80 * p : 80 * p + 80, :] = jnp.concatenate(
-            [
-                r0[0:16], r1[0:16], r0[32:40] + r1[32:40],
-                r0[16:32], r1[16:32], r0[40:48] + r1[40:48],
-            ],
-            axis=0,
-        ).astype(BF)
+    row = lax.dot_general(
+        jnp.concatenate([gu_ref[0, 0], gu_ref[1, 0]], axis=0), w_ref[0],
+        (((1,), (1,)), ((), ())), preferred_element_type=F32,
+    )
+    add = jnp.concatenate([add_ref[0, 0], add_ref[1, 0]], axis=0)
+    re_ref[expert] = (row + add * router[0:1]).astype(BF)
+
+    @pl.when(expert == 1)
+    def _():
+        chunks = sems.shape[0]
+        pairs = HOSTS // 2 // chunks
+        copies = []
+        for c in range(chunks):
+            for p in range(pairs * c, pairs * c + pairs):
+                r0 = re_ref[0, 48 * p : 48 * p + 48, :].astype(F32)
+                r1 = re_ref[1, 48 * p : 48 * p + 48, :].astype(F32)
+                out_ref[80 * p : 80 * p + 80, :] = jnp.concatenate(
+                    [
+                        r0[0:16], r1[0:16], r0[32:40] + r1[32:40],
+                        r0[16:32], r1[16:32], r0[40:48] + r1[40:48],
+                    ],
+                    axis=0,
+                ).astype(BF)
+            at = pl.ds(80 * pairs * c, 80 * pairs)
+            copies.append(pltpu.make_async_copy(out_ref.at[at], out_hbm.at[at], sems.at[c]))
+            copies[c].start()
+        for copy in copies:
+            copy.wait()
 
 
 def backward(host, gu, add, rw_t, weights):
     double = gu.shape[3]
     model = weights.shape[1]
+    one = lambda last: pl.BlockSpec((HALVES, 1, COMPACT, last), lambda e: (0, e, 0, 0))
     return pl.pallas_call(
         backward_kernel,
-        grid=(HALVES,),
+        grid=(2,),
         out_shape=jax.ShapeDtypeStruct((ROWS, model), BF),
         in_specs=[
-            smem(), compact_spec(double), compact_spec(1),
-            pl.BlockSpec(rw_t.shape, lambda i: (0, 0)),
-            pl.BlockSpec((2, model, double), lambda i: (0, 0, 0)),
+            smem(), one(double), one(1),
+            pl.BlockSpec(rw_t.shape, lambda e: (0, 0)),
+            pl.BlockSpec((1, model, double), lambda e: (e, 0, 0)),
         ],
-        out_specs=pl.BlockSpec((ROWS // HALVES, model), lambda i: (i, 0)),
-        scratch_shapes=[pltpu.VMEM((2, COMPACT, model), BF)],
+        out_specs=pl.BlockSpec(memory_space=pl.ANY),
+        scratch_shapes=[
+            pltpu.VMEM((2, HALVES * COMPACT, model), BF),
+            pltpu.VMEM((ROWS, model), BF),
+            pltpu.SemaphoreType.DMA((4,)),
+        ],
         compiler_params=params(56),
         cost_estimate=cost(4 * HALVES * COMPACT * model * double, 10_000_000),
         name="backward",

time: 183 us -> 183 us (level)
  no operation moved by 1% of the time
where the time goes in v8:
time: 183 us; the launch traced here: 182 us
  waiting for transfers between devices  73.8 us (40%)
  starting transfers between devices  33.9 us (19%)
  Pallas kernels  27.2 us (15%)
  blocking collectives  25 us (14%)
  between operations  14.2 us (8%)
  local copies, waits for them, and re-layouts  8.13 us (4%)
    all_to_all x4, waiting for transfers between devices, exchange(): lax.all_to_all(rows, 'expert', split_axis=0, concat_axis=0, tiled=True)  73.8 us
    all_to_all x4, starting transfers between devices, exchange(): lax.all_to_all(rows, 'expert', split_axis=0, concat_axis=0, tiled=True)  33.9 us
    psum x1, blocking collectives, body(): lax.psum(column, 'dp', axis_index_groups=far).reshape(per_host, model)  15.6 us
    pallas_call x1, Pallas kernels, forward(): pl.pallas_call(forward_kernel, grid=(HALVES,), out_shape=(compact_shape(m...  9.89 us
    psum x1, blocking collectives, body(): column = lax.psum(piece.reshape(-1, 128), 'dp', axis_index_groups=near)  9.34 us
    pallas_call x1, Pallas kernels, backward(): pl.pallas_call(backward_kernel, grid=(2,), out_shape=jax.ShapeDtypeStruct...  6.41 us
    pallas_call x1, Pallas kernels, dispatch(): pl.pallas_call(dispatch_kernel, grid=(steps,), out_shape=jax.ShapeDtypeSt...  5.04 us
    unnamed x22, local copies, waits for them, and re-layouts  4.93 us
  transfers between devices with their start and end apart: 5, of which 4 were waited for; matrix products, arithmetic and copies ran while one was open for 1% of the time, Pallas kernels for 9%

profile of v8, /device:TPU:1, one launch (start us, length us, event | category | flops | bytes accessed | tf_op | source)
XLA Modules:
  0.0 182.3 jit_solution(16616243981962456553)
XLA Ops:
  7.2 0.0 all-gather.2.cloned.1.call-start
  7.2 1.7 copy.19
  8.9 0.0 all-gather.2.cloned.1.call-update
  8.9 5.0 %dispatch.1 = bf16[32,656,128]{2,1,0:T(8,128)(2,1)} custom-call(s32[8,128]{1,0:T(8,128)} %bitcast.17, f32[8,128]{1,0:T(8,128)} %bitcast.18, bf16[128,1024]{1,0:T(8,128)(2,1)} %x_ref.1, bf16[128,1024]{1,0:T(8,128)(2,1)} %dy_ref.1), custom_call_target="tpu_custom_call" | custom-call | tf_op jit(solution)/shard_map/dispatch/pallas_call | solution.py:119
  14.0 0.0 copy-start.8
  14.0 0.0 copy-start.9
  14.0 11.5 %all-to-all-start = ((bf16[32,656,128]{2,1,0:T(8,128)(2,1)}), bf16[32,656,128]{2,1,0:T(8,128)(2,1)}, u32[]{:S(2)}, u32[]{:S(2)}) async-start(bf16[32,656,128]{2,1,0:T(8,128)(2,1)} %dispatch.1), calls=%async_computation | async-start | bytes 10747904 | tf_op jit(solution)/shard_map/all_to_all | solution.py:470
  25.5 0.0 copy-done.8
  25.5 0.7 copy.16.ids_ref
  26.2 0.0 copy-done.9
  26.2 0.7 copy.17.gates_ref
  27.0 2.4 %lookup.1 = (bf16[128,1280]{1,0:T(8,128)(2,1)}, f32[128,64]{1,0:T(8,128)}) custom-call(s32[128,8]{1,0:T(8,128)} %copy.16.ids_ref, f32[128,8]{1,0:T(8,128)} %copy.17.gates_ref, bf16[64,1280]{1,0:T(8,128)(2,1)} %constant.19.clone.expand_ref, f32[1,1280]{1,0:T(1,128)} %constant.20.clone.rank_ref), custom_call_target="tpu_custom_call" | custom-call | tf_op jit(solution)/shard_map/lookup/pallas_call | solution.py:404
  29.3 62.5 %all-to-all-done.rows_ref = bf16[32,656,128]{2,1,0:T(8,128)(2,1)} async-done(((bf16[32,656,128]{2,1,0:T(8,128)(2,1)}), bf16[32,656,128]{2,1,0:T(8,128)(2,1)}, u32[]{:S(2)}, u32[]{:S(2)}) %all-to-all-start) | async-done | bytes 5373984 | tf_op jit(solution)/shard_map/all_to_all | solution.py:470
  91.8 0.0 all-gather.2.cloned.1.call-done.w_ref
  91.8 9.9 %forward.1 = (bf16[2,2,384,1024]{3,2,1,0:T(8,128)(2,1)}, bf16[2,2,384,128]{3,2,1,0:T(8,128)(2,1)}, bf16[2,2,384,768]{3,2,1,0:T(8,128)(2,1)}, f32[2,2,384,1]{3,2,...) custom-call(s32[1]{0:T(128)} %bitcast.host_ref, ...), custom_call_target="tpu_custom_call" | custom-call | flops 3623878656 | bytes 20000000 | tf_op jit(solution)/shard_map/forward/pallas_call | solution.py:239
  101.7 11.1 %all-to-all-start.1 = ((bf16[32,32,128]{2,1,0:T(8,128)(2,1)}), bf16[32,32,128]{2,1,0:T(8,128)(2,1)S(1)}, u32[]{:S(2)}, u32[]{:S(2)}) async-start(bf16[32,32,128]{2,1,0:T(8,128)(2,1)} %get-tuple-element.23), calls=%async_computation.1 | async-start | bytes 524288 | tf_op jit(solution)/shard_map/all_to_all | solution.py:470
  112.8 6.4 %backward.1 = bf16[1280,1024]{1,0:T(8,128)(2,1)} custom-call(s32[1]{0:T(128)} %bitcast.host_ref, bf16[2,2,384,768]{3,2,1,0:T(8,128)(2,1)} %get-tuple-element.30.gu_ref, f32[2,2,384,1]{3,2,1,0:T(8,128)} %get-tuple-element.31.add_ref, bf16[64,1024]{1,0:T(8,128)(2,1)} %bitcast.11, bf16[2,1024,1152]{2,1,0:T(8,128)(2,1)} %all-gather.2.cloned.1.call-done.w_ref), custom_call_target="tpu_custom_call" | custom-call | flops 2415919104 | bytes 10000000 | tf_op jit(solution)/shard_map/backward/pallas_call | solution.py:309
  119.2 0.0 copy-start.2
  119.2 0.0 copy-start.5
  119.2 0.0 copy-start.6
  119.3 2.5 %all-to-all-done.1.shares_ref = bf16[32,32,128]{2,1,0:T(8,128)(2,1)S(1)} async-done(((bf16[32,32,128]{2,1,0:T(8,128)(2,1)}), bf16[32,32,128]{2,1,0:T(8,128)(2,1)S(1)}, u32[]{:S(2)}, u32[]{:S(2)}) %all-to-all-start.1) | async-done | bytes 262176 | tf_op jit(solution)/shard_map/all_to_all | solution.py:470
  121.8 0.0 copy-start.1
  121.8 0.0 copy-start.4
  121.8 5.0 %all-to-all-start.2 = ((bf16[32,40,1024]{2,1,0:T(8,128)(2,1)}), bf16[32,40,1024]{2,1,0:T(8,128)(2,1)S(1)}, u32[]{:S(2)}, u32[]{:S(2)}) async-start(bf16[32,40,1024]{2,1,0:T(8,128)(2,1)} %bitcast.14), calls=%async_computation.2 | async-start | bytes 5242880 | tf_op jit(solution)/shard_map/all_to_all | solution.py:470
  126.8 0.0 copy-done.2
  126.8 0.0 copy-done.5
  126.8 0.0 copy-done.6
  126.8 0.0 copy-start
  126.9 1.9 %copy-done = bf16[2,2,384,1024]{3,2,1,0:T(8,128)(2,1)S(1)} copy-done((bf16[2,2,384,1024]{3,2,1,0:T(8,128)(2,1)S(1)}, bf16[2,2,384,1024]{3,2,1,0:T(8,128)(2,1)}, u32[]{:S(2)}) %copy-start) | copy-done | bytes 3145752
  128.7 1.3 router_part.1
  130.1 0.0 copy-start.7
  130.1 0.6 copy-done.7
  130.7 0.7 reshape.29
  131.4 9.3 %psum.14 = f32[16,128]{1,0:T(8,128)S(1)} all-reduce(f32[16,128]{1,0:T(8,128)S(1)} %reshape.29), channel_id=1, replica_groups={{0,32,64,96},{128,160,192,224},{256,288,320,352},{384,416,448,480},{1,3..., use_global_device_ids=true, to_apply=%region_0.0 | all-reduce | flops 2048 | bytes 16384 | tf_op jit(solution)/shard_map/psum | solution.py:494
  140.7 15.6 %psum.15 = f32[2,1024]{1,0:T(2,128)S(1)} all-reduce(f32[2,1024]{1,0:T(2,128)S(1)} %reshape.30), channel_id=1, replica_groups={{0,128,256,384},{32,160,288,416},{64,192,320,448},{96,224,352,480},{1,1..., use_global_device_ids=true, to_apply=%region_1.0 | all-reduce | flops 2048 | bytes 16384 | tf_op jit(solution)/shard_map/psum | solution.py:495
  156.4 0.1 constant_dynamic-slice_fusion
  156.4 4.3 %all-to-all-done.2 = bf16[32,40,1024]{2,1,0:T(8,128)(2,1)S(1)} async-done(((bf16[32,40,1024]{2,1,0:T(8,128)(2,1)}), bf16[32,40,1024]{2,1,0:T(8,128)(2,1)S(1)}, u32[]{:S(2)}, u32[]{:S(2)}) %all-to-all-start.2) | async-done | bytes 2621472 | tf_op jit(solution)/shard_map/all_to_all | solution.py:470
  160.7 0.1 broadcast_in_dim.7
  160.8 0.6 broadcast_in_dim.8
  161.4 6.3 %all-to-all-start.3 = ((f32[32,1,128]{2,1,0:T(1,128)}), f32[32,1,128]{2,1,0:T(1,128)S(1)}, u32[]{:S(2)}, u32[]{:S(2)}) async-start(f32[32,1,128]{2,1,0:T(1,128)} %broadcast_in_dim.8), calls=%async_computation.3 | async-start | bytes 32768 | tf_op jit(solution)/shard_map/all_to_all | solution.py:470
  167.7 0.0 copy-done.1
  167.7 0.0 copy-done.4
  167.7 0.0 copy-start.3
  167.7 1.0 copy-done.3
  168.7 1.3 combine.1
  170.0 4.5 %all-to-all-done.3 = f32[32,1,128]{2,1,0:T(1,128)S(1)} async-done(((f32[32,1,128]{2,1,0:T(1,128)}), f32[32,1,128]{2,1,0:T(1,128)S(1)}, u32[]{:S(2)}, u32[]{:S(2)}) %all-to-all-start.3) | async-done | bytes 16416 | tf_op jit(solution)/shard_map/all_to_all | solution.py:470
  174.6 0.9 layout.1
  (1 shorter events, 0.0 us)
Async XLA Ops:
  7.2 84.6 %all-gather.2.cloned.1.call-start = ((), (), s32[]{:S(2)}) async-start(), calls=%async_computation.4 | async-start | bytes 5013504 | tf_op jit(solution)/shard_map/all_gather | solution.py:481
  14.0 11.5 %copy-start.8 = (s32[128,8]{0,1:T(8,128)S(1)}, s32[128,8]{0,1:T(8,128)}, u32[]{:S(2)}) copy-start(s32[128,8]{0,1:T(8,128)} %param.10) | copy-start | bytes 12292
  14.0 12.3 %copy-start.9 = (f32[128,8]{0,1:T(8,128)S(1)}, f32[128,8]{0,1:T(8,128)}, u32[]{:S(2)}) copy-start(f32[128,8]{0,1:T(8,128)} %param.11) | copy-start | bytes 12292
  14.0 77.8 %all-to-all-start = ((bf16[32,656,128]{2,1,0:T(8,128)(2,1)}), bf16[32,656,128]{2,1,0:T(8,128)(2,1)}, u32[]{:S(2)}, u32[]{:S(2)}) async-start(bf16[32,656,128]{2,1,0:T(8,128)(2,1)} %dispatch.1), calls=%async_computation | async-start | bytes 10747904 | tf_op jit(solution)/shard_map/all_to_all | solution.py:470
  101.7 20.1 %all-to-all-start.1 = ((bf16[32,32,128]{2,1,0:T(8,128)(2,1)}), bf16[32,32,128]{2,1,0:T(8,128)(2,1)S(1)}, u32[]{:S(2)}, u32[]{:S(2)}) async-start(bf16[32,32,128]{2,1,0:T(8,128)(2,1)} %get-tuple-element.23), calls=%async_computation.1 | async-start | bytes 524288 | tf_op jit(solution)/shard_map/all_to_all | solution.py:470
  119.2 7.6 %copy-start.2 = (bf16[2,2,384,128]{3,2,1,0:T(8,128)(2,1)S(1)}, bf16[2,2,384,128]{3,2,1,0:T(8,128)(2,1)}, u32[]{:S(2)}) copy-start(bf16[2,2,384,128]{3,2,1,0:T(8,128)(2,1)} %get-tuple-element.26.hot_hbm) | copy-start | bytes 1179652
  119.2 7.6 %copy-start.5 = (f32[2,32,128]{2,1,0:T(8,128)S(1)}, f32[2,32,128]{2,1,0:T(8,128)}, u32[]{:S(2)}) copy-start(f32[2,32,128]{2,1,0:T(8,128)} %get-tuple-element.24.gg_ref) | copy-start | bytes 98308
  119.2 7.6 %copy-start.6 = (f32[2,32,128]{2,1,0:T(8,128)S(1)}, f32[2,32,128]{2,1,0:T(8,128)}, u32[]{:S(2)}) copy-start(f32[2,32,128]{2,1,0:T(8,128)} %get-tuple-element.25.gate_ref) | copy-start | bytes 98308
  121.8 45.9 %copy-start.1 = (bf16[1024,64]{0,1:T(8,128)(2,1)S(1)}, bf16[1024,64]{0,1:T(8,128)(2,1)}, u32[]{:S(2)}) copy-start(bf16[1024,64]{0,1:T(8,128)(2,1)} %param.13) | copy-start | bytes 393220
  121.8 45.9 %copy-start.4 = (f32[128,64]{1,0:T(8,128)S(1)}, f32[128,64]{1,0:T(8,128)}, u32[]{:S(2)}) copy-start(f32[128,64]{1,0:T(8,128)} %get-tuple-element.21.dense_ref) | copy-start | bytes 98308
  121.8 38.9 %all-to-all-start.2 = ((bf16[32,40,1024]{2,1,0:T(8,128)(2,1)}), bf16[32,40,1024]{2,1,0:T(8,128)(2,1)S(1)}, u32[]{:S(2)}, u32[]{:S(2)}) async-start(bf16[32,40,1024]{2,1,0:T(8,128)(2,1)} %bitcast.14), calls=%async_computation.2 | async-start | bytes 5242880 | tf_op jit(solution)/shard_map/all_to_all | solution.py:470
  126.8 1.9 %copy-start = (bf16[2,2,384,1024]{3,2,1,0:T(8,128)(2,1)S(1)}, bf16[2,2,384,1024]{3,2,1,0:T(8,128)(2,1)}, u32[]{:S(2)}) copy-start(bf16[2,2,384,1024]{3,2,1,0:T(8,128)(2,1)} %get-tuple-element.27.xe_hbm) | copy-start | bytes 9437188
  130.1 0.6 copy-start.7
  161.4 13.2 %all-to-all-start.3 = ((f32[32,1,128]{2,1,0:T(1,128)}), f32[32,1,128]{2,1,0:T(1,128)S(1)}, u32[]{:S(2)}, u32[]{:S(2)}) async-start(f32[32,1,128]{2,1,0:T(1,128)} %broadcast_in_dim.8), calls=%async_computation.3 | async-start | bytes 32768 | tf_op jit(solution)/shard_map/all_to_all | solution.py:470
  167.7 1.0 copy-start.3
Sparse Core Ops, SparseCore 0:
  10.1 77.4 all-gather.1

commit v9 on v7

--- a/solution.py
+++ b/solution.py
@@ -452,7 +452,6 @@
 
 
 def body(tokens, upstream, expert_ids, gates, expert_weights, router_weight):
-    model = tokens.shape[1]
     per_host, _, part, ff = expert_weights.shape
     host = lax.axis_index("expert").astype(jnp.int32)
     group = lax.axis_index("dp").astype(jnp.int32)
@@ -472,11 +471,12 @@
     side = math.isqrt(lax.axis_size("dp"))
     near = [[side * h + l for l in range(side)] for h in range(side)]
     far = [[side * h + l for h in range(side)] for l in range(side)]
-    column = lax.psum(piece.reshape(-1, 128), "dp", axis_index_groups=near)
-    column = lax.psum(column, "dp", axis_index_groups=far).reshape(per_host, model)
+    column = lax.psum(piece, "dp", axis_index_groups=near)
+    column = lax.psum(column, "dp", axis_index_groups=far)
     column = lax.dynamic_slice_in_dim(column, part * group, part, 1)
-    column, back = lax.optimization_barrier((column, back))
-    columns = exchange(jnp.broadcast_to(column.reshape(1, -1), (HOSTS, per_host * part)))
+    spread = jnp.broadcast_to(column.reshape(1, 1, -1), (HOSTS, 1, per_host * part))
+    spread, back = lax.optimization_barrier((spread, back))
+    columns = exchange(spread).reshape(HOSTS, per_host * part)
     router_grad = layout(columns)
     token_grad = combine(host_arr, places, dense, sums, rw_t, back)
     return (token_grad, router_grad)

time: 183 us -> 182 us (level)
  no operation moved by 1% of the time
where the time goes in v9:
time: 182 us
  waiting for transfers between devices  74.4 us (41%)
  starting transfers between devices  33.4 us (18%)
  Pallas kernels  27.3 us (15%)
  blocking collectives  25.1 us (14%)
  between operations  14.2 us (8%)
  local copies, waits for them, and re-layouts  7.41 us (4%)
    all_to_all x4, waiting for transfers between devices, exchange(): lax.all_to_all(rows, 'expert', split_axis=0, concat_axis=0, tiled=True)  74.3 us
    all_to_all x4, starting transfers between devices, exchange(): lax.all_to_all(rows, 'expert', split_axis=0, concat_axis=0, tiled=True)  33.4 us
    psum x1, blocking collectives, body(): column = lax.psum(column, 'dp', axis_index_groups=far)  15.6 us
    pallas_call x1, Pallas kernels, forward(): pl.pallas_call(forward_kernel, grid=(HALVES,), out_shape=(compact_shape(m...  9.89 us
    psum x1, blocking collectives, body(): column = lax.psum(piece, 'dp', axis_index_groups=near)  9.44 us
    pallas_call x1, Pallas kernels, backward(): pl.pallas_call(backward_kernel, grid=(HALVES,), out_shape=jax.ShapeDtypeS...  6.45 us
    pallas_call x1, Pallas kernels, dispatch(): pl.pallas_call(dispatch_kernel, grid=(steps,), out_shape=jax.ShapeDtypeSt...  5.04 us
    unnamed x22, local copies, waits for them, and re-layouts  4.92 us
  transfers between devices with their start and end apart: 5, of which 4 were waited for; matrix products, arithmetic and copies ran while one was open for 1% of the time, Pallas kernels for 9%

profile of v9, /device:TPU:1, one launch (start us, length us, event | category | flops | bytes accessed | tf_op | source)
XLA Modules:
  0.0 181.7 jit_solution(751781461642093131)
XLA Ops:
  7.2 0.0 all-gather.2.cloned.1.call-start
  7.2 1.7 copy.19
  8.9 0.0 all-gather.2.cloned.1.call-update
  8.9 5.0 %dispatch.1 = bf16[32,656,128]{2,1,0:T(8,128)(2,1)} custom-call(s32[8,128]{1,0:T(8,128)} %bitcast.17, f32[8,128]{1,0:T(8,128)} %bitcast.18, bf16[128,1024]{1,0:T(8,128)(2,1)} %x_ref.1, bf16[128,1024]{1,0:T(8,128)(2,1)} %dy_ref.1), custom_call_target="tpu_custom_call" | custom-call | tf_op jit(solution)/shard_map/dispatch/pallas_call | solution.py:119
  14.0 0.0 copy-start.8
  14.0 0.0 copy-start.9
  14.0 11.5 %all-to-all-start = ((bf16[32,656,128]{2,1,0:T(8,128)(2,1)}), bf16[32,656,128]{2,1,0:T(8,128)(2,1)}, u32[]{:S(2)}, u32[]{:S(2)}) async-start(bf16[32,656,128]{2,1,0:T(8,128)(2,1)} %dispatch.1), calls=%async_computation | async-start | bytes 10747904 | tf_op jit(solution)/shard_map/all_to_all | solution.py:451
  25.5 0.0 copy-done.8
  25.5 0.7 copy.16.ids_ref
  26.2 0.0 copy-done.9
  26.2 0.7 copy.17.gates_ref
  27.0 2.4 %lookup.1 = (bf16[128,1280]{1,0:T(8,128)(2,1)}, f32[128,64]{1,0:T(8,128)}) custom-call(s32[128,8]{1,0:T(8,128)} %copy.16.ids_ref, f32[128,8]{1,0:T(8,128)} %copy.17.gates_ref, bf16[64,1280]{1,0:T(8,128)(2,1)} %constant.19.clone.expand_ref, f32[1,1280]{1,0:T(1,128)} %constant.20.clone.rank_ref), custom_call_target="tpu_custom_call" | custom-call | tf_op jit(solution)/shard_map/lookup/pallas_call | solution.py:385
  29.3 62.5 %all-to-all-done.rows_ref = bf16[32,656,128]{2,1,0:T(8,128)(2,1)} async-done(((bf16[32,656,128]{2,1,0:T(8,128)(2,1)}), bf16[32,656,128]{2,1,0:T(8,128)(2,1)}, u32[]{:S(2)}, u32[]{:S(2)}) %all-to-all-start) | async-done | bytes 5373984 | tf_op jit(solution)/shard_map/all_to_all | solution.py:451
  91.8 0.0 all-gather.2.cloned.1.call-done.w_ref
  91.8 9.9 %forward.1 = (bf16[2,2,384,1024]{3,2,1,0:T(8,128)(2,1)}, bf16[2,2,384,128]{3,2,1,0:T(8,128)(2,1)}, bf16[2,2,384,768]{3,2,1,0:T(8,128)(2,1)}, f32[2,2,384,1]{3,2,...) custom-call(s32[1]{0:T(128)} %bitcast.host_ref, ...), custom_call_target="tpu_custom_call" | custom-call | flops 3623878656 | bytes 20000000 | tf_op jit(solution)/shard_map/forward/pallas_call | solution.py:239
  101.7 11.1 %all-to-all-start.1 = ((bf16[32,32,128]{2,1,0:T(8,128)(2,1)}), bf16[32,32,128]{2,1,0:T(8,128)(2,1)S(1)}, u32[]{:S(2)}, u32[]{:S(2)}) async-start(bf16[32,32,128]{2,1,0:T(8,128)(2,1)} %get-tuple-element.23), calls=%async_computation.1 | async-start | bytes 524288 | tf_op jit(solution)/shard_map/all_to_all | solution.py:451
  112.8 6.4 %backward.1 = bf16[1280,1024]{1,0:T(8,128)(2,1)} custom-call(s32[1]{0:T(128)} %bitcast.host_ref, bf16[2,2,384,768]{3,2,1,0:T(8,128)(2,1)} %get-tuple-element.30.gu_ref, f32[2,2,384,1]{3,2,1,0:T(8,128)} %get-tuple-element.31.add_ref, bf16[64,1024]{1,0:T(8,128)(2,1)} %bitcast.11, bf16[2,1024,1152]{2,1,0:T(8,128)(2,1)} %all-gather.2.cloned.1.call-done.w_ref), custom_call_target="tpu_custom_call" | custom-call | flops 2415919104 | bytes 10000000 | tf_op jit(solution)/shard_map/backward/pallas_call | solution.py:294
  119.3 0.0 copy-start.2
  119.3 0.0 copy-start.5
  119.3 0.0 copy-start.6
  119.3 2.5 %all-to-all-done.1.shares_ref = bf16[32,32,128]{2,1,0:T(8,128)(2,1)S(1)} async-done(((bf16[32,32,128]{2,1,0:T(8,128)(2,1)}), bf16[32,32,128]{2,1,0:T(8,128)(2,1)S(1)}, u32[]{:S(2)}, u32[]{:S(2)}) %all-to-all-start.1) | async-done | bytes 262176 | tf_op jit(solution)/shard_map/all_to_all | solution.py:451
  121.8 0.0 copy-start.1
  121.8 0.0 copy-start.4
  121.8 5.0 %all-to-all-start.2 = ((bf16[32,40,1024]{2,1,0:T(8,128)(2,1)}), bf16[32,40,1024]{2,1,0:T(8,128)(2,1)S(1)}, u32[]{:S(2)}, u32[]{:S(2)}) async-start(bf16[32,40,1024]{2,1,0:T(8,128)(2,1)} %bitcast.14), calls=%async_computation.2 | async-start | bytes 5242880 | tf_op jit(solution)/shard_map/all_to_all | solution.py:451
  126.8 0.0 copy-done.2
  126.9 0.0 copy-done.5
  126.9 0.0 copy-done.6
  126.9 0.0 copy-start
  126.9 1.9 %copy-done = bf16[2,2,384,1024]{3,2,1,0:T(8,128)(2,1)S(1)} copy-done((bf16[2,2,384,1024]{3,2,1,0:T(8,128)(2,1)S(1)}, bf16[2,2,384,1024]{3,2,1,0:T(8,128)(2,1)}, u32[]{:S(2)}) %copy-start) | copy-done | bytes 3145752
  128.8 1.3 router_part.1
  130.1 0.0 copy-start.7
  130.1 0.6 copy-done.7
  130.7 9.4 %psum.14 = f32[2,1024]{1,0:T(2,128)S(1)} all-reduce(f32[2,1024]{1,0:T(2,128)} %copy-done.7), channel_id=1, replica_groups={{0,32,64,96},{128,160,192,224},{256,288,320,352},{384,416,448,480},{1,3..., use_global_device_ids=true, to_apply=%region_0.0 | all-reduce | flops 2048 | bytes 16384 | tf_op jit(solution)/shard_map/psum | solution.py:474
  140.1 15.6 %psum.15 = f32[2,1024]{1,0:T(2,128)S(1)} all-reduce(f32[2,1024]{1,0:T(2,128)S(1)} %psum.14), channel_id=1, replica_groups={{0,128,256,384},{32,160,288,416},{64,192,320,448},{96,224,352,480},{1,1..., use_global_device_ids=true, to_apply=%region_1.0 | all-reduce | flops 2048 | bytes 16384 | tf_op jit(solution)/shard_map/psum | solution.py:475
  155.8 0.1 constant_dynamic-slice_fusion
  155.8 0.1 broadcast_in_dim.7
  155.9 4.8 %all-to-all-done.2 = bf16[32,40,1024]{2,1,0:T(8,128)(2,1)S(1)} async-done(((bf16[32,40,1024]{2,1,0:T(8,128)(2,1)}), bf16[32,40,1024]{2,1,0:T(8,128)(2,1)S(1)}, u32[]{:S(2)}, u32[]{:S(2)}) %all-to-all-start.2) | async-done | bytes 2621472 | tf_op jit(solution)/shard_map/all_to_all | solution.py:451
  160.7 0.6 broadcast_in_dim.8
  161.3 5.7 %all-to-all-start.3 = ((f32[32,1,128]{2,1,0:T(1,128)}), f32[32,1,128]{2,1,0:T(1,128)S(1)}, u32[]{:S(2)}, u32[]{:S(2)}) async-start(f32[32,1,128]{2,1,0:T(1,128)} %broadcast_in_dim.8), calls=%async_computation.3 | async-start | bytes 32768 | tf_op jit(solution)/shard_map/all_to_all | solution.py:451
  167.1 0.0 copy-done.1
  167.1 0.0 copy-done.4
  167.1 0.0 copy-start.3
  167.1 1.0 copy-done.3
  168.1 1.3 combine.1
  169.4 4.5 %all-to-all-done.3 = f32[32,1,128]{2,1,0:T(1,128)S(1)} async-done(((f32[32,1,128]{2,1,0:T(1,128)}), f32[32,1,128]{2,1,0:T(1,128)S(1)}, u32[]{:S(2)}, u32[]{:S(2)}) %all-to-all-start.3) | async-done | bytes 16416 | tf_op jit(solution)/shard_map/all_to_all | solution.py:451
  174.0 0.9 layout.1
Async XLA Ops:
  7.2 84.6 %all-gather.2.cloned.1.call-start = ((), (), s32[]{:S(2)}) async-start(), calls=%async_computation.4 | async-start | bytes 5013504 | tf_op jit(solution)/shard_map/all_gather | solution.py:461
  14.0 11.5 %copy-start.8 = (s32[128,8]{0,1:T(8,128)S(1)}, s32[128,8]{0,1:T(8,128)}, u32[]{:S(2)}) copy-start(s32[128,8]{0,1:T(8,128)} %param.10) | copy-start | bytes 12292
  14.0 12.3 %copy-start.9 = (f32[128,8]{0,1:T(8,128)S(1)}, f32[128,8]{0,1:T(8,128)}, u32[]{:S(2)}) copy-start(f32[128,8]{0,1:T(8,128)} %param.11) | copy-start | bytes 12292
  14.0 77.8 %all-to-all-start = ((bf16[32,656,128]{2,1,0:T(8,128)(2,1)}), bf16[32,656,128]{2,1,0:T(8,128)(2,1)}, u32[]{:S(2)}, u32[]{:S(2)}) async-start(bf16[32,656,128]{2,1,0:T(8,128)(2,1)} %dispatch.1), calls=%async_computation | async-start | bytes 10747904 | tf_op jit(solution)/shard_map/all_to_all | solution.py:451
  101.7 20.1 %all-to-all-start.1 = ((bf16[32,32,128]{2,1,0:T(8,128)(2,1)}), bf16[32,32,128]{2,1,0:T(8,128)(2,1)S(1)}, u32[]{:S(2)}, u32[]{:S(2)}) async-start(bf16[32,32,128]{2,1,0:T(8,128)(2,1)} %get-tuple-element.23), calls=%async_computation.1 | async-start | bytes 524288 | tf_op jit(solution)/shard_map/all_to_all | solution.py:451
  119.3 7.6 %copy-start.2 = (bf16[2,2,384,128]{3,2,1,0:T(8,128)(2,1)S(1)}, bf16[2,2,384,128]{3,2,1,0:T(8,128)(2,1)}, u32[]{:S(2)}) copy-start(bf16[2,2,384,128]{3,2,1,0:T(8,128)(2,1)} %get-tuple-element.26.hot_hbm) | copy-start | bytes 1179652
  119.3 7.6 %copy-start.5 = (f32[2,32,128]{2,1,0:T(8,128)S(1)}, f32[2,32,128]{2,1,0:T(8,128)}, u32[]{:S(2)}) copy-start(f32[2,32,128]{2,1,0:T(8,128)} %get-tuple-element.24.gg_ref) | copy-start | bytes 98308
  119.3 7.6 %copy-start.6 = (f32[2,32,128]{2,1,0:T(8,128)S(1)}, f32[2,32,128]{2,1,0:T(8,128)}, u32[]{:S(2)}) copy-start(f32[2,32,128]{2,1,0:T(8,128)} %get-tuple-element.25.gate_ref) | copy-start | bytes 98308
  121.8 45.3 %copy-start.1 = (bf16[1024,64]{0,1:T(8,128)(2,1)S(1)}, bf16[1024,64]{0,1:T(8,128)(2,1)}, u32[]{:S(2)}) copy-start(bf16[1024,64]{0,1:T(8,128)(2,1)} %param.13) | copy-start | bytes 393220
  121.8 45.3 %copy-start.4 = (f32[128,64]{1,0:T(8,128)S(1)}, f32[128,64]{1,0:T(8,128)}, u32[]{:S(2)}) copy-start(f32[128,64]{1,0:T(8,128)} %get-tuple-element.21.dense_ref) | copy-start | bytes 98308
  121.8 38.9 %all-to-all-start.2 = ((bf16[32,40,1024]{2,1,0:T(8,128)(2,1)}), bf16[32,40,1024]{2,1,0:T(8,128)(2,1)S(1)}, u32[]{:S(2)}, u32[]{:S(2)}) async-start(bf16[32,40,1024]{2,1,0:T(8,128)(2,1)} %bitcast.14), calls=%async_computation.2 | async-start | bytes 5242880 | tf_op jit(solution)/shard_map/all_to_all | solution.py:451
  126.9 1.9 %copy-start = (bf16[2,2,384,1024]{3,2,1,0:T(8,128)(2,1)S(1)}, bf16[2,2,384,1024]{3,2,1,0:T(8,128)(2,1)}, u32[]{:S(2)}) copy-start(bf16[2,2,384,1024]{3,2,1,0:T(8,128)(2,1)} %get-tuple-element.27.xe_hbm) | copy-start | bytes 9437188
  130.1 0.6 copy-start.7
  161.3 12.6 %all-to-all-start.3 = ((f32[32,1,128]{2,1,0:T(1,128)}), f32[32,1,128]{2,1,0:T(1,128)S(1)}, u32[]{:S(2)}, u32[]{:S(2)}) async-start(f32[32,1,128]{2,1,0:T(1,128)} %broadcast_in_dim.8), calls=%async_computation.3 | async-start | bytes 32768 | tf_op jit(solution)/shard_map/all_to_all | solution.py:451
  167.1 1.0 copy-start.3
Sparse Core Ops, SparseCore 0:
  10.1 77.4 all-gather.1
